TPU v7x, 32 devices: a whole 2x2x4 slice. The times are simulated.
32 devices in a mesh: seq: 8 (over z, x), tensor: 4 (over y, core).
Axes of the slice: x: 2, y: 2, z: 4, core: 2. Of those that a mesh axis runs over, the one named last changes fastest.
Arguments:
- queries: bfloat16 [1024, 32, 128], P('seq', 'tensor'), may hold values from -6 to 6
- keys: bfloat16 [2, 1024, 32, 128], P(None, 'seq', 'tensor'), may hold values from -6 to 6
- values: bfloat16 [2, 1024, 32, 128], P(None, 'seq', 'tensor'), may hold values from -24 to 24
- beta: float32 [2, 32, 1024], P(None, 'tensor', 'seq'), may hold values from 0.25 to 2
- decay: float32 [32, 1024], P('tensor', 'seq'), may hold values from -0.75 to 0
- out_gain: float32 [128], replicated, may hold values from 0.1 to 1.9
- residual: bfloat16 [1024, 4096], P('seq', 'tensor'), may hold values from -40 to 40
- ffn_gain: float32 [4096], replicated, may hold values from 0.1 to 1.9
- up_blocks: bfloat16 [64, 16, 128, 128], P('tensor'), may hold values from -0.125 to 0.125
- up_index: int32 [64, 16], P('tensor'), may hold values from 0 to 31, as said below
- down_kept_tiles: bfloat16 [64, 16, 128, 128], P('tensor'), may hold values from -0.09375 to 0.09375
- down_index: int32 [64, 16], P('tensor'), may hold values from 0 to 31, as said below
Outputs:
- layer_out: bfloat16 [1024, 4096], P('seq', 'tensor')
Inputs may be any that keep to these rules, and one draw needn't show every extreme that they name: `up_index`: each row names 16 different tiles. `down_index`: each row names 16 different tiles.
All inputs are finite; a program needn't handle non-finite values.
Results may differ from a plain program's by a relative error of at most 0.014.
Values may be sent and summed in bfloat16 or wider, within the bound.
No kernel may reach another device: no remote copies, remote signals or barrier semaphores. Data moves between devices by JAX's collectives and lax.ppermute only.
A program may use at most 128 MiB of HBM per device.

v0:
```python
import jax
import jax.numpy as jnp
from jax import lax
from jax.sharding import PartitionSpec as P

BLOCK_TOK = 64


def entering(value, axis, combine, identity):
    count, index = (lax.axis_size(axis), lax.axis_index(axis))
    everything = jax.tree.map(
        lambda part, kind: lax.all_gather(part.astype(kind), axis),
        value,
        (jnp.bfloat16, jnp.bfloat16),
    )
    start = jax.tree.map(
        lambda part, zero: jnp.broadcast_to(jnp.asarray(zero, part.dtype), part.shape),
        value,
        identity,
    )

    def lap(k, before):
        reached = k < index
        new = combine(
            before, jax.tree.map(lambda part, own: part[k].astype(own.dtype), everything, value)
        )
        return jax.tree.map(lambda a, b: jnp.where(reached, a, b), new, before)

    return lax.fori_loop(0, count, lap, start)


def normed(given):
    wide = given.astype(jnp.float32)
    return wide * lax.rsqrt(jnp.sum(wide * wide, -1, keepdims=True) + 1e-06)


def product(left, right):
    return jnp.einsum("hde,hef->hdf", left, right, precision=lax.Precision.HIGHEST)


def block_terms(queries, keys, values, beta, decay):
    highest = lax.Precision.HIGHEST
    tok_count, heads_dev, width = queries.shape
    span = 2 * BLOCK_TOK
    blocks = tok_count // BLOCK_TOK
    key_unit = normed(keys).transpose(2, 1, 0, 3).reshape(heads_dev, blocks, span, width)
    value_all = (
        values.astype(jnp.float32).transpose(2, 1, 0, 3).reshape(heads_dev, blocks, span, width)
    )
    beta_all = beta.transpose(1, 2, 0).reshape(heads_dev, blocks, span)
    log_gate = jnp.stack([decay, jnp.zeros_like(decay)], -1).reshape(heads_dev, blocks, span)
    query_unit = normed(queries).transpose(1, 0, 2).reshape(heads_dev, blocks, BLOCK_TOK, width)
    running = jnp.cumsum(log_gate, -1)
    rows_at = lax.broadcasted_iota(jnp.int32, (span, span), 0)
    cols_at = lax.broadcasted_iota(jnp.int32, (span, span), 1)
    below = cols_at < rows_at
    key_inner_products = jnp.einsum("hcid,hcmd->hcim", key_unit, key_unit, precision=highest)
    spread = running[..., :, None] - running[..., None, :]
    factor_decay = jnp.exp(jnp.where(below, spread, 0.0))
    lower_part = jnp.where(below, beta_all[..., :, None] * factor_decay * key_inner_products, 0.0)
    system = jnp.eye(span, dtype=jnp.float32) + lower_part
    gamma = jnp.exp(running)
    rhs = beta_all[..., None] * jnp.concatenate([value_all, gamma[..., None] * key_unit], -1)
    solved = jax.scipy.linalg.solve_triangular(system, rhs, lower=True)
    value_new = solved[..., :width]
    weight_rows = solved[..., width:]
    remain = jnp.exp(running[..., -1:] - running)
    key_scaled = remain[..., None] * key_unit
    eye_wide = jnp.eye(width, dtype=jnp.float32)
    block_trans = gamma[..., -1][..., None, None] * eye_wide - jnp.einsum(
        "hcmd,hcme->hcde", key_scaled, weight_rows, precision=highest
    )
    block_write = jnp.einsum("hcmd,hcme->hcde", key_scaled, value_new, precision=highest)
    query_running = running[..., 1::2]
    token_at = lax.broadcasted_iota(jnp.int32, (BLOCK_TOK, span), 0)
    factor_at = lax.broadcasted_iota(jnp.int32, (BLOCK_TOK, span), 1)
    attained_count = factor_at <= 2 * token_at + 1
    query_key = jnp.einsum("hcrd,hcmd->hcrm", query_unit, key_unit, precision=highest)
    query_spread = query_running[..., :, None] - running[..., None, :]
    mixing = jnp.where(
        attained_count, jnp.exp(jnp.where(attained_count, query_spread, 0.0)) * query_key, 0.0
    )
    query_tilde = jnp.exp(query_running)[..., None] * query_unit - jnp.einsum(
        "hcrm,hcme->hcre", mixing, weight_rows, precision=highest
    )
    local_out = jnp.einsum("hcrm,hcme->hcre", mixing, value_new, precision=highest)
    return (block_trans, block_write, query_tilde, local_out)


def incoming_state(dev_trans, dev_write):
    heads_dev, width = (dev_trans.shape[0], dev_trans.shape[1])
    eye_all = jnp.broadcast_to(jnp.eye(width, dtype=jnp.float32), (heads_dev, width, width))
    empty = jnp.zeros((heads_dev, width, width), jnp.float32)

    def linked(earlier, later):
        return (product(later[0], earlier[0]), product(later[0], earlier[1]) + later[1])

    prefix = entering((dev_trans, dev_write), "seq", linked, (eye_all, empty))
    return prefix[1]


def per_device(
    queries,
    keys,
    values,
    beta,
    decay,
    out_gain,
    residual,
    ffn_gain,
    up_blocks,
    up_index,
    down_kept_tiles,
    down_index,
):
    highest = lax.Precision.HIGHEST
    tok_count, heads_dev, width = queries.shape
    block_trans, block_write, query_tilde, local_out = block_terms(
        queries, keys, values, beta, decay
    )
    trans_seq = jnp.moveaxis(block_trans, 1, 0)
    write_seq = jnp.moveaxis(block_write, 1, 0)
    tilde_seq = jnp.moveaxis(query_tilde, 1, 0)
    local_seq = jnp.moveaxis(local_out, 1, 0)
    eye_all = jnp.broadcast_to(jnp.eye(width, dtype=jnp.float32), (heads_dev, width, width))
    empty = jnp.zeros((heads_dev, width, width), jnp.float32)

    def compose(carry, pair):
        prefix, state = carry
        trans_one, write_one = pair
        return (
            (product(trans_one, prefix), product(trans_one, state) + write_one),
            (prefix, state),
        )

    (dev_trans, dev_write), _ = lax.scan(compose, (eye_all, empty), (trans_seq, write_seq))
    arrived = incoming_state(dev_trans, dev_write)

    def emit(state, pieces):
        trans_one, write_one, tilde_one, local_one = pieces
        result = jnp.einsum("hrd,hde->hre", tilde_one, state, precision=highest) + local_one
        return (product(trans_one, state) + write_one, result)

    _, block_out = lax.scan(emit, arrived, (trans_seq, write_seq, tilde_seq, local_seq))
    head_out = jnp.moveaxis(block_out, 0, 1).reshape(heads_dev, tok_count, width).transpose(1, 0, 2)
    normed_out = (
        head_out * lax.rsqrt(jnp.mean(head_out * head_out, -1, keepdims=True) + 1e-05) * out_gain
    )
    hidden_state = (
        residual.astype(jnp.float32) + normed_out.reshape(tok_count, heads_dev * width)
    ).astype(jnp.bfloat16)
    full_rows = lax.all_gather(hidden_state, "tensor", axis=1, tiled=True)
    full_wide = full_rows.astype(jnp.float32)
    ffn_in = (
        full_wide * lax.rsqrt(jnp.mean(full_wide * full_wide, -1, keepdims=True) + 1e-05) * ffn_gain
    ).astype(jnp.bfloat16)
    tile_side = up_blocks.shape[-1]
    tile_count = ffn_in.shape[1] // tile_side
    group_count = up_blocks.shape[0]
    tiles_in = ffn_in.reshape(tok_count, tile_count, tile_side)
    picked = jnp.take(tiles_in, up_index, axis=1)
    pre_act = jnp.einsum("tcjd,cjdh->tch", picked, up_blocks, preferred_element_type=jnp.float32)
    activation = (
        jax.nn.gelu(pre_act).astype(jnp.bfloat16).reshape(tok_count, group_count * tile_side)
    )
    group_ids = jnp.arange(group_count, dtype=jnp.int32)[:, None]
    placed = (
        jnp.zeros((group_count, tile_count, tile_side, tile_side), jnp.bfloat16)
        .at[group_ids, down_index]
        .set(down_kept_tiles)
    )
    dense_down = placed.transpose(0, 2, 1, 3).reshape(
        group_count * tile_side, tile_count * tile_side
    )
    partial_sum = jnp.dot(activation, dense_down, preferred_element_type=jnp.float32)
    ffn_part = lax.psum_scatter(
        partial_sum.astype(jnp.bfloat16), "tensor", scatter_dimension=1, tiled=True
    ).astype(jnp.float32)
    return (hidden_state.astype(jnp.float32) + ffn_part).astype(jnp.bfloat16)


def solution(mesh):
    placed = (
        P("seq", "tensor", None),
        P(None, "seq", "tensor", None),
        P(None, "seq", "tensor", None),
        P(None, "tensor", "seq"),
        P("tensor", "seq"),
        P(),
        P("seq", "tensor"),
        P(),
        P("tensor", None, None, None),
        P("tensor", None),
        P("tensor", None, None, None),
        P("tensor", None),
    )
    return jax.shard_map(
        per_device, mesh=mesh, in_specs=placed, out_specs=P("seq", "tensor"), check_vma=False
    )
```

profile of v0, /device:TPU:0, one launch (start us, length us, event | category | flops | bytes accessed | tf_op | source)
XLA Modules:
  0.0 440.5 jit_solution(11242318794661103190)
XLA Ops:
  6.6 0.8 copy.145
  8.9 0.8 copy.104
  9.8 1.5 fusion.53
  11.7 2.4 fusion.50
  14.2 157.9 %custom-call.4 = f32[8,2,1,128,128]{3,4,2,1,0:T(8,128)} custom-call(f32[8,2,1,128,128]{4,3,2,1,0:T(8,128)S(1)} %fusion.50), custom_call_target="InvertDiagBlocksLowerTriangular" | custom-call | tf_op jit(solution)/shard_map/jit(_solve_triangular)/vmap(vmap())/triangular_solve | solution.py:64
  172.0 1.6 broadcast_multiply_fusion
  174.1 1.2 copy_convert_fusion
  175.8 0.9 copy-done.7
  176.7 2.6 fusion.41
  179.2 1.2 convolution_bitcast_fusion
  180.4 1.2 fusion.46
  181.9 3.0 while.40
  182.2 0.6 convolution_add_fusion.7
  182.9 0.6 fusion.121
  183.6 0.6 convolution_add_fusion.7
  184.3 0.6 fusion.121
  185.0 0.7 convert_element_type.70
  185.8 0.7 convert_element_type.69
  188.1 2.1 fusion.52
  190.2 1.9 convolution_bitcast_fusion.2
  192.1 1.1 fusion.51
  193.1 44.7 %all-gather.10.cloned.1.call-done = bf16[64,128,128]{2,1,0:T(8,128)(2,1)} async-done(((bf16[8,128,128]{2,1,0:T(8,128)(2,1)}), bf16[64,128,128]{2,1,0:T(8,128)(2,1)}) %all-gather.10.cloned.1.call-update) | async-done | bytes 2097168 | tf_op jit(solution)/shard_map/all_gather | solution.py:12
  237.9 49.9 %all-gather.8.cloned.1.call-done = bf16[64,128,128]{2,1,0:T(8,128)(2,1)} async-done(((bf16[8,128,128]{2,1,0:T(8,128)(2,1)}), bf16[64,128,128]{2,1,0:T(8,128)(2,1)}) %all-gather.8.cloned.1.call-update) | async-done | bytes 2097168 | tf_op jit(solution)/shard_map/all_gather | solution.py:12
  287.8 12.6 %while.41 = (s32[]{:T(128)}, f32[8,128,128]{2,1,0:T(8,128)S(1)}, s32[]{:T(128)}, bf16[8,8,128,128]{3,2,1,0:T(8,128)(2,1)}, bf16[8,8,128,128]{3,2,1,0:T(8,128)(2,1)}, /*index=5*/s32[]{:T(128)}, s32[]{:T(128)}) while((s32[]{:T(128)}, f32[8,128,128]{2,1,0:T(8,128)S(1)}, s32[]{:T(128)}, bf16[8,8,128,128]{3,2,1,0:T(8,128)(2,1)}, ...), condition=%wide.region_5.6_spmd.clone, body=%wide.region_4.5_spmd.clone.sunk | while | flops 201981952 | bytes 3148391 | solution.py:29
  287.8 1.5 fusion.124
  289.4 1.5 fusion.124
  291.0 1.5 fusion.124
  292.6 1.5 fusion.124
  294.2 1.5 fusion.124
  295.7 1.5 fusion.124
  297.3 1.5 fusion.124
  298.9 1.5 fusion.124
  300.4 6.0 %while.39 = (s32[]{:T(128)}, f32[8,128,128]{2,1,0:T(8,128)S(1)}, f32[2,8,64,128]{3,2,0,1:T(8,128)}, f32[2,8,128,128]{3,2,1,0:T(8,128)S(1)}, f32[2,8,128,128]{3,2...) while((s32[]{:T(128)}, f32[8,128,128]{2,1,0:T(8,128)S(1)}, ...), condition=%wide.region_8.9_spmd, body=%wide.region_7.8_spmd.sunk | while | flops 302186496 | bytes 4458589 | solution.py:144
  300.5 2.3 fusion.116
  303.5 2.3 fusion.116
  306.5 1.3 fusion.77
  307.7 1.2 fusion.78
  309.0 0.8 fusion.76
  310.0 6.4 %broadcast_in_dim.82 = bf16[16,32,128,128]{3,2,1,0:T(8,128)(2,1)} broadcast(bf16[]{:T(256)} %constant.109.clone.1), dimensions={} | broadcast | bytes 16777218 | tf_op jit(solution)/shard_map/broadcast_in_dim | solution.py:168
  316.4 40.5 %scatter_fusion = bf16[16,32,128,128]{3,2,1,0:T(8,128)(2,1)} fusion(bf16[16,32,128,128]{3,2,1,0:T(8,128)(2,1)} %broadcast_in_dim.82, s32[256]{0:T(256)S(1)} %reshape.118, bf16[256,128,128]{2,1,0:T(8,128)(2,1)} %bitcast.164), kind=kCustom, calls=%fused_computation.1 | custom fusion | bytes 25167872 | tf_op jit(solution)/shard_map/scatter | solution.py:170
  356.9 18.5 %copy.131 = bf16[16,128,32,128]{3,2,1,0:T(8,128)(2,1)} copy(bf16[16,128,32,128]{3,1,2,0:T(8,128)(2,1)} %bitcast.159) | data formatting | bytes 33554432 | tf_op jit(solution)/shard_map/transpose | solution.py:172
  375.5 1.5 fusion.38
  377.0 1.6 copy_bitcast_fusion
  378.7 8.6 %gather_fusion = bf16[256,128,128]{2,1,0:T(8,128)(2,1)} fusion(bf16[128,32,128]{2,0,1:T(8,128)(2,1)S(1)} %copy_bitcast_fusion, s32[1024]{0:T(1024)S(1)} %pad_clamp_fusion), kind=kCustom, calls=%fused_computation | custom fusion | bytes 16778240 | tf_op jit(solution)/shard_map/jit(_take)/gather | solution.py:161
  387.3 8.8 %fusion.63 = bf16[128,16,128]{0,2,1:T(8,128)(2,1)S(1)} fusion(bf16[16,16,128,128]{3,2,1,0:T(8,128)(2,1)} %param.26, bf16[16,16,128,128]{3,2,1,0:T(8,128)(2,1)} %bitcast.165, pred[16,16]{1,0:T(8,128)(4,1)S(1)} %compare_and_fusion), kind=kOutput, calls=%fused_computation.75 | convolution fusion | flops 1080295424 | bytes 17301760 | tf_op jit(solution)/shard_map/tcjd,cjdh->tch/dot_general | solution.py:162
  396.1 12.6 %fusion.34 = bf16[128,4096]{1,0:T(8,128)(2,1)} fusion(bf16[128,2048]{0,1:T(8,128)(2,1)S(1)} %bitcast.177, bf16[256,8,32,128]{3,2,1,0:T(8,128)(2,1)} %bitcast.160), kind=kOutput, calls=%fused_computation.40 | convolution fusion | flops 2148007936 | bytes 18350080 | tf_op jit(solution)/shard_map/dot_general | solution.py:175
  408.7 23.6 %reduce-scatter.2.cloned.1.call-done = bf16[128,1024]{1,0:T(8,128)(2,1)} async-done(((bf16[128,4096]{1,0:T(8,128)(2,1)}), bf16[128,1024]{1,0:T(8,128)(2,1)}) %reduce-scatter.2.cloned.1.call-update) | async-done | bytes 262160 | tf_op jit(solution)/shard_map/reduce_scatter | solution.py:176
  432.3 1.7 add_convert_fusion
  (93 shorter events, 6.7 us)
Async XLA Ops:
  6.5 4.8 %copy-start.6 = (bf16[2,128,8,128]{3,2,1,0:T(8,128)(2,1)S(1)}, bf16[2,128,8,128]{3,2,1,0:T(8,128)(2,1)}, u32[]{:S(2)}) copy-start(bf16[2,128,8,128]{3,2,1,0:T(8,128)(2,1)} %param.19) | copy-start | bytes 1572868
  6.5 231.3 %all-gather.10.cloned.1.call-start = ((), (), s32[]{:S(2)}) async-start(), calls=%async_computation.4 | async-start | bytes 2359296 | tf_op jit(solution)/shard_map/all_gather | solution.py:12
  11.7 161.9 %copy-start.2 = (f32[2,128,8,128]{3,2,0,1:T(8,128)}, f32[2,128,8,128]{3,2,0,1:T(8,128)S(1)}, u32[]{:S(2)}) copy-start(f32[2,128,8,128]{3,2,0,1:T(8,128)S(1)} %convert_multiply_fusion.2) | copy-start | bytes 3145732
  174.0 1.4 copy-start.4
  175.4 1.2 copy-start.7
  179.2 2.5 copy-start
  184.9 1.9 copy-start.8
  185.7 102.1 %all-gather.8.cloned.1.call-start = ((), (), s32[]{:S(2)}) async-start(), calls=%async_computation.3 | async-start | bytes 2359296 | tf_op jit(solution)/shard_map/all_gather | solution.py:12
  186.5 188.9 %all-gather.6.cloned.1.call-start = ((), (), s32[]{:S(2)}) async-start(), calls=%async_computation.1 | async-start | bytes 1310720 | tf_op jit(solution)/shard_map/all_gather | solution.py:152
  186.8 1.2 copy-start.3
  187.1 3.1 copy-start.1
  300.4 7.3 %copy-start.13 = (f32[128]{0:T(128)S(1)}, f32[128]{0:T(128)}, u32[]{:S(2)}) copy-start(f32[128]{0:T(128)} %param.23) | copy-start | bytes 1540
  300.4 8.6 %copy-start.9 = (bf16[128,1024]{1,0:T(8,128)(2,1)S(1)}, bf16[128,1024]{1,0:T(8,128)(2,1)}, u32[]{:S(2)}) copy-start(bf16[128,1024]{1,0:T(8,128)(2,1)} %param.24) | copy-start | bytes 786436
  306.4 3.4 copy-start.12
  306.4 3.5 copy-start.10
  309.8 122.5 %reduce-scatter.2.cloned.1.call-start = ((), (), s32[]{:S(2)}) async-start(), calls=%async_computation.2 | async-start | bytes 1310720 | tf_op jit(solution)/shard_map/reduce_scatter | solution.py:176
  356.9 20.1 %copy-start.11 = (f32[4096]{0:T(1024)S(1)}, f32[4096]{0:T(1024)}, u32[]{:S(2)}) copy-start(f32[4096]{0:T(1024)} %param.25) | copy-start | bytes 49156
  396.1 36.2 %copy-start.5 = (bf16[128,1024]{1,0:T(8,128)(2,1)S(1)}, bf16[128,1024]{1,0:T(8,128)(2,1)}, u32[]{:S(2)}) copy-start(bf16[128,1024]{1,0:T(8,128)(2,1)} %fusion.76) | copy-start | bytes 786436
Sparse Core Ops, SparseCore 0:
  185.8 51.9 all-gather.9
  240.0 47.7 all-gather.7
  309.9 15.2 all-gather.5
  408.8 23.3 reduce-scatter.1
where the time goes:
time: 442 us; the launch traced here: 441 us
  other arithmetic  174 us (39%)
  waiting for transfers between devices  118 us (27%)
  local copies, waits for them, and re-layouts  79.7 us (18%)
  matrix products  54.3 us (12%)
  between operations  13.6 us (3%)
    another operation x1, other arithmetic, block_terms(): solved = jax.scipy.linalg.solve_triangular(system, rhs, lower=True)  158 us
    all_gather x2, waiting for transfers between devices, entering(): lax.all_gather(part.astype(kind), axis)  94.7 us
    scatter x1, local copies, waits for them, and re-layouts, per_device(): placed = jnp.zeros((group_count, tile_count, tile_side, tile_side), jnp.b...  40.5 us
    reduce_scatter x1, waiting for transfers between devices, per_device(): lax.psum_scatter(partial_sum.astype(jnp.bfloat16), 'tensor', scatter_dime...  23.6 us
    transpose x1, local copies, waits for them, and re-layouts, per_device(): placed.transpose(0, 2, 1, 3)  18.5 us
    dot_general x14, matrix products, product(): jnp.einsum('hde,hef->hdf', left, right, precision=lax.Precision.HIGHEST)  15.9 us
    dot_general x1, matrix products, per_device(): jnp.dot(activation, dense_down, preferred_element_type=jnp.float32)  12.6 us
  transfers between devices with their start and end apart: 4, of which 3 were waited for; matrix products, arithmetic and copies ran while one was open for 16% of the time, Pallas kernels for 0%

commit v1 on v0

v1 whole, which is shorter than its diff:
```python
import functools

import jax
import jax.numpy as jnp
from jax import lax
from jax.experimental import pallas as pl
from jax.experimental.pallas import tpu as pltpu
from jax.sharding import PartitionSpec as P

F32 = jnp.float32
BF16 = jnp.bfloat16
HEAD_GROUP = 4
MIB = 1 << 20
VMEM = pl.BlockSpec(memory_space=pltpu.VMEM)
SMEM = pl.BlockSpec(memory_space=pltpu.SMEM)
ANY = pl.BlockSpec(memory_space=pl.ANY)


def dot(a, b):
    return jnp.dot(a, b, preferred_element_type=F32)


def dot_nt(a, b):
    return lax.dot_general(a, b, (((1,), (1,)), ((), ())), preferred_element_type=F32)


def dot_tn(a, b):
    return lax.dot_general(a, b, (((0,), (0,)), ((), ())), preferred_element_type=F32)


def split(x):
    high = x.astype(BF16)
    return high, (x - high.astype(F32)).astype(BF16)


def dot_wide(a, b):
    width = a[0].shape[1]
    row = jnp.concatenate([b[0], b[1]], 1)
    out = dot(jnp.concatenate([a[0], a[1]], 1), jnp.concatenate([row, row], 0))
    return out[:, :width] + out[:, width:]


def column(row):
    n = row.shape[1]
    return jnp.broadcast_to(row, (n, n)).T


def head_rows(ref, h, stride):
    return ref[pl.ds(h, ref.shape[0] // stride, stride=stride), :]


def stacked(first, second):
    half = first.shape[0] // 2
    return [
        jnp.concatenate([first[i * half : (i + 1) * half], second[i * half : (i + 1) * half]], 0)
        for i in range(2)
    ]


def running_rows(decay_ref):
    tokens = decay_ref.shape[1]
    earlier = lax.broadcasted_iota(jnp.int32, (tokens, tokens), 0)
    later = lax.broadcasted_iota(jnp.int32, (tokens, tokens), 1)
    return jnp.dot(
        decay_ref[...],
        (earlier <= later).astype(F32),
        preferred_element_type=F32,
        precision=lax.Precision.HIGHEST,
    )


def doubled(rows, half):
    return [
        jnp.concatenate([rows[:, i * half : (i + 1) * half]] * 2, 1) for i in range(2)
    ]


def terms_kernel(exchange, beta_ref, decay_ref, k_ref, v_ref, *refs):
    heads, tokens = decay_ref.shape
    width = k_ref.shape[-1]
    half = tokens // 2
    span = 2 * half
    out_refs, sol_ref = refs[:heads], refs[heads]
    k_all, v_all, row_ref = refs[heads + 1 :]
    me = lax.axis_index("seq") if exchange else 0
    for j in range(2):
        k_all[j] = k_ref[j].astype(F32).reshape(tokens * heads, width)
        v_all[j] = v_ref[j].astype(F32).reshape(tokens * heads, width)
    run = running_rows(decay_ref)
    run_half = doubled(run, half)
    beta_half = stacked_beta(beta_ref, half)
    last = jnp.broadcast_to(run[:, tokens - 1 :], (heads, span))
    for i in range(2):
        row_ref[i] = run_half[i]
        row_ref[2 + i] = beta_half[i]
    row_ref[4] = last

    row_at = lax.broadcasted_iota(jnp.int32, (span, span), 0)
    col_at = lax.broadcasted_iota(jnp.int32, (span, span), 1)
    row_time = 2 * lax.rem(row_at, half) + row_at // half
    col_time = 2 * lax.rem(col_at, half) + col_at // half
    below = col_time < row_time
    apart = jnp.where(below, row_time ^ col_time, 0)
    eye = (row_at == col_at).astype(F32)
    eye_wide = eye[:width, :width]
    left = col_at < half

    for start in range(0, heads, HEAD_GROUP):
        slots = range(start, min(start + HEAD_GROUP, heads))
        chains = []
        for s in slots:
            h = lax.rem(me + s, heads)
            keys = stacked(*(head_rows(k_all.at[j], h, heads) for j in range(2)))
            values = stacked(*(head_rows(v_all.at[j], h, heads) for j in range(2)))
            keys = [x.astype(BF16) for x in keys]
            values = [x.astype(BF16) for x in values]
            run_row = [row_ref[i, pl.ds(h, 1), :] for i in range(2)]
            beta_row = [row_ref[2 + i, pl.ds(h, 1), :] for i in range(2)]
            run_col = [column(x) for x in run_row]
            beta_col = [column(x) for x in beta_row]
            last_row = row_ref[4, pl.ds(h, 1), :]
            grams = [dot_nt(x, x) for x in keys]
            inv_row = [lax.rsqrt(jnp.sum(g * eye, 0, keepdims=True) + 1e-06) for g in grams]
            inv_col = [lax.rsqrt(jnp.sum(g * eye, 1, keepdims=True) + 1e-06) for g in grams]
            lowers, inverses = [], []
            for i in range(2):
                spread = jnp.exp(jnp.where(below, run_col[i] - run_row[i], 0.0))
                scaled = grams[i] * inv_row[i] * inv_col[i]
                lower = jnp.where(below, beta_col[i] * spread * scaled, 0.0)
                pair = jnp.where(apart == 1, lower, 0.0)
                step = jnp.where((apart >= 2) & (apart < 4), lower, 0.0)
                by_row = jnp.sum(pair, 1, keepdims=True)
                by_col = jnp.sum(pair, 0, keepdims=True)
                step = jnp.concatenate(
                    [step[:half], step[half:] - by_row[half:] * step[:half]], 0
                )
                swapped = jnp.concatenate([step[:, half:], step[:, :half]], 1)
                step = step - jnp.where(left, swapped * by_col, 0.0)
                lowers.append(lower)
                inverses.append(eye - pair - step)
            cross = dot_nt(keys[1], keys[0]) * inv_row[0] * inv_col[1]
            cross = cross * beta_col[1] * jnp.exp(run_col[1] - run_row[0])
            chains.append(
                dict(
                    s=s, keys=keys, values=values, run_row=run_row, beta_row=beta_row,
                    run_col=run_col, last_row=last_row, inv_row=inv_row, inv_col=inv_col,
                    lowers=lowers, inverses=inverses, cross=cross,
                )
            )
        size = 4
        while size < span:
            for c in chains:
                c["parts"] = [split(x) for x in c["inverses"]]
                c["middle"] = [
                    dot_wide(
                        split(jnp.where((apart >= size) & (apart < 2 * size), low, 0.0)), part
                    )
                    for low, part in zip(c["lowers"], c["parts"])
                ]
            for c in chains:
                c["inverses"] = [
                    x - dot_wide(part, split(mid))
                    for x, part, mid in zip(c["inverses"], c["parts"], c["middle"])
                ]
            size *= 2
        for c in chains:
            c["parts"] = [split(x) for x in c["inverses"]]
            c["middle"] = dot_wide(split(c["cross"]), c["parts"][0])
        for c in chains:
            c["corner"] = -dot_wide(c["parts"][1], split(c["middle"]))
        for c in chains:
            scale_v = c["beta_row"]
            scale_k = [
                b * jnp.exp(r) * n for b, r, n in zip(c["beta_row"], c["run_row"], c["inv_row"])
            ]
            solved = []
            for scale, source in ((scale_k, c["keys"]), (scale_v, c["values"])):
                first = split(c["inverses"][0] * scale[0])
                upper = dot(jnp.concatenate(first, 1), jnp.concatenate([source[0]] * 2, 0))
                corner = split(c["corner"] * scale[0])
                second = split(c["inverses"][1] * scale[1])
                both = jnp.concatenate(source, 0)
                lower = dot(jnp.concatenate([corner[0], second[0]], 1), both) + dot(
                    jnp.concatenate([corner[1], second[1]], 1), both
                )
                solved.append((upper, lower))
            rows = [jnp.concatenate([solved[0][i], solved[1][i]], 1) for i in range(2)]
            c["rows"] = rows
            for i in range(2):
                sol_ref[c["s"], i * span : (i + 1) * span, :] = rows[i]
        for c in chains:
            last_col = column(c["last_row"])
            weighted = []
            for i in range(2):
                remain = jnp.exp(last_col - c["run_col"][i]) * c["inv_col"][i]
                weighted.append(c["rows"][i] * jnp.concatenate([remain, remain], 1))
            high, low = split(jnp.concatenate(weighted, 0))
            keys = jnp.concatenate(c["keys"], 0)
            ends = dot_tn(keys, high) + dot_tn(keys, low)
            gate = jnp.exp(c["last_row"])
            trans = eye_wide * gate - ends[:, :width]
            out_refs[c["s"]][...] = jnp.concatenate([trans, ends[:, width:]], 1).astype(BF16)


def stacked_beta(beta_ref, half):
    first, second = beta_ref[0], beta_ref[1]
    return [
        jnp.concatenate(
            [first[:, i * half : (i + 1) * half], second[:, i * half : (i + 1) * half]], 1
        )
        for i in range(2)
    ]


def mixing_kernel(exchange, decay_ref, q_ref, k_ref, sol_ref, out_ref, q_all, k_all, run_ref):
    heads, tokens = decay_ref.shape
    width = k_ref.shape[-1]
    half = tokens // 2
    span = 2 * half
    me = lax.axis_index("seq") if exchange else 0
    q_all[...] = q_ref[...].astype(F32).reshape(tokens * heads, width)
    for j in range(2):
        k_all[j] = k_ref[j].astype(F32).reshape(tokens * heads, width)
    run_ref[...] = running_rows(decay_ref)
    token_at = lax.broadcasted_iota(jnp.int32, (tokens, 2 * span), 0)
    row_at = lax.broadcasted_iota(jnp.int32, (tokens, 2 * span), 1)
    seen = (row_at // span) * half + lax.rem(row_at, half) <= token_at
    row_at = lax.broadcasted_iota(jnp.int32, (span, span), 0)
    col_at = lax.broadcasted_iota(jnp.int32, (span, span), 1)
    eye = (row_at == col_at).astype(F32)

    def one_head(s, carry):
        h = lax.rem(me + s, heads)
        queries = head_rows(q_all, h, heads)
        keys = stacked(*(head_rows(k_all.at[j], h, heads) for j in range(2)))
        run = run_ref[pl.ds(h, 1), :]
        run_col = column(run)
        run_row = jnp.concatenate(doubled(run, half), 1)
        keys = [x.astype(BF16) for x in keys]
        inv_row = [
            lax.rsqrt(jnp.sum(dot_nt(x, x) * eye, 0, keepdims=True) + 1e-06) for x in keys
        ]
        inv_q = lax.rsqrt(jnp.sum(queries * queries, 1, keepdims=True) + 1e-06)
        inner = dot_nt(queries.astype(BF16), jnp.concatenate(keys, 0))
        spread = jnp.concatenate([run_col, run_col], 1) - run_row
        mixing = inner * inv_q * jnp.concatenate(inv_row, 1)
        mixing = jnp.where(seen, jnp.exp(jnp.where(seen, spread, 0.0)) * mixing, 0.0)
        mix_high, mix_low = split(mixing)
        sol_high, sol_low = split(sol_ref[s])
        mixed = dot(mix_high, sol_high) + dot(mix_low, sol_high) + dot(mix_high, sol_low)
        tilde = jnp.exp(run_col) * (queries * inv_q) - mixed[:, :width]
        out_ref[s] = jnp.concatenate([tilde, mixed[:, width:]], 1)
        return carry

    lax.fori_loop(0, heads, one_head, 0, unroll=2)


def chain_kernel(count, *refs):
    held = refs[2 * count]
    width = refs[0].shape[0]
    me = lax.axis_index("seq")
    for s in range(count):
        held[s] = refs[s][...]
    outs = refs[2 * count + 1]
    state = jnp.zeros((width, width), F32)
    for k in range(count):
        outs[lax.rem(k - me + count, count)] = state.astype(BF16)
        if k + 1 < count:
            block = held[lax.rem(me - k + count, count)]
            high, low = split(state)
            both = dot(block[:, :width], jnp.concatenate([high, low], 1))
            state = both[:, :width] + both[:, width:] + block[:, width:].astype(F32)
    for s in range(count):
        refs[count + s][...] = outs[s]


def emit_kernel(exchange, mixed_ref, gain_ref, residual_ref, *refs):
    heads = mixed_ref.shape[0]
    width = mixed_ref.shape[2] // 2
    state_refs, out_ref, row_all = refs[:heads], refs[heads], refs[heads + 1]
    me = lax.axis_index("seq") if exchange else 0
    for s in range(heads):
        row_all[s] = state_refs[s][...]
    for h in range(heads):
        slot_terms = lax.rem(h - me + heads, heads) if exchange else h
        slot_state = lax.rem(me - h + heads, heads) if exchange else h
        mixed = mixed_ref[slot_terms]
        high, low = split(mixed[:, :width])
        state = row_all[slot_state]
        out = dot(
            jnp.concatenate([high, low], 1), jnp.concatenate([state, state], 0)
        ) + mixed[:, width:]
        scale = lax.rsqrt(jnp.mean(out * out, 1, keepdims=True) + 1e-05)
        out = out * scale * gain_ref[...]
        out_ref[h] = (residual_ref[:, h * width : (h + 1) * width].astype(F32) + out).astype(BF16)


def ffn_kernel(count, gain_ref, up_at, down_at, up_hbm, down_hbm, *refs):
    parts, outs = refs[:count], refs[count : 2 * count]
    tiles_in, act, total, up_ref, down_ref, up_sem, down_sem = refs[2 * count :]
    groups, kept, side, _ = up_hbm.shape
    tiles, tokens, _ = tiles_in.shape
    each = tiles // count
    me = lax.axis_index("tensor")
    ups = [pltpu.make_async_copy(up_hbm.at[c], up_ref.at[c], up_sem.at[c]) for c in range(groups)]
    downs = [
        pltpu.make_async_copy(down_hbm.at[c], down_ref.at[c], down_sem.at[c]) for c in range(groups)
    ]
    for copy in ups + downs:
        copy.start()
    squares = jnp.zeros((tokens, side), F32)
    for part in parts:
        for b in range(each):
            wide = part[b].astype(F32)
            squares += wide * wide
    scale = lax.rsqrt(jnp.sum(squares, 1, keepdims=True) / (tiles * side) + 1e-05)
    for m, part in enumerate(parts):
        base = (me ^ m) * each
        for b in range(each):
            gain = gain_ref[pl.ds(base + b, 1), :]
            tiles_in[base + b] = (part[b].astype(F32) * scale * gain).astype(BF16)
    for c in range(groups):
        ups[c].wait()
        picked = jnp.concatenate([tiles_in[up_at[c, j]] for j in range(kept)], 1)
        pre = dot(picked, up_ref[c].reshape(kept * side, side))
        act[c] = jax.nn.gelu(pre).astype(BF16)
    total[...] = jnp.zeros_like(total)
    for c in range(groups):
        downs[c].wait()
        now = act[c]
        for j in range(0, kept, 2):
            both = dot(now, jnp.concatenate([down_ref[c, j], down_ref[c, j + 1]], 1))
            total[down_at[c, j]] += both[:, :side]
            total[down_at[c, j + 1]] += both[:, side:]
    for m, out in enumerate(outs):
        base = (me ^ m) * each
        out[...] = total[pl.ds(base, each)].astype(BF16)


def final_kernel(hidden_ref, *refs):
    out_ref = refs[-1]
    tiles, _, side = hidden_ref.shape
    for b in range(tiles):
        total = refs[0][b].astype(F32)
        for ref in refs[1:-1]:
            total += ref[b].astype(F32)
        out_ref[:, b * side : (b + 1) * side] = (hidden_ref[b].astype(F32) + total).astype(BF16)


def local_call(kernel, out_shape, ins, args, scratch=(), flops=0, moved=0, limit=48 * MIB):
    return pl.pallas_call(
        kernel,
        out_shape=out_shape,
        in_specs=ins,
        out_specs=jax.tree.map(lambda _: VMEM, out_shape),
        scratch_shapes=scratch,
        compiler_params=pltpu.CompilerParams(vmem_limit_bytes=limit),
        cost_estimate=pl.CostEstimate(flops=flops, bytes_accessed=moved, transcendentals=0),
    )(*args)


def prefix_states(terms):
    count, index = lax.axis_size("seq"), lax.axis_index("seq")
    everything = lax.all_gather(jnp.stack(terms), "seq")
    width = terms[0].shape[0]

    def step(k, state):
        block = everything[k]
        new = jnp.einsum(
            "hde,hef->hdf",
            block[..., :width].astype(F32),
            state,
            precision=lax.Precision.HIGHEST,
        ) + block[..., width:].astype(F32)
        return jnp.where(k < index, new, state)

    start = jnp.zeros((len(terms), width, width), F32)
    states = lax.fori_loop(0, count, step, start).astype(BF16)
    return [states[h] for h in range(len(terms))]


def per_device(
    queries, keys, values, beta, decay, out_gain, residual, ffn_gain,
    up_blocks, up_index, down_kept_tiles, down_index,
):
    tokens, heads, width = queries.shape
    seq_count, tensor_count = lax.axis_size("seq"), lax.axis_size("tensor")
    exchange = seq_count == heads
    span = tokens
    term = jax.ShapeDtypeStruct((width, 2 * width), BF16)
    *terms, solved = local_call(
        functools.partial(terms_kernel, exchange),
        [term] * heads + [jax.ShapeDtypeStruct((heads, 2 * span, 2 * width), F32)],
        [VMEM] * 4,
        (beta, decay, keys, values),
        [
            pltpu.VMEM((2, tokens * heads, width), F32),
            pltpu.VMEM((2, tokens * heads, width), F32),
            pltpu.VMEM((5, heads, span), F32),
        ],
        flops=5_000_000_000,
    )
    mixed = local_call(
        functools.partial(mixing_kernel, exchange),
        jax.ShapeDtypeStruct((heads, tokens, 2 * width), F32),
        [VMEM] * 4,
        (decay, queries, keys, solved),
        [
            pltpu.VMEM((tokens * heads, width), F32),
            pltpu.VMEM((2, tokens * heads, width), F32),
            pltpu.VMEM((heads, tokens), F32),
        ],
        flops=5_000_000_000,
    )
    if exchange:
        shifts = [[(k, (k + s) % seq_count) for k in range(seq_count)] for s in range(seq_count)]
        arrived = [terms[0]] + [
            lax.ppermute(terms[s], "seq", shifts[s]) for s in range(1, seq_count)
        ]
        state = jax.ShapeDtypeStruct((width, width), BF16)
        outgoing = local_call(
            functools.partial(chain_kernel, seq_count),
            [state] * seq_count,
            [VMEM] * seq_count,
            arrived,
            [
                pltpu.VMEM((seq_count, width, 2 * width), BF16),
                pltpu.VMEM((seq_count, width, width), BF16),
            ],
        )
        states = [outgoing[0]] + [
            lax.ppermute(outgoing[s], "seq", shifts[s]) for s in range(1, seq_count)
        ]
    else:
        states = prefix_states(terms)
    hidden = local_call(
        functools.partial(emit_kernel, exchange),
        jax.ShapeDtypeStruct((heads, tokens, width), BF16),
        [VMEM] * (3 + heads),
        (mixed, out_gain.reshape(1, width), residual, *states),
        [pltpu.VMEM((heads, width, width), BF16)],
    )

    flips = {
        d: [(k, k ^ d) for k in range(tensor_count)]
        for d in (1 << b for b in range(tensor_count.bit_length() - 1))
    }
    parts = {0: hidden}
    for d in sorted(flips, reverse=True):
        for m in list(parts):
            parts[m | d] = lax.ppermute(parts[m], "tensor", flips[d])
    groups, kept, side, _ = up_blocks.shape
    tiles = heads * tensor_count
    sums = local_call(
        functools.partial(ffn_kernel, tensor_count),
        [jax.ShapeDtypeStruct((heads, tokens, side), BF16)] * tensor_count,
        [VMEM, SMEM, SMEM, ANY, ANY] + [VMEM] * tensor_count,
        (
            ffn_gain.reshape(tiles, side), up_index, down_index, up_blocks, down_kept_tiles,
            *(parts[m] for m in range(tensor_count)),
        ),
        [
            pltpu.VMEM((tiles, tokens, side), BF16),
            pltpu.VMEM((groups, tokens, side), BF16),
            pltpu.VMEM((tiles, tokens, side), F32),
            pltpu.VMEM((groups, kept, side, side), BF16),
            pltpu.VMEM((groups, kept, side, side), BF16),
            pltpu.SemaphoreType.DMA((groups,)),
            pltpu.SemaphoreType.DMA((groups,)),
        ],
    )
    held = {m: [part] for m, part in enumerate(sums)}
    for d in sorted(flips):
        for m in [m for m in held if not m & d]:
            moved = lax.ppermute(added(held.pop(m | d)), "tensor", flips[d])
            held[m].append(moved)
    return local_call(
        final_kernel,
        jax.ShapeDtypeStruct((tokens, heads * side), BF16),
        [VMEM] * (1 + len(held[0])),
        (hidden, *held[0]),
    )


def added(terms):
    if len(terms) == 1:
        return terms[0]
    return sum(term.astype(F32) for term in terms).astype(BF16)


def solution(mesh):
    placed = (
        P("seq", "tensor", None),
        P(None, "seq", "tensor", None),
        P(None, "seq", "tensor", None),
        P(None, "tensor", "seq"),
        P("tensor", "seq"),
        P(),
        P("seq", "tensor"),
        P(),
        P("tensor", None, None, None),
        P("tensor", None),
        P("tensor", None, None, None),
        P("tensor", None),
    )
    return jax.shard_map(
        per_device, mesh=mesh, in_specs=placed, out_specs=P("seq", "tensor"), check_vma=False
    )
```

time: 442 us -> 77.5 us (0.18)
  other arithmetic: 174 us -> 0.07 us
  waiting for transfers between devices: 118 us -> 18.4 us
  local copies, waits for them, and re-layouts: 79.7 us -> 3.5 us
  matrix products: 54.3 us -> 0 us
  starting transfers between devices: 0.13 us -> 29 us
  Pallas kernels: 0 us -> 26.1 us
  between operations: 13.6 us -> 0.13 us
    another operation x2 -> x0, other arithmetic: 158 us -> none  [the longest x1 158 us: block_terms(): solved = jax.scipy.linalg.solve_triangular(system, rhs, lower=True)]
    all_gather x3 -> x0, waiting for transfers between devices: 94.7 us -> none  [the longest x2 94.7 us: entering(): lax.all_gather(part.astype(kind), axis)]
    dot_general x24 -> x0, matrix products: 51.8 us -> none  [the longest x14 15.9 us: product(): jnp.einsum('hde,hef->hdf', left, right, precision=lax.Precision.HIGHEST)]
    scatter x1 -> x0, local copies, waits for them, and re-layouts: 40.5 us -> none  [per_device(): placed = jnp.zeros((group_count, tile_count, tile_side, tile_side), jnp.b...]
    ppermute x0 -> x20, starting transfers between devices: none -> 29 us  [the longest x7 13.8 us: per_device(): lax.ppermute(terms[s], 'seq', shifts[s])]
    pallas_call x0 -> x6, Pallas kernels: none -> 26.1 us  [local_call(): pl.pallas_call(kernel, out_shape=out_shape, in_specs=ins, out_specs=jax.t...]
    reduce_scatter x1 -> x0, waiting for transfers between devices: 23.6 us -> none  [per_device(): lax.psum_scatter(partial_sum.astype(jnp.bfloat16), 'tensor', scatter_dime...]
    transpose x3 -> x0, local copies, waits for them, and re-layouts: 19.5 us -> none  [the longest x1 18.5 us: per_device(): placed.transpose(0, 2, 1, 3)]
  transfers between devices with their start and end apart: 4 -> 20, of which waited for: 3 -> 11; matrix products, arithmetic and copies ran while one was open for 16% -> 0% of each run, Pallas kernels for 0% -> 3%
where the time goes in v1:
time: 77.5 us; the launch traced here: 77.2 us
  starting transfers between devices  29 us (37%)
  Pallas kernels  26.1 us (34%)
  waiting for transfers between devices  18.4 us (24%)
  local copies, waits for them, and re-layouts  3.5 us (5%)
    pallas_call x6, Pallas kernels, local_call(): pl.pallas_call(kernel, out_shape=out_shape, in_specs=ins, out_specs=jax.t...  26.1 us
    ppermute x7, starting transfers between devices, per_device(): lax.ppermute(terms[s], 'seq', shifts[s])  13.8 us
    ppermute x7, starting transfers between devices, per_device(): lax.ppermute(outgoing[s], 'seq', shifts[s])  11.2 us
    ppermute x3, waiting for transfers between devices, per_device(): moved = lax.ppermute(added(held.pop(m | d)), 'tensor', flips[d])  7.73 us
    ppermute x3, waiting for transfers between devices, per_device(): parts[m | d] = lax.ppermute(parts[m], 'tensor', flips[d])  6.26 us
    unnamed x24, local copies, waits for them, and re-layouts  3.5 us
    ppermute x7, waiting for transfers between devices, per_device(): lax.ppermute(terms[s], 'seq', shifts[s])  3.18 us
    ppermute x3, starting transfers between devices, per_device(): moved = lax.ppermute(added(held.pop(m | d)), 'tensor', flips[d])  2.29 us
  transfers between devices with their start and end apart: 20, of which 11 were waited for; matrix products, arithmetic and copies ran while one was open for 0% of the time, Pallas kernels for 3%

profile of v1, /device:TPU:0, one launch (start us, length us, event | category | flops | bytes accessed | tf_op | source)
XLA Modules:
  0.0 77.2 jit_solution(4211406016275957308)
XLA Ops:
  0.0 1.0 %copy-done.5 = bf16[2,128,8,128]{3,2,1,0:T(8,128)(2,1)S(1)} copy-done((bf16[2,128,8,128]{3,2,1,0:T(8,128)(2,1)S(1)}, bf16[2,128,8,128]{3,2,1,0:T(8,128)(2,1)}, u32[]{:S(2)}) %copy-start.5) | copy-done | bytes 524312
  1.0 1.0 %copy-done.6 = bf16[2,128,8,128]{3,2,1,0:T(8,128)(2,1)S(1)} copy-done((bf16[2,128,8,128]{3,2,1,0:T(8,128)(2,1)S(1)}, bf16[2,128,8,128]{3,2,1,0:T(8,128)(2,1)}, u32[]{:S(2)}) %copy-start.6) | copy-done | bytes 524312
  2.1 0.7 copy-done.9
  2.8 0.7 copy-done.10
  3.5 8.4 %shard_map.118 = (bf16[128,256]{1,0:T(8,128)(2,1)S(1)}, bf16[128,256]{1,0:T(8,128)(2,1)S(1)}, bf16[128,256]{1,0:T(8,128)(2,1)S(1)}, bf16[128,256]{1,0:T(8,128)(2...) custom-call(f32[2,8,128]{2,1,0:T(8,128)S(1)} %copy-done.9, ...), custom_call_target="tpu_custom_call" | custom-call | flops 5000000000 | tf_op jit(solution)/shard_map/pallas_call | solution.py:351
  11.9 3.0 %collective-permute-start = (bf16[128,256]{1,0:T(8,128)(2,1)S(1)}, bf16[128,256]{1,0:T(8,128)(2,1)S(1)}, u32[]{:S(2)}, u32[]{:S(2)}) collective-permute-start(bf16[128,256]{1,0:T(8,128)(2,1)S(1)} %get-tuple-element.28), channel_id=1, source_target_pairs={{0,4},{4,8},{8,12},{12,16},{16,20},{20,24},{24,28},{28,0},{1,5},{5... | collective-permute-start | bytes 196616 | tf_op jit(solution)/shard_map/ppermute | solution.py:418
  14.9 1.6 %collective-permute-start.1 = (bf16[128,256]{1,0:T(8,128)(2,1)S(1)}, bf16[128,256]{1,0:T(8,128)(2,1)S(1)}, u32[]{:S(2)}, u32[]{:S(2)}) collective-permute-start(bf16[128,256]{1,0:T(8,128)(2,1)S(1)} %get-tuple-element.29), channel_id=1, source_target_pairs={{0,8},{4,12},{8,16},{12,20},{16,24},{20,28},{24,0},{28,4},{1,9},{5... | collective-permute-start | bytes 196616 | tf_op jit(solution)/shard_map/ppermute | solution.py:418
  16.5 2.6 %collective-permute-start.2 = (bf16[128,256]{1,0:T(8,128)(2,1)S(1)}, bf16[128,256]{1,0:T(8,128)(2,1)S(1)}, u32[]{:S(2)}, u32[]{:S(2)}) collective-permute-start(bf16[128,256]{1,0:T(8,128)(2,1)S(1)} %get-tuple-element.30), channel_id=1, source_target_pairs={{0,12},{4,16},{8,20},{12,24},{16,28},{20,0},{24,4},{28,8},{1,13},{... | collective-permute-start | bytes 196616 | tf_op jit(solution)/shard_map/ppermute | solution.py:418
  19.0 1.2 %collective-permute-start.3 = (bf16[128,256]{1,0:T(8,128)(2,1)S(1)}, bf16[128,256]{1,0:T(8,128)(2,1)S(1)}, u32[]{:S(2)}, u32[]{:S(2)}) collective-permute-start(bf16[128,256]{1,0:T(8,128)(2,1)S(1)} %get-tuple-element.31), channel_id=1, source_target_pairs={{0,16},{4,20},{8,24},{12,28},{16,0},{20,4},{24,8},{28,12},{1,17},{... | collective-permute-start | bytes 196616 | tf_op jit(solution)/shard_map/ppermute | solution.py:418
  20.3 2.6 %collective-permute-start.4 = (bf16[128,256]{1,0:T(8,128)(2,1)S(1)}, bf16[128,256]{1,0:T(8,128)(2,1)S(1)}, u32[]{:S(2)}, u32[]{:S(2)}) collective-permute-start(bf16[128,256]{1,0:T(8,128)(2,1)S(1)} %get-tuple-element.32), channel_id=1, source_target_pairs={{0,20},{4,24},{8,28},{12,0},{16,4},{20,8},{24,12},{28,16},{1,21},{... | collective-permute-start | bytes 196616 | tf_op jit(solution)/shard_map/ppermute | solution.py:418
  22.9 0.0 collective-permute-done.refs_1_
  22.9 1.4 %collective-permute-start.5 = (bf16[128,256]{1,0:T(8,128)(2,1)S(1)}, bf16[128,256]{1,0:T(8,128)(2,1)S(1)}, u32[]{:S(2)}, u32[]{:S(2)}) collective-permute-start(bf16[128,256]{1,0:T(8,128)(2,1)S(1)} %get-tuple-element.33), channel_id=1, source_target_pairs={{0,24},{4,28},{8,0},{12,4},{16,8},{20,12},{24,16},{28,20},{1,25},{... | collective-permute-start | bytes 196616 | tf_op jit(solution)/shard_map/ppermute | solution.py:418
  24.2 0.0 collective-permute-done.1.refs_2_
  24.2 1.4 %collective-permute-start.6 = (bf16[128,256]{1,0:T(8,128)(2,1)S(1)}, bf16[128,256]{1,0:T(8,128)(2,1)S(1)}, u32[]{:S(2)}, u32[]{:S(2)}) collective-permute-start(bf16[128,256]{1,0:T(8,128)(2,1)S(1)} %get-tuple-element.34), channel_id=1, source_target_pairs={{0,28},{4,0},{8,4},{12,8},{16,12},{20,16},{24,20},{28,24},{1,29},{... | collective-permute-start | bytes 196616 | tf_op jit(solution)/shard_map/ppermute | solution.py:418
  25.7 0.5 collective-permute-done.2.refs_3_
  26.2 0.6 collective-permute-done.3.refs_4_
  26.8 0.8 collective-permute-done.4.refs_5_
  27.6 1.3 %collective-permute-done.5.refs_6_ = bf16[128,256]{1,0:T(8,128)(2,1)S(1)} collective-permute-done((bf16[128,256]{1,0:T(8,128)(2,1)S(1)}, bf16[128,256]{1,0:T(8,128)(2,1)S(1)}, u32[]{:S(2)}, u32[]{:S(2)}) %collective-permute-start.5) | collective-permute-done | bytes 65568 | tf_op jit(solution)/shard_map/ppermute | solution.py:418
  28.8 0.0 collective-permute-done.6.refs_7_
  28.8 1.1 %shard_map.120 = (bf16[128,128]{1,0:T(8,128)(2,1)S(1)}, bf16[128,128]{1,0:T(8,128)(2,1)S(1)}, bf16[128,128]{1,0:T(8,128)(2,1)S(1)}, bf16[128,128]{1,0:T(8,128)(2...) custom-call(bf16[128,256]{1,0:T(8,128)(2,1)S(1)} %get-tuple-element., ...), custom_call_target="tpu_custom_call" | custom-call | tf_op jit(solution)/shard_map/pallas_call | solution.py:351
  30.0 2.4 %collective-permute-start.10 = (bf16[128,128]{1,0:T(8,128)(2,1)S(1)}, bf16[128,128]{1,0:T(8,128)(2,1)S(1)}, u32[]{:S(2)}, u32[]{:S(2)}) collective-permute-start(bf16[128,128]{1,0:T(8,128)(2,1)S(1)} %get-tuple-element.39), channel_id=1, source_target_pairs={{0,16},{4,20},{8,24},{12,28},{16,0},{20,4},{24,8},{28,12},{1,17},{... | collective-permute-start | bytes 98312 | tf_op jit(solution)/shard_map/ppermute | solution.py:432
  32.4 2.4 %collective-permute-start.11 = (bf16[128,128]{1,0:T(8,128)(2,1)S(1)}, bf16[128,128]{1,0:T(8,128)(2,1)S(1)}, u32[]{:S(2)}, u32[]{:S(2)}) collective-permute-start(bf16[128,128]{1,0:T(8,128)(2,1)S(1)} %get-tuple-element.40), channel_id=1, source_target_pairs={{0,20},{4,24},{8,28},{12,0},{16,4},{20,8},{24,12},{28,16},{1,21},{... | collective-permute-start | bytes 98312 | tf_op jit(solution)/shard_map/ppermute | solution.py:432
  34.8 2.4 %collective-permute-start.12 = (bf16[128,128]{1,0:T(8,128)(2,1)S(1)}, bf16[128,128]{1,0:T(8,128)(2,1)S(1)}, u32[]{:S(2)}, u32[]{:S(2)}) collective-permute-start(bf16[128,128]{1,0:T(8,128)(2,1)S(1)} %get-tuple-element.41), channel_id=1, source_target_pairs={{0,24},{4,28},{8,0},{12,4},{16,8},{20,12},{24,16},{28,20},{1,25},{... | collective-permute-start | bytes 98312 | tf_op jit(solution)/shard_map/ppermute | solution.py:432
  37.2 0.2 collective-permute-start.13
  37.3 1.9 %collective-permute-start.7 = (bf16[128,128]{1,0:T(8,128)(2,1)S(1)}, bf16[128,128]{1,0:T(8,128)(2,1)S(1)}, u32[]{:S(2)}, u32[]{:S(2)}) collective-permute-start(bf16[128,128]{1,0:T(8,128)(2,1)S(1)} %get-tuple-element.36), channel_id=1, source_target_pairs={{0,4},{4,8},{8,12},{12,16},{16,20},{20,24},{24,28},{28,0},{1,5},{5... | collective-permute-start | bytes 98312 | tf_op jit(solution)/shard_map/ppermute | solution.py:432
  39.2 0.0 collective-permute-done.10.refs_4_
  39.2 0.0 collective-permute-start.8
  39.2 2.0 %collective-permute-start.9 = (bf16[128,128]{1,0:T(8,128)(2,1)S(1)}, bf16[128,128]{1,0:T(8,128)(2,1)S(1)}, u32[]{:S(2)}, u32[]{:S(2)}) collective-permute-start(bf16[128,128]{1,0:T(8,128)(2,1)S(1)} %get-tuple-element.38), channel_id=1, source_target_pairs={{0,12},{4,16},{8,20},{12,24},{16,28},{20,0},{24,4},{28,8},{1,13},{... | collective-permute-start | bytes 98312 | tf_op jit(solution)/shard_map/ppermute | solution.py:432
  41.2 0.0 copy-start.4
  41.2 0.0 copy-start.1
  41.2 0.0 copy-start.2
  41.2 0.0 copy-start.3
  41.2 2.6 %shard_map.119.mixed_ref = f32[8,128,256]{2,1,0:T(8,128)S(1)} custom-call(f32[8,128]{1,0:T(8,128)S(1)} %copy-done.11, bf16[128,8,128]{2,1,0:T(8,128)(2,1)S(1)} %copy-done.8, bf16[2,128,8,128]{3,2,1,0:T(8,128)(2,1)S(1)} %copy-done.7, f32[8,256,256]{2,1,0:T(8,128)S(1)} %get-tuple-element.26.sol_ref), custom_call_target="tpu_custom_call" | custom-call | flops 5000000000 | tf_op jit(solution)/shard_map/pallas_call | solution.py:351
  43.9 0.1 collective-permute-done.7.refs_1_
  44.0 1.0 %collective-permute-done.8.refs_2_ = bf16[128,128]{1,0:T(8,128)(2,1)S(1)} collective-permute-done((bf16[128,128]{1,0:T(8,128)(2,1)S(1)}, bf16[128,128]{1,0:T(8,128)(2,1)S(1)}, u32[]{:S(2)}, u32[]{:S(2)}) %collective-permute-start.8) | collective-permute-done | bytes 32800 | tf_op jit(solution)/shard_map/ppermute | solution.py:432
  44.9 0.2 collective-permute-done.9.refs_3_
  45.2 0.4 shard_map.121.refs_0_.hidden_ref
  45.6 1.7 %collective-permute-start.15 = (bf16[8,128,128]{2,1,0:T(8,128)(2,1)S(1)}, bf16[8,128,128]{2,1,0:T(8,128)(2,1)S(1)}, u32[]{:S(2)}, u32[]{:S(2)}) collective-permute-start(bf16[8,128,128]{2,1,0:T(8,128)(2,1)S(1)} %shard_map.121.refs_0_.hidden_ref), channel_id=1, source_target_pairs={{0,2},{1,3},{2,0},{3,1},{4,6},{5,7},{6,4},{7,5},{8,10},{9,11},{10,... | collective-permute-start | bytes 786440 | tf_op jit(solution)/shard_map/ppermute | solution.py:451
  47.3 4.7 %collective-permute-done.15.refs_2_ = bf16[8,128,128]{2,1,0:T(8,128)(2,1)S(1)} collective-permute-done((bf16[8,128,128]{2,1,0:T(8,128)(2,1)S(1)}, bf16[8,128,128]{2,1,0:T(8,128)(2,1)S(1)}, u32[]{:S(2)}, u32[]{:S(2)}) %collective-permute-start.15) | collective-permute-done | bytes 262176 | tf_op jit(solution)/shard_map/ppermute | solution.py:451
  52.0 1.5 %collective-permute-done.16.refs_3_ = bf16[8,128,128]{2,1,0:T(8,128)(2,1)S(1)} collective-permute-done((bf16[8,128,128]{2,1,0:T(8,128)(2,1)S(1)}, bf16[8,128,128]{2,1,0:T(8,128)(2,1)S(1)}, u32[]{:S(2)}, u32[]{:S(2)}) %collective-permute-start.16) | collective-permute-done | bytes 262176 | tf_op jit(solution)/shard_map/ppermute | solution.py:451
  53.6 12.7 %shard_map.122 = (bf16[8,128,128]{2,1,0:T(8,128)(2,1)S(1)}, bf16[8,128,128]{2,1,0:T(8,128)(2,1)S(1)}, bf16[8,128,128]{2,1,0:T(8,128)(2,1)S(1)}, bf16[8,128,128]{2,1,0:T(8,128)(2,1)S(1)}) custom-call(f32[32,128]{1,0:T(8,128)S(1)} %bitcast.2, s32[16,16]{1,0:T(8,128)S(1)} %copy-done.2, s32[16,16]{1,0:T(8,128)S(1)} %copy-done.3, ...), custom_call_target="tpu_custom_call" | custom-call | tf_op jit(solution)/shard_map/pallas_call | solution.py:351
  66.3 0.2 collective-permute-start.18
  66.5 0.4 collective-permute-start.17
  66.8 1.0 %collective-permute-done.18 = bf16[8,128,128]{2,1,0:T(8,128)(2,1)S(1)} collective-permute-done((bf16[8,128,128]{2,1,0:T(8,128)(2,1)S(1)}, bf16[8,128,128]{2,1,0:T(8,128)(2,1)S(1)}, u32[]{:S(2)}, u32[]{:S(2)}) %collective-permute-start.18) | collective-permute-done | bytes 262176 | tf_op jit(solution)/shard_map/ppermute | solution.py:475
  67.9 0.1 add_convert_fusion
  67.9 1.7 %collective-permute-start.19 = (bf16[8,128,128]{2,1,0:T(8,128)(2,1)S(1)}, bf16[8,128,128]{2,1,0:T(8,128)(2,1)S(1)}, u32[]{:S(2)}, u32[]{:S(2)}) collective-permute-start(bf16[8,128,128]{2,1,0:T(8,128)(2,1)S(1)} %add_convert_fusion), channel_id=1, source_target_pairs={{0,2},{1,3},{2,0},{3,1},{4,6},{5,7},{6,4},{7,5},{8,10},{9,11},{10,... | collective-permute-start | bytes 786440 | tf_op jit(solution)/shard_map/ppermute | solution.py:475
  69.7 6.7 %collective-permute-done.19.refs_2_ = bf16[8,128,128]{2,1,0:T(8,128)(2,1)S(1)} collective-permute-done((bf16[8,128,128]{2,1,0:T(8,128)(2,1)S(1)}, bf16[8,128,128]{2,1,0:T(8,128)(2,1)S(1)}, u32[]{:S(2)}, u32[]{:S(2)}) %collective-permute-start.19) | collective-permute-done | bytes 262176 | tf_op jit(solution)/shard_map/ppermute | solution.py:475
  76.4 0.8 %shard_map.123 = bf16[128,1024]{1,0:T(8,128)(2,1)} custom-call(bf16[8,128,128]{2,1,0:T(8,128)(2,1)S(1)} %shard_map.121.refs_0_.hidden_ref, bf16[8,128,128]{2,1,0:T(8,128)(2,1)S(1)} %get-tuple-element.43.refs_0_, bf16[8,128,128]{2,1,0:T(8,128)(2,1)S(1)} %collective-permute-done.17.refs_1_, bf16[8,128,128]{2,1,0:T(8,128)(2,1)S(1)} %collective-permute-done.19.refs_2_), custom_call_target="tpu_custom_call" | custom-call | tf_op jit(solution)/shard_map/pallas_call | solution.py:351
  (23 shorter events, 0.0 us)
Async XLA Ops:
  0.0 1.0 %copy-start.5 = (bf16[2,128,8,128]{3,2,1,0:T(8,128)(2,1)S(1)}, bf16[2,128,8,128]{3,2,1,0:T(8,128)(2,1)}, u32[]{:S(2)}) copy-start(bf16[2,128,8,128]{3,2,1,0:T(8,128)(2,1)} %v_ref.1) | copy-start | bytes 1572868
  1.0 1.0 %copy-start.6 = (bf16[2,128,8,128]{3,2,1,0:T(8,128)(2,1)S(1)}, bf16[2,128,8,128]{3,2,1,0:T(8,128)(2,1)}, u32[]{:S(2)}) copy-start(bf16[2,128,8,128]{3,2,1,0:T(8,128)(2,1)} %k_ref.3) | copy-start | bytes 1572868
  2.1 0.7 copy-start.9
  2.8 0.7 copy-start.10
  3.5 37.7 %copy-start.7 = (bf16[2,128,8,128]{3,2,1,0:T(8,128)(2,1)S(1)}, bf16[2,128,8,128]{3,2,1,0:T(8,128)(2,1)}, u32[]{:S(2)}) copy-start(bf16[2,128,8,128]{3,2,1,0:T(8,128)(2,1)} %k_ref.3) | copy-start | bytes 1572868
  3.5 37.7 %copy-start.8 = (bf16[128,8,128]{2,1,0:T(8,128)(2,1)S(1)}, bf16[128,8,128]{2,1,0:T(8,128)(2,1)}, u32[]{:S(2)}) copy-start(bf16[128,8,128]{2,1,0:T(8,128)(2,1)} %q_ref.1) | copy-start | bytes 786436
  3.5 37.7 %copy-start.11 = (f32[8,128]{1,0:T(8,128)S(1)}, f32[8,128]{1,0:T(8,128)}, u32[]{:S(2)}) copy-start(f32[8,128]{1,0:T(8,128)} %decay_ref.3) | copy-start | bytes 12292
  11.9 11.0 %collective-permute-start = (bf16[128,256]{1,0:T(8,128)(2,1)S(1)}, bf16[128,256]{1,0:T(8,128)(2,1)S(1)}, u32[]{:S(2)}, u32[]{:S(2)}) collective-permute-start(bf16[128,256]{1,0:T(8,128)(2,1)S(1)} %get-tuple-element.28), channel_id=1, source_target_pairs={{0,4},{4,8},{8,12},{12,16},{16,20},{20,24},{24,28},{28,0},{1,5},{5... | collective-permute-start | bytes 196616 | tf_op jit(solution)/shard_map/ppermute | solution.py:418
  14.9 9.4 %collective-permute-start.1 = (bf16[128,256]{1,0:T(8,128)(2,1)S(1)}, bf16[128,256]{1,0:T(8,128)(2,1)S(1)}, u32[]{:S(2)}, u32[]{:S(2)}) collective-permute-start(bf16[128,256]{1,0:T(8,128)(2,1)S(1)} %get-tuple-element.29), channel_id=1, source_target_pairs={{0,8},{4,12},{8,16},{12,20},{16,24},{20,28},{24,0},{28,4},{1,9},{5... | collective-permute-start | bytes 196616 | tf_op jit(solution)/shard_map/ppermute | solution.py:418
  16.5 9.7 %collective-permute-start.2 = (bf16[128,256]{1,0:T(8,128)(2,1)S(1)}, bf16[128,256]{1,0:T(8,128)(2,1)S(1)}, u32[]{:S(2)}, u32[]{:S(2)}) collective-permute-start(bf16[128,256]{1,0:T(8,128)(2,1)S(1)} %get-tuple-element.30), channel_id=1, source_target_pairs={{0,12},{4,16},{8,20},{12,24},{16,28},{20,0},{24,4},{28,8},{1,13},{... | collective-permute-start | bytes 196616 | tf_op jit(solution)/shard_map/ppermute | solution.py:418
  19.0 7.8 %collective-permute-start.3 = (bf16[128,256]{1,0:T(8,128)(2,1)S(1)}, bf16[128,256]{1,0:T(8,128)(2,1)S(1)}, u32[]{:S(2)}, u32[]{:S(2)}) collective-permute-start(bf16[128,256]{1,0:T(8,128)(2,1)S(1)} %get-tuple-element.31), channel_id=1, source_target_pairs={{0,16},{4,20},{8,24},{12,28},{16,0},{20,4},{24,8},{28,12},{1,17},{... | collective-permute-start | bytes 196616 | tf_op jit(solution)/shard_map/ppermute | solution.py:418
  20.3 7.3 %collective-permute-start.4 = (bf16[128,256]{1,0:T(8,128)(2,1)S(1)}, bf16[128,256]{1,0:T(8,128)(2,1)S(1)}, u32[]{:S(2)}, u32[]{:S(2)}) collective-permute-start(bf16[128,256]{1,0:T(8,128)(2,1)S(1)} %get-tuple-element.32), channel_id=1, source_target_pairs={{0,20},{4,24},{8,28},{12,0},{16,4},{20,8},{24,12},{28,16},{1,21},{... | collective-permute-start | bytes 196616 | tf_op jit(solution)/shard_map/ppermute | solution.py:418
  22.9 6.0 %collective-permute-start.5 = (bf16[128,256]{1,0:T(8,128)(2,1)S(1)}, bf16[128,256]{1,0:T(8,128)(2,1)S(1)}, u32[]{:S(2)}, u32[]{:S(2)}) collective-permute-start(bf16[128,256]{1,0:T(8,128)(2,1)S(1)} %get-tuple-element.33), channel_id=1, source_target_pairs={{0,24},{4,28},{8,0},{12,4},{16,8},{20,12},{24,16},{28,20},{1,25},{... | collective-permute-start | bytes 196616 | tf_op jit(solution)/shard_map/ppermute | solution.py:418
  24.2 4.6 %collective-permute-start.6 = (bf16[128,256]{1,0:T(8,128)(2,1)S(1)}, bf16[128,256]{1,0:T(8,128)(2,1)S(1)}, u32[]{:S(2)}, u32[]{:S(2)}) collective-permute-start(bf16[128,256]{1,0:T(8,128)(2,1)S(1)} %get-tuple-element.34), channel_id=1, source_target_pairs={{0,28},{4,0},{8,4},{12,8},{16,12},{20,16},{24,20},{28,24},{1,29},{... | collective-permute-start | bytes 196616 | tf_op jit(solution)/shard_map/ppermute | solution.py:418
  30.0 9.2 %collective-permute-start.10 = (bf16[128,128]{1,0:T(8,128)(2,1)S(1)}, bf16[128,128]{1,0:T(8,128)(2,1)S(1)}, u32[]{:S(2)}, u32[]{:S(2)}) collective-permute-start(bf16[128,128]{1,0:T(8,128)(2,1)S(1)} %get-tuple-element.39), channel_id=1, source_target_pairs={{0,16},{4,20},{8,24},{12,28},{16,0},{20,4},{24,8},{28,12},{1,17},{... | collective-permute-start | bytes 98312 | tf_op jit(solution)/shard_map/ppermute | solution.py:432
  32.4 6.8 %collective-permute-start.11 = (bf16[128,128]{1,0:T(8,128)(2,1)S(1)}, bf16[128,128]{1,0:T(8,128)(2,1)S(1)}, u32[]{:S(2)}, u32[]{:S(2)}) collective-permute-start(bf16[128,128]{1,0:T(8,128)(2,1)S(1)} %get-tuple-element.40), channel_id=1, source_target_pairs={{0,20},{4,24},{8,28},{12,0},{16,4},{20,8},{24,12},{28,16},{1,21},{... | collective-permute-start | bytes 98312 | tf_op jit(solution)/shard_map/ppermute | solution.py:432
  34.8 9.1 %collective-permute-start.12 = (bf16[128,128]{1,0:T(8,128)(2,1)S(1)}, bf16[128,128]{1,0:T(8,128)(2,1)S(1)}, u32[]{:S(2)}, u32[]{:S(2)}) collective-permute-start(bf16[128,128]{1,0:T(8,128)(2,1)S(1)} %get-tuple-element.41), channel_id=1, source_target_pairs={{0,24},{4,28},{8,0},{12,4},{16,8},{20,12},{24,16},{28,20},{1,25},{... | collective-permute-start | bytes 98312 | tf_op jit(solution)/shard_map/ppermute | solution.py:432
  37.2 6.7 %collective-permute-start.13 = (bf16[128,128]{1,0:T(8,128)(2,1)S(1)}, bf16[128,128]{1,0:T(8,128)(2,1)S(1)}, u32[]{:S(2)}, u32[]{:S(2)}) collective-permute-start(bf16[128,128]{1,0:T(8,128)(2,1)S(1)} %get-tuple-element.42), channel_id=1, source_target_pairs={{0,28},{4,0},{8,4},{12,8},{16,12},{20,16},{24,20},{28,24},{1,29},{... | collective-permute-start | bytes 98312 | tf_op jit(solution)/shard_map/ppermute | solution.py:432
  37.3 6.6 %collective-permute-start.7 = (bf16[128,128]{1,0:T(8,128)(2,1)S(1)}, bf16[128,128]{1,0:T(8,128)(2,1)S(1)}, u32[]{:S(2)}, u32[]{:S(2)}) collective-permute-start(bf16[128,128]{1,0:T(8,128)(2,1)S(1)} %get-tuple-element.36), channel_id=1, source_target_pairs={{0,4},{4,8},{8,12},{12,16},{16,20},{20,24},{24,28},{28,0},{1,5},{5... | collective-permute-start | bytes 98312 | tf_op jit(solution)/shard_map/ppermute | solution.py:432
  39.2 5.7 %collective-permute-start.8 = (bf16[128,128]{1,0:T(8,128)(2,1)S(1)}, bf16[128,128]{1,0:T(8,128)(2,1)S(1)}, u32[]{:S(2)}, u32[]{:S(2)}) collective-permute-start(bf16[128,128]{1,0:T(8,128)(2,1)S(1)} %get-tuple-element.37), channel_id=1, source_target_pairs={{0,8},{4,12},{8,16},{12,20},{16,24},{20,28},{24,0},{28,4},{1,9},{5... | collective-permute-start | bytes 98312 | tf_op jit(solution)/shard_map/ppermute | solution.py:432
  39.2 5.9 %collective-permute-start.9 = (bf16[128,128]{1,0:T(8,128)(2,1)S(1)}, bf16[128,128]{1,0:T(8,128)(2,1)S(1)}, u32[]{:S(2)}, u32[]{:S(2)}) collective-permute-start(bf16[128,128]{1,0:T(8,128)(2,1)S(1)} %get-tuple-element.38), channel_id=1, source_target_pairs={{0,12},{4,16},{8,20},{12,24},{16,28},{20,0},{24,4},{28,8},{1,13},{... | collective-permute-start | bytes 98312 | tf_op jit(solution)/shard_map/ppermute | solution.py:432
  41.2 4.0 %copy-start = (bf16[128,1024]{1,0:T(8,128)(2,1)S(1)}, bf16[128,1024]{1,0:T(8,128)(2,1)}, u32[]{:S(2)}) copy-start(bf16[128,1024]{1,0:T(8,128)(2,1)} %residual_ref.1) | copy-start | bytes 786436
  41.2 4.0 %copy-start.4 = (f32[128]{0:T(128)S(1)}, f32[128]{0:T(128)}, u32[]{:S(2)}) copy-start(f32[128]{0:T(128)} %param.17) | copy-start | bytes 1540
  41.2 12.4 %copy-start.1 = (f32[4096]{0:T(1024)S(1)}, f32[4096]{0:T(1024)}, u32[]{:S(2)}) copy-start(f32[4096]{0:T(1024)} %param.19) | copy-start | bytes 49156
  41.2 12.4 %copy-start.2 = (s32[16,16]{1,0:T(8,128)S(1)}, s32[16,16]{1,0:T(8,128)}, u32[]{:S(2)}) copy-start(s32[16,16]{1,0:T(8,128)} %up_at.1) | copy-start | bytes 3076
  41.2 12.3 %copy-start.3 = (s32[16,16]{1,0:T(8,128)S(1)}, s32[16,16]{1,0:T(8,128)}, u32[]{:S(2)}) copy-start(s32[16,16]{1,0:T(8,128)} %down_at.1) | copy-start | bytes 3076
  45.6 6.4 %collective-permute-start.15 = (bf16[8,128,128]{2,1,0:T(8,128)(2,1)S(1)}, bf16[8,128,128]{2,1,0:T(8,128)(2,1)S(1)}, u32[]{:S(2)}, u32[]{:S(2)}) collective-permute-start(bf16[8,128,128]{2,1,0:T(8,128)(2,1)S(1)} %shard_map.121.refs_0_.hidden_ref), channel_id=1, source_target_pairs={{0,2},{1,3},{2,0},{3,1},{4,6},{5,7},{6,4},{7,5},{8,10},{9,11},{10,... | collective-permute-start | bytes 786440 | tf_op jit(solution)/shard_map/ppermute | solution.py:451
  47.3 4.7 %collective-permute-start.14 = (bf16[8,128,128]{2,1,0:T(8,128)(2,1)S(1)}, bf16[8,128,128]{2,1,0:T(8,128)(2,1)S(1)}, u32[]{:S(2)}, u32[]{:S(2)}) collective-permute-start(bf16[8,128,128]{2,1,0:T(8,128)(2,1)S(1)} %shard_map.121.refs_0_.hidden_ref), channel_id=1, source_target_pairs={{0,1},{1,0},{2,3},{3,2},{4,5},{5,4},{6,7},{7,6},{8,9},{9,8},{10,11... | collective-permute-start | bytes 786440 | tf_op jit(solution)/shard_map/ppermute | solution.py:451
  52.0 1.5 %collective-permute-start.16 = (bf16[8,128,128]{2,1,0:T(8,128)(2,1)S(1)}, bf16[8,128,128]{2,1,0:T(8,128)(2,1)S(1)}, u32[]{:S(2)}, u32[]{:S(2)}) collective-permute-start(bf16[8,128,128]{2,1,0:T(8,128)(2,1)S(1)} %collective-permute-done.15.refs_2_), channel_id=1, source_target_pairs={{0,1},{1,0},{2,3},{3,2},{4,5},{5,4},{6,7},{7,6},{8,9},{9,8},{10,11... | collective-permute-start | bytes 786440 | tf_op jit(solution)/shard_map/ppermute | solution.py:451
  66.3 1.6 %collective-permute-start.18 = (bf16[8,128,128]{2,1,0:T(8,128)(2,1)S(1)}, bf16[8,128,128]{2,1,0:T(8,128)(2,1)S(1)}, u32[]{:S(2)}, u32[]{:S(2)}) collective-permute-start(bf16[8,128,128]{2,1,0:T(8,128)(2,1)S(1)} %get-tuple-element.46), channel_id=1, source_target_pairs={{0,1},{1,0},{2,3},{3,2},{4,5},{5,4},{6,7},{7,6},{8,9},{9,8},{10,11... | collective-permute-start | bytes 786440 | tf_op jit(solution)/shard_map/ppermute | solution.py:475
  66.5 3.2 %collective-permute-start.17 = (bf16[8,128,128]{2,1,0:T(8,128)(2,1)S(1)}, bf16[8,128,128]{2,1,0:T(8,128)(2,1)S(1)}, u32[]{:S(2)}, u32[]{:S(2)}) collective-permute-start(bf16[8,128,128]{2,1,0:T(8,128)(2,1)S(1)} %get-tuple-element.44), channel_id=1, source_target_pairs={{0,1},{1,0},{2,3},{3,2},{4,5},{5,4},{6,7},{7,6},{8,9},{9,8},{10,11... | collective-permute-start | bytes 786440 | tf_op jit(solution)/shard_map/ppermute | solution.py:475
  67.9 8.4 %collective-permute-start.19 = (bf16[8,128,128]{2,1,0:T(8,128)(2,1)S(1)}, bf16[8,128,128]{2,1,0:T(8,128)(2,1)S(1)}, u32[]{:S(2)}, u32[]{:S(2)}) collective-permute-start(bf16[8,128,128]{2,1,0:T(8,128)(2,1)S(1)} %add_convert_fusion), channel_id=1, source_target_pairs={{0,2},{1,3},{2,0},{3,1},{4,6},{5,7},{6,4},{7,5},{8,10},{9,11},{10,... | collective-permute-start | bytes 786440 | tf_op jit(solution)/shard_map/ppermute | solution.py:475

commit v2 on v1

--- a/solution.py
+++ b/solution.py
@@ -10,6 +10,9 @@
 F32 = jnp.float32
 BF16 = jnp.bfloat16
 HEAD_GROUP = 4
+PER_SLOT = 2
+CUTS = (2, 3)
+FIRST_LIMIT = 20 * (1 << 20)
 MIB = 1 << 20
 VMEM = pl.BlockSpec(memory_space=pltpu.VMEM)
 SMEM = pl.BlockSpec(memory_space=pltpu.SMEM)
@@ -75,26 +78,58 @@
     ]
 
 
-def terms_kernel(exchange, beta_ref, decay_ref, k_ref, v_ref, *refs):
-    heads, tokens = decay_ref.shape
-    width = k_ref.shape[-1]
+def head_of(exchange, slot, u):
+    if exchange:
+        return PER_SLOT * (lax.rem(lax.axis_index("seq"), exchange) ^ slot) + u
+    return PER_SLOT * slot + u
+
+
+def first_kernel(exchange, order, beta_hbm, decay_hbm, k_hbm, v_hbm, *refs):
+    _, heads, tokens = beta_hbm.shape
+    width = k_hbm.shape[-1]
     half = tokens // 2
-    span = 2 * half
-    out_refs, sol_ref = refs[:heads], refs[heads]
-    k_all, v_all, row_ref = refs[heads + 1 :]
-    me = lax.axis_index("seq") if exchange else 0
-    for j in range(2):
-        k_all[j] = k_ref[j].astype(F32).reshape(tokens * heads, width)
-        v_all[j] = v_ref[j].astype(F32).reshape(tokens * heads, width)
+    out_refs, (sol_ref, k_heads, v_heads, row_ref) = refs[: len(order)], refs[len(order) :][:4]
+    beta_ref, decay_ref, k_ref, v_ref, k_all, v_all, sems = refs[len(order) + 4 :]
+    copies = [
+        pltpu.make_async_copy(source, target, sems.at[n])
+        for n, (source, target) in enumerate(
+            ((beta_hbm, beta_ref), (decay_hbm, decay_ref), (k_hbm, k_ref), (v_hbm, v_ref))
+        )
+    ]
+    for copy in copies:
+        copy.start()
+    for copy in copies[:2]:
+        copy.wait()
     run = running_rows(decay_ref)
     run_half = doubled(run, half)
     beta_half = stacked_beta(beta_ref, half)
-    last = jnp.broadcast_to(run[:, tokens - 1 :], (heads, span))
     for i in range(2):
         row_ref[i] = run_half[i]
         row_ref[2 + i] = beta_half[i]
-    row_ref[4] = last
-
+    row_ref[4] = jnp.broadcast_to(run[:, tokens - 1 :], (heads, 2 * half))
+    row_ref[5] = run
+    for copy, source, wide, target in (
+        (copies[2], k_ref, k_all, k_heads),
+        (copies[3], v_ref, v_all, v_heads),
+    ):
+        copy.wait()
+        for j in range(2):
+            wide[j] = source[j].astype(F32).reshape(tokens * heads, width)
+        for h in range(heads):
+            rows = stacked(*(head_rows(wide.at[j], h, heads) for j in range(2)))
+            for i in range(2):
+                target[h, i] = rows[i].astype(BF16)
+    solve_heads(exchange, order, k_heads, v_heads, row_ref, out_refs, sol_ref)
+
+
+def later_kernel(exchange, order, k_heads, v_heads, row_ref, *refs):
+    out_refs, sol_ref = refs[: len(order)], refs[len(order)]
+    solve_heads(exchange, order, k_heads, v_heads, row_ref, out_refs, sol_ref)
+
+
+def solve_heads(exchange, order, k_heads, v_heads, row_ref, out_refs, sol_ref):
+    span, width = k_heads.shape[2:]
+    half = span // 2
     row_at = lax.broadcasted_iota(jnp.int32, (span, span), 0)
     col_at = lax.broadcasted_iota(jnp.int32, (span, span), 1)
     row_time = 2 * lax.rem(row_at, half) + row_at // half
@@ -105,15 +140,13 @@
     eye_wide = eye[:width, :width]
     left = col_at < half
 
-    for start in range(0, heads, HEAD_GROUP):
-        slots = range(start, min(start + HEAD_GROUP, heads))
+    places = [(n, u) for n in range(len(order)) for u in range(PER_SLOT)]
+    for start in range(0, len(places), HEAD_GROUP):
         chains = []
-        for s in slots:
-            h = lax.rem(me + s, heads)
-            keys = stacked(*(head_rows(k_all.at[j], h, heads) for j in range(2)))
-            values = stacked(*(head_rows(v_all.at[j], h, heads) for j in range(2)))
-            keys = [x.astype(BF16) for x in keys]
-            values = [x.astype(BF16) for x in values]
+        for s in places[start : start + HEAD_GROUP]:
+            h = head_of(exchange, order[s[0]], s[1])
+            keys = [k_heads[h, i] for i in range(2)]
+            values = [v_heads[h, i] for i in range(2)]
             run_row = [row_ref[i, pl.ds(h, 1), :] for i in range(2)]
             beta_row = [row_ref[2 + i, pl.ds(h, 1), :] for i in range(2)]
             run_col = [column(x) for x in run_row]
@@ -187,7 +220,8 @@
             rows = [jnp.concatenate([solved[0][i], solved[1][i]], 1) for i in range(2)]
             c["rows"] = rows
             for i in range(2):
-                sol_ref[c["s"], i * span : (i + 1) * span, :] = rows[i]
+                at = PER_SLOT * c["s"][0] + c["s"][1]
+                sol_ref[at, i * span : (i + 1) * span, :] = rows[i]
         for c in chains:
             last_col = column(c["last_row"])
             weighted = []
@@ -199,7 +233,8 @@
             ends = dot_tn(keys, high) + dot_tn(keys, low)
             gate = jnp.exp(c["last_row"])
             trans = eye_wide * gate - ends[:, :width]
-            out_refs[c["s"]][...] = jnp.concatenate([trans, ends[:, width:]], 1).astype(BF16)
+            slot, u = c["s"]
+            out_refs[slot][u] = jnp.concatenate([trans, ends[:, width:]], 1).astype(BF16)
 
 
 def stacked_beta(beta_ref, half):
@@ -212,16 +247,12 @@
     ]
 
 
-def mixing_kernel(exchange, decay_ref, q_ref, k_ref, sol_ref, out_ref, q_all, k_all, run_ref):
-    heads, tokens = decay_ref.shape
-    width = k_ref.shape[-1]
+def mixing_kernel(exchange, orders, q_ref, k_heads, row_ref, *refs):
+    sol_refs, (out_ref, q_all) = refs[: len(orders)], refs[len(orders) :]
+    tokens, heads, width = q_ref.shape
     half = tokens // 2
     span = 2 * half
-    me = lax.axis_index("seq") if exchange else 0
     q_all[...] = q_ref[...].astype(F32).reshape(tokens * heads, width)
-    for j in range(2):
-        k_all[j] = k_ref[j].astype(F32).reshape(tokens * heads, width)
-    run_ref[...] = running_rows(decay_ref)
     token_at = lax.broadcasted_iota(jnp.int32, (tokens, 2 * span), 0)
     row_at = lax.broadcasted_iota(jnp.int32, (tokens, 2 * span), 1)
     seen = (row_at // span) * half + lax.rem(row_at, half) <= token_at
@@ -229,14 +260,11 @@
     col_at = lax.broadcasted_iota(jnp.int32, (span, span), 1)
     eye = (row_at == col_at).astype(F32)
 
-    def one_head(s, carry):
-        h = lax.rem(me + s, heads)
+    def one_head(sol_ref, s, at, h):
         queries = head_rows(q_all, h, heads)
-        keys = stacked(*(head_rows(k_all.at[j], h, heads) for j in range(2)))
-        run = run_ref[pl.ds(h, 1), :]
-        run_col = column(run)
-        run_row = jnp.concatenate(doubled(run, half), 1)
-        keys = [x.astype(BF16) for x in keys]
+        keys = [k_heads[h, i] for i in range(2)]
+        run_col = column(row_ref[5, pl.ds(h, 1), :])
+        run_row = jnp.concatenate([row_ref[i, pl.ds(h, 1), :] for i in range(2)], 1)
         inv_row = [
             lax.rsqrt(jnp.sum(dot_nt(x, x) * eye, 0, keepdims=True) + 1e-06) for x in keys
         ]
@@ -249,65 +277,77 @@
         sol_high, sol_low = split(sol_ref[s])
         mixed = dot(mix_high, sol_high) + dot(mix_low, sol_high) + dot(mix_high, sol_low)
         tilde = jnp.exp(run_col) * (queries * inv_q) - mixed[:, :width]
-        out_ref[s] = jnp.concatenate([tilde, mixed[:, width:]], 1)
-        return carry
-
-    lax.fori_loop(0, heads, one_head, 0, unroll=2)
-
-
-def chain_kernel(count, *refs):
-    held = refs[2 * count]
-    width = refs[0].shape[0]
-    me = lax.axis_index("seq")
-    for s in range(count):
-        held[s] = refs[s][...]
-    outs = refs[2 * count + 1]
-    state = jnp.zeros((width, width), F32)
-    for k in range(count):
-        outs[lax.rem(k - me + count, count)] = state.astype(BF16)
-        if k + 1 < count:
-            block = held[lax.rem(me - k + count, count)]
-            high, low = split(state)
-            both = dot(block[:, :width], jnp.concatenate([high, low], 1))
-            state = both[:, :width] + both[:, width:] + block[:, width:].astype(F32)
-    for s in range(count):
-        refs[count + s][...] = outs[s]
-
-
-def emit_kernel(exchange, mixed_ref, gain_ref, residual_ref, *refs):
-    heads = mixed_ref.shape[0]
+        out_ref[at] = jnp.concatenate([tilde, mixed[:, width:]], 1)
+
+    at = 0
+    for order, sol_ref in zip(orders, sol_refs):
+        for n, slot in enumerate(order):
+            for u in range(PER_SLOT):
+                one_head(sol_ref, PER_SLOT * n + u, at, head_of(exchange, slot, u))
+                at += 1
+
+
+def chain_kernel(group, *refs):
+    term_refs, (local_ref, prefix_ref, end_ref) = refs[:group], refs[group : group + 3]
+    held = refs[group + 3]
+    width = term_refs[0].shape[1]
+    me = lax.rem(lax.axis_index("seq"), group)
+    for s in range(group):
+        held[s] = term_refs[s][...]
+    for u in range(PER_SLOT):
+        first = held[me, u]
+        state = first[:, width:].astype(F32)
+        prefix = first[:, :width].astype(F32)
+        for k in range(1, group):
+            local_ref[k - 1, u] = state
+            prefix_ref[k - 1, u] = prefix
+            block = held[me ^ k, u]
+            both = dot(block[:, :width], jnp.concatenate([*split(state), *split(prefix)], 1))
+            state = both[:, :width] + both[:, width : 2 * width] + block[:, width:].astype(F32)
+            prefix = both[:, 2 * width : 3 * width] + both[:, 3 * width :]
+        end_ref[u] = state.astype(BF16)
+
+
+def entry_kernel(group, local_ref, prefix_ref, before_ref, *refs):
+    out_refs, held = refs[:group], refs[group]
+    me = lax.rem(lax.axis_index("seq"), group)
+    for u in range(PER_SLOT):
+        before = before_ref[u]
+        held[0, u] = before
+        for k in range(1, group):
+            high, low = split(prefix_ref[k - 1, u])
+            state = dot(
+                jnp.concatenate([high, low], 1), jnp.concatenate([before, before], 0)
+            ) + local_ref[k - 1, u]
+            held[k, u] = state.astype(BF16)
+    for s in range(group):
+        out_refs[s][...] = held[me ^ s]
+
+
+def emit_kernel(exchange, order, mixed_ref, gain_ref, residual_ref, *refs):
     width = mixed_ref.shape[2] // 2
-    state_refs, out_ref, row_all = refs[:heads], refs[heads], refs[heads + 1]
-    me = lax.axis_index("seq") if exchange else 0
-    for s in range(heads):
-        row_all[s] = state_refs[s][...]
-    for h in range(heads):
-        slot_terms = lax.rem(h - me + heads, heads) if exchange else h
-        slot_state = lax.rem(me - h + heads, heads) if exchange else h
-        mixed = mixed_ref[slot_terms]
-        high, low = split(mixed[:, :width])
-        state = row_all[slot_state]
-        out = dot(
-            jnp.concatenate([high, low], 1), jnp.concatenate([state, state], 0)
-        ) + mixed[:, width:]
-        scale = lax.rsqrt(jnp.mean(out * out, 1, keepdims=True) + 1e-05)
-        out = out * scale * gain_ref[...]
-        out_ref[h] = (residual_ref[:, h * width : (h + 1) * width].astype(F32) + out).astype(BF16)
-
-
-def ffn_kernel(count, gain_ref, up_at, down_at, up_hbm, down_hbm, *refs):
+    state_refs, out_ref = refs[: len(order)], refs[len(order)]
+    for n, slot in enumerate(order):
+        for u in range(PER_SLOT):
+            h = head_of(exchange, slot, u)
+            mixed = mixed_ref[PER_SLOT * n + u]
+            state = state_refs[slot][u]
+            out = dot(
+                jnp.concatenate(split(mixed[:, :width]), 1), jnp.concatenate([state, state], 0)
+            ) + mixed[:, width:]
+            scale = lax.rsqrt(jnp.mean(out * out, 1, keepdims=True) + 1e-05)
+            out = out * scale * gain_ref[...]
+            columns = pl.ds(pl.multiple_of(h * width, width), width)
+            out_ref[h] = (residual_ref[:, columns].astype(F32) + out).astype(BF16)
+
+
+def ffn_kernel(count, gain_ref, up_at, down_at, up_ref, down_ref, *refs):
     parts, outs = refs[:count], refs[count : 2 * count]
-    tiles_in, act, total, up_ref, down_ref, up_sem, down_sem = refs[2 * count :]
-    groups, kept, side, _ = up_hbm.shape
+    tiles_in, act, total = refs[2 * count :]
+    groups, kept, side, _ = up_ref.shape
     tiles, tokens, _ = tiles_in.shape
     each = tiles // count
     me = lax.axis_index("tensor")
-    ups = [pltpu.make_async_copy(up_hbm.at[c], up_ref.at[c], up_sem.at[c]) for c in range(groups)]
-    downs = [
-        pltpu.make_async_copy(down_hbm.at[c], down_ref.at[c], down_sem.at[c]) for c in range(groups)
-    ]
-    for copy in ups + downs:
-        copy.start()
     squares = jnp.zeros((tokens, side), F32)
     for part in parts:
         for b in range(each):
@@ -320,13 +360,11 @@
             gain = gain_ref[pl.ds(base + b, 1), :]
             tiles_in[base + b] = (part[b].astype(F32) * scale * gain).astype(BF16)
     for c in range(groups):
-        ups[c].wait()
         picked = jnp.concatenate([tiles_in[up_at[c, j]] for j in range(kept)], 1)
         pre = dot(picked, up_ref[c].reshape(kept * side, side))
         act[c] = jax.nn.gelu(pre).astype(BF16)
     total[...] = jnp.zeros_like(total)
     for c in range(groups):
-        downs[c].wait()
         now = act[c]
         for j in range(0, kept, 2):
             both = dot(now, jnp.concatenate([down_ref[c, j], down_ref[c, j + 1]], 1))
@@ -347,7 +385,7 @@
         out_ref[:, b * side : (b + 1) * side] = (hidden_ref[b].astype(F32) + total).astype(BF16)
 
 
-def local_call(kernel, out_shape, ins, args, scratch=(), flops=0, moved=0, limit=48 * MIB):
+def local_call(kernel, out_shape, ins, args, scratch=(), flops=0, moved=0, limit=20 * MIB):
     return pl.pallas_call(
         kernel,
         out_shape=out_shape,
@@ -361,22 +399,23 @@
 
 def prefix_states(terms):
     count, index = lax.axis_size("seq"), lax.axis_index("seq")
-    everything = lax.all_gather(jnp.stack(terms), "seq")
-    width = terms[0].shape[0]
+    own = jnp.stack([terms[s] for s in sorted(terms)])
+    everything = lax.all_gather(own, "seq")
+    width = own.shape[2]
 
     def step(k, state):
         block = everything[k]
         new = jnp.einsum(
-            "hde,hef->hdf",
+            "sude,suef->sudf",
             block[..., :width].astype(F32),
             state,
             precision=lax.Precision.HIGHEST,
         ) + block[..., width:].astype(F32)
         return jnp.where(k < index, new, state)
 
-    start = jnp.zeros((len(terms), width, width), F32)
+    start = jnp.zeros((*own.shape[:3], width), F32)
     states = lax.fori_loop(0, count, step, start).astype(BF16)
-    return [states[h] for h in range(len(terms))]
+    return {s: states[s] for s in range(len(terms))}
 
 
 def per_device(
@@ -385,60 +424,86 @@
 ):
     tokens, heads, width = queries.shape
     seq_count, tensor_count = lax.axis_size("seq"), lax.axis_size("tensor")
-    exchange = seq_count == heads
-    span = tokens
-    term = jax.ShapeDtypeStruct((width, 2 * width), BF16)
-    *terms, solved = local_call(
-        functools.partial(terms_kernel, exchange),
-        [term] * heads + [jax.ShapeDtypeStruct((heads, 2 * span, 2 * width), F32)],
-        [VMEM] * 4,
-        (beta, decay, keys, values),
-        [
-            pltpu.VMEM((2, tokens * heads, width), F32),
-            pltpu.VMEM((2, tokens * heads, width), F32),
-            pltpu.VMEM((5, heads, span), F32),
-        ],
-        flops=5_000_000_000,
-    )
+    slots = heads // PER_SLOT
+    exchange = slots if seq_count == 2 * slots and slots & (slots - 1) == 0 else 0
+    order = sorted(range(slots), key=lambda s: -(s & 1) * slots - s)
+    cuts = [0, *(n for n in CUTS if n < slots), slots]
+    orders = [order[n:m] for n, m in zip(cuts, cuts[1:])]
+    swaps = [[(k, k ^ s) for k in range(seq_count)] for s in range(slots)]
+    term = jax.ShapeDtypeStruct((PER_SLOT, width, 2 * width), BF16)
+    by_head = jax.ShapeDtypeStruct((heads, 2, tokens, width), BF16)
+    rows = jax.ShapeDtypeStruct((6, heads, tokens), F32)
+    terms, solved, arrived = {}, [], {}
+    for part in orders:
+        solution_rows = jax.ShapeDtypeStruct(
+            (PER_SLOT * len(part), 2 * tokens, 2 * width), F32
+        )
+        outs = [term] * len(part) + [solution_rows]
+        if not terms:
+            *given, sol, k_heads, v_heads, row_terms = local_call(
+                functools.partial(first_kernel, exchange, part),
+                outs + [by_head, by_head, rows],
+                [ANY] * 4,
+                (beta, decay, keys, values),
+                [
+                    pltpu.VMEM(beta.shape, F32),
+                    pltpu.VMEM(decay.shape, F32),
+                    pltpu.VMEM(keys.shape, BF16),
+                    pltpu.VMEM(values.shape, BF16),
+                    pltpu.VMEM((2, tokens * heads, width), F32),
+                    pltpu.VMEM((2, tokens * heads, width), F32),
+                    pltpu.SemaphoreType.DMA((4,)),
+                ],
+                limit=FIRST_LIMIT,
+            )
+        else:
+            *given, sol = local_call(
+                functools.partial(later_kernel, exchange, part),
+                outs,
+                [VMEM] * 3,
+                (k_heads, v_heads, row_terms),
+            )
+        terms.update(zip(part, given))
+        solved.append(sol)
+        if exchange:
+            for s in part:
+                arrived[s] = lax.ppermute(terms[s], "seq", swaps[s]) if s else terms[s]
     mixed = local_call(
-        functools.partial(mixing_kernel, exchange),
+        functools.partial(mixing_kernel, exchange, orders),
         jax.ShapeDtypeStruct((heads, tokens, 2 * width), F32),
-        [VMEM] * 4,
-        (decay, queries, keys, solved),
-        [
-            pltpu.VMEM((tokens * heads, width), F32),
-            pltpu.VMEM((2, tokens * heads, width), F32),
-            pltpu.VMEM((heads, tokens), F32),
-        ],
-        flops=5_000_000_000,
-    )
+        [VMEM] * (3 + len(orders)),
+        (queries, k_heads, row_terms, *solved),
+        [pltpu.VMEM((tokens * heads, width), F32)],
+        flops=3_000_000_000,
+    )
+    state = jax.ShapeDtypeStruct((PER_SLOT, width, width), BF16)
     if exchange:
-        shifts = [[(k, (k + s) % seq_count) for k in range(seq_count)] for s in range(seq_count)]
-        arrived = [terms[0]] + [
-            lax.ppermute(terms[s], "seq", shifts[s]) for s in range(1, seq_count)
-        ]
-        state = jax.ShapeDtypeStruct((width, width), BF16)
+        inner = jax.ShapeDtypeStruct((slots - 1, PER_SLOT, width, width), F32)
+        local, prefix, end = local_call(
+            functools.partial(chain_kernel, slots),
+            [inner, inner, state],
+            [VMEM] * slots,
+            [arrived[s] for s in range(slots)],
+            [pltpu.VMEM((slots, PER_SLOT, width, 2 * width), BF16)],
+        )
+        before = lax.ppermute(end, "seq", [(k, k + slots) for k in range(slots)])
         outgoing = local_call(
-            functools.partial(chain_kernel, seq_count),
-            [state] * seq_count,
-            [VMEM] * seq_count,
-            arrived,
-            [
-                pltpu.VMEM((seq_count, width, 2 * width), BF16),
-                pltpu.VMEM((seq_count, width, width), BF16),
-            ],
+            functools.partial(entry_kernel, slots),
+            [state] * slots,
+            [VMEM] * 3,
+            (local, prefix, before),
+            [pltpu.VMEM((slots, PER_SLOT, width, width), BF16)],
         )
-        states = [outgoing[0]] + [
-            lax.ppermute(outgoing[s], "seq", shifts[s]) for s in range(1, seq_count)
-        ]
+        states = {0: outgoing[0]}
+        for s in order[:-1]:
+            states[s] = lax.ppermute(outgoing[s], "seq", swaps[s])
     else:
         states = prefix_states(terms)
     hidden = local_call(
-        functools.partial(emit_kernel, exchange),
+        functools.partial(emit_kernel, exchange, order),
         jax.ShapeDtypeStruct((heads, tokens, width), BF16),
-        [VMEM] * (3 + heads),
-        (mixed, out_gain.reshape(1, width), residual, *states),
-        [pltpu.VMEM((heads, width, width), BF16)],
+        [VMEM] * (3 + slots),
+        (mixed, out_gain.reshape(1, width), residual, *(states[s] for s in range(slots))),
     )
 
     flips = {
@@ -454,7 +519,7 @@
     sums = local_call(
         functools.partial(ffn_kernel, tensor_count),
         [jax.ShapeDtypeStruct((heads, tokens, side), BF16)] * tensor_count,
-        [VMEM, SMEM, SMEM, ANY, ANY] + [VMEM] * tensor_count,
+        [VMEM, SMEM, SMEM, VMEM, VMEM] + [VMEM] * tensor_count,
         (
             ffn_gain.reshape(tiles, side), up_index, down_index, up_blocks, down_kept_tiles,
             *(parts[m] for m in range(tensor_count)),
@@ -463,10 +528,6 @@
             pltpu.VMEM((tiles, tokens, side), BF16),
             pltpu.VMEM((groups, tokens, side), BF16),
             pltpu.VMEM((tiles, tokens, side), F32),
-            pltpu.VMEM((groups, kept, side, side), BF16),
-            pltpu.VMEM((groups, kept, side, side), BF16),
-            pltpu.SemaphoreType.DMA((groups,)),
-            pltpu.SemaphoreType.DMA((groups,)),
         ],
     )
     held = {m: [part] for m, part in enumerate(sums)}

time: 77.5 us -> 63.9 us (0.82)
  starting transfers between devices: 29 us -> 16.6 us
  Pallas kernels: 26.1 us -> 22.2 us
  waiting for transfers between devices: 18.4 us -> 20 us
  local copies, waits for them, and re-layouts: 3.5 us -> 4.46 us
    ppermute x14 -> x7, starting transfers between devices: 25 us -> 12.9 us  [the longest x1 4.68 us: per_device(): before = lax.ppermute(end, 'seq', [(k, k + slots) for k in range(slots)])]
    pallas_call x6 -> x9, Pallas kernels: 26.1 us -> 22.2 us  [local_call(): pl.pallas_call(kernel, out_shape=out_shape, in_specs=ins, out_specs=jax.t...]
    ppermute x14 -> x7, waiting for transfers between devices: 4.45 us -> 5.8 us  [the longest x3 2.84 us: per_device(): arrived[s] = lax.ppermute(terms[s], 'seq', swaps[s]) if s else terms[s]]
    unnamed x24 -> x26, local copies, waits for them, and re-layouts: 3.5 us -> 4.46 us
  transfers between devices with their start and end apart: 20 -> 13, of which waited for: 11 -> 7; matrix products, arithmetic and copies ran while one was open for 0% -> 0% of each run, Pallas kernels for 3% -> 8%
where the time goes in v2:
time: 63.9 us; the launch traced here: 63.6 us
  Pallas kernels  22.2 us (35%)
  waiting for transfers between devices  20 us (31%)
  starting transfers between devices  16.6 us (26%)
  local copies, waits for them, and re-layouts  4.46 us (7%)
    pallas_call x9, Pallas kernels, local_call(): pl.pallas_call(kernel, out_shape=out_shape, in_specs=ins, out_specs=jax.t...  22.2 us
    ppermute x3, waiting for transfers between devices, per_device(): moved = lax.ppermute(added(held.pop(m | d)), 'tensor', flips[d])  7.85 us
    ppermute x3, waiting for transfers between devices, per_device(): parts[m | d] = lax.ppermute(parts[m], 'tensor', flips[d])  6.38 us
    ppermute x1, starting transfers between devices, per_device(): before = lax.ppermute(end, 'seq', [(k, k + slots) for k in range(slots)])  4.68 us
    ppermute x3, starting transfers between devices, per_device(): arrived[s] = lax.ppermute(terms[s], 'seq', swaps[s]) if s else terms[s]  4.63 us
    unnamed x26, local copies, waits for them, and re-layouts  4.46 us
    ppermute x3, starting transfers between devices, per_device(): states[s] = lax.ppermute(outgoing[s], 'seq', swaps[s])  3.55 us
    ppermute x3, waiting for transfers between devices, per_device(): arrived[s] = lax.ppermute(terms[s], 'seq', swaps[s]) if s else terms[s]  2.84 us
  transfers between devices with their start and end apart: 13, of which 7 were waited for; matrix products, arithmetic and copies ran while one was open for 0% of the time, Pallas kernels for 8%

profile of v2, /device:TPU:0, one launch (start us, length us, event | category | flops | bytes accessed | tf_op | source)
XLA Modules:
  0.0 63.6 jit_solution(12928356622412797223)
XLA Ops:
  0.0 1.0 %copy-done.1 = bf16[2,128,8,128]{3,2,1,0:T(8,128)(2,1)S(1)} copy-done((bf16[2,128,8,128]{3,2,1,0:T(8,128)(2,1)S(1)}, bf16[2,128,8,128]{3,2,1,0:T(8,128)(2,1)}, u32[]{:S(2)}) %copy-start.1) | copy-done | bytes 524312
  1.0 1.0 %copy-done.2 = bf16[2,128,8,128]{3,2,1,0:T(8,128)(2,1)S(1)} copy-done((bf16[2,128,8,128]{3,2,1,0:T(8,128)(2,1)S(1)}, bf16[2,128,8,128]{3,2,1,0:T(8,128)(2,1)}, u32[]{:S(2)}) %copy-start.2) | copy-done | bytes 524312
  2.1 0.7 %copy-done.5 = f32[2,8,128]{2,1,0:T(8,128)S(1)} copy-done((f32[2,8,128]{2,1,0:T(8,128)S(1)}, f32[2,8,128]{2,1,0:T(8,128)}, u32[]{:S(2)}) %copy-start.5) | copy-done | bytes 8216
  2.8 0.7 %copy-done.8 = f32[8,128]{1,0:T(8,128)S(1)} copy-done((f32[8,128]{1,0:T(8,128)S(1)}, f32[8,128]{1,0:T(8,128)}, u32[]{:S(2)}) %copy-start.8) | copy-done | bytes 4120
  3.5 5.3 %shard_map.118 = (bf16[2,128,256]{2,1,0:T(8,128)(2,1)S(1)}, bf16[2,128,256]{2,1,0:T(8,128)(2,1)S(1)}, f32[4,256,256]{2,1,0:T(8,128)S(1)}, bf16[8,2,128,128]{3,2,...) custom-call(f32[2,8,128]{2,1,0:T(8,128)S(1)} %copy-done.5, f32[8,128]{1,0:T(8,128)S(1)} %copy-done.8, ...), custom_call_target="tpu_custom_call" | custom-call | tf_op jit(solution)/shard_map/pallas_call | solution.py:389
  8.8 0.0 slice-start
  8.8 0.0 copy-start.4
  8.8 0.0 copy-start.6
  8.8 0.0 copy-start.7
  8.8 3.4 %shard_map.119 = (bf16[2,128,256]{2,1,0:T(8,128)(2,1)S(1)}, f32[2,256,256]{2,1,0:T(8,128)S(1)}) custom-call(bf16[8,2,128,128]{3,2,1,0:T(8,128)(2,1)S(1)} %get-tuple-element.26.k_heads, bf16[8,2,128,128]{3,2,1,0:T(8,128)(2,1)S(1)} %get-tuple-element.29.v_heads, f32[6,8,128]{2,1,0:T(8,128)S(1)} %get-tuple-element.27.row_ref), custom_call_target="tpu_custom_call" | custom-call | tf_op jit(solution)/shard_map/pallas_call | solution.py:389
  12.2 3.1 %collective-permute-start.1 = (bf16[2,128,256]{2,1,0:T(8,128)(2,1)S(1)}, bf16[2,128,256]{2,1,0:T(8,128)(2,1)S(1)}, u32[]{:S(2)}, u32[]{:S(2)}) collective-permute-start(bf16[2,128,256]{2,1,0:T(8,128)(2,1)S(1)} %get-tuple-element.34), channel_id=1, source_target_pairs={{0,8},{4,12},{8,0},{12,4},{16,24},{20,28},{24,16},{28,20},{1,9},{5... | collective-permute-start | bytes 393224 | tf_op jit(solution)/shard_map/ppermute | solution.py:470
  15.3 1.5 %collective-permute-start = (bf16[2,128,256]{2,1,0:T(8,128)(2,1)S(1)}, bf16[2,128,256]{2,1,0:T(8,128)(2,1)S(1)}, u32[]{:S(2)}, u32[]{:S(2)}) collective-permute-start(bf16[2,128,256]{2,1,0:T(8,128)(2,1)S(1)} %get-tuple-element.33), channel_id=1, source_target_pairs={{0,4},{4,0},{8,12},{12,8},{16,20},{20,16},{24,28},{28,24},{1,5},{5... | collective-permute-start | bytes 393224 | tf_op jit(solution)/shard_map/ppermute | solution.py:470
  16.8 0.1 collective-permute-start.2
  16.9 3.4 %shard_map.120 = (bf16[2,128,256]{2,1,0:T(8,128)(2,1)S(1)}, f32[2,256,256]{2,1,0:T(8,128)S(1)}) custom-call(bf16[8,2,128,128]{3,2,1,0:T(8,128)(2,1)S(1)} %get-tuple-element.26.k_heads, bf16[8,2,128,128]{3,2,1,0:T(8,128)(2,1)S(1)} %get-tuple-element.29.v_heads, f32[6,8,128]{2,1,0:T(8,128)S(1)} %get-tuple-element.27.row_ref), custom_call_target="tpu_custom_call" | custom-call | tf_op jit(solution)/shard_map/pallas_call | solution.py:389
  20.2 0.0 collective-permute-done.1.refs_2_
  20.3 2.8 %collective-permute-done.refs_1_ = bf16[2,128,256]{2,1,0:T(8,128)(2,1)S(1)} collective-permute-done((bf16[2,128,256]{2,1,0:T(8,128)(2,1)S(1)}, bf16[2,128,256]{2,1,0:T(8,128)(2,1)S(1)}, u32[]{:S(2)}, u32[]{:S(2)}) %collective-permute-start) | collective-permute-done | bytes 131104 | tf_op jit(solution)/shard_map/ppermute | solution.py:470
  23.1 0.0 collective-permute-done.2.refs_3_
  23.1 0.8 %shard_map.122 = (f32[3,2,128,128]{3,2,1,0:T(8,128)S(1)}, f32[3,2,128,128]{3,2,1,0:T(8,128)S(1)}, bf16[2,128,128]{2,1,0:T(8,128)(2,1)S(1)}) custom-call(bf16[2,128,256]{2,1,0:T(8,128)(2,1)S(1)} %get-tuple-element.32.refs_0_, bf16[2,128,256]{2,1,0:T(8,128)(2,1)S(1)} %collective-permute-done.refs_1_, bf16[2,128,256]{2,1,0:T(8,128)(2,1)S(1)} %collective-permute-done.1.refs_2_, ...), custom_call_target="tpu_custom_call" | custom-call | tf_op jit(solution)/shard_map/pallas_call | solution.py:389
  23.8 4.7 %collective-permute-start.3 = (bf16[2,128,128]{2,1,0:T(8,128)(2,1)S(1)}, bf16[2,128,128]{2,1,0:T(8,128)(2,1)S(1)}, u32[]{:S(2)}, u32[]{:S(2)}) collective-permute-start(bf16[2,128,128]{2,1,0:T(8,128)(2,1)S(1)} %get-tuple-element.38), channel_id=1, source_target_pairs={{0,16},{4,20},{8,24},{12,28},{1,17},{5,21},{9,25},{13,29},{2,18},{... | collective-permute-start | bytes 196616 | tf_op jit(solution)/shard_map/ppermute | solution.py:489
  28.5 1.7 %collective-permute-done.3.before_ref = bf16[2,128,128]{2,1,0:T(8,128)(2,1)S(1)} collective-permute-done((bf16[2,128,128]{2,1,0:T(8,128)(2,1)S(1)}, bf16[2,128,128]{2,1,0:T(8,128)(2,1)S(1)}, u32[]{:S(2)}, u32[]{:S(2)}) %collective-permute-start.3) | collective-permute-done | bytes 65568 | tf_op jit(solution)/shard_map/ppermute | solution.py:489
  30.2 0.3 shard_map.123
  30.5 1.5 %collective-permute-start.4 = (bf16[2,128,128]{2,1,0:T(8,128)(2,1)S(1)}, bf16[2,128,128]{2,1,0:T(8,128)(2,1)S(1)}, u32[]{:S(2)}, u32[]{:S(2)}) collective-permute-start(bf16[2,128,128]{2,1,0:T(8,128)(2,1)S(1)} %get-tuple-element.40), channel_id=1, source_target_pairs={{0,4},{4,0},{8,12},{12,8},{16,20},{20,16},{24,28},{28,24},{1,5},{5... | collective-permute-start | bytes 196616 | tf_op jit(solution)/shard_map/ppermute | solution.py:499
  32.1 0.5 collective-permute-start.5
  32.6 1.5 %collective-permute-start.6 = (bf16[2,128,128]{2,1,0:T(8,128)(2,1)S(1)}, bf16[2,128,128]{2,1,0:T(8,128)(2,1)S(1)}, u32[]{:S(2)}, u32[]{:S(2)}) collective-permute-start(bf16[2,128,128]{2,1,0:T(8,128)(2,1)S(1)} %get-tuple-element.42), channel_id=1, source_target_pairs={{0,12},{4,8},{8,4},{12,0},{16,28},{20,24},{24,20},{28,16},{1,13},{... | collective-permute-start | bytes 196616 | tf_op jit(solution)/shard_map/ppermute | solution.py:499
  34.1 0.9 %copy-done.10 = bf16[128,8,128]{2,1,0:T(8,128)(2,1)S(1)} copy-done((bf16[128,8,128]{2,1,0:T(8,128)(2,1)S(1)}, bf16[128,8,128]{2,1,0:T(8,128)(2,1)}, u32[]{:S(2)}) %copy-start.10) | copy-done | bytes 262168
  35.0 1.4 %shard_map.121.mixed_ref = f32[8,128,256]{2,1,0:T(8,128)S(1)} custom-call(bf16[128,8,128]{2,1,0:T(8,128)(2,1)S(1)} %copy-done.10, bf16[8,2,128,128]{3,2,1,0:T(8,128)(2,1)S(1)} %get-tuple-element.26.k_heads, f32[6,8,128]{2,1,0:T(8,128)S(1)} %get-tuple-element.27.row_ref, f32[4,256,256]{2,1,0:T(8,128)S(1)} %get-tuple-element.28.refs_0_, ...), custom_call_target="tpu_custom_call" | custom-call | flops 3000000000 | tf_op jit(solution)/shard_map/pallas_call | solution.py:389
  36.5 0.0 collective-permute-done.4.refs_1_
  36.5 0.0 collective-permute-done.5.refs_2_
  36.5 1.2 %collective-permute-done.6.refs_3_ = bf16[2,128,128]{2,1,0:T(8,128)(2,1)S(1)} collective-permute-done((bf16[2,128,128]{2,1,0:T(8,128)(2,1)S(1)}, bf16[2,128,128]{2,1,0:T(8,128)(2,1)S(1)}, u32[]{:S(2)}, u32[]{:S(2)}) %collective-permute-start.6) | collective-permute-done | bytes 65568 | tf_op jit(solution)/shard_map/ppermute | solution.py:499
  37.7 0.0 copy-done.3
  37.7 0.0 copy-done.9
  37.7 0.4 shard_map.124.refs_0_.hidden_ref
  38.1 1.6 %collective-permute-start.8 = (bf16[8,128,128]{2,1,0:T(8,128)(2,1)S(1)}, bf16[8,128,128]{2,1,0:T(8,128)(2,1)S(1)}, u32[]{:S(2)}, u32[]{:S(2)}) collective-permute-start(bf16[8,128,128]{2,1,0:T(8,128)(2,1)S(1)} %shard_map.124.refs_0_.hidden_ref), channel_id=1, source_target_pairs={{0,2},{1,3},{2,0},{3,1},{4,6},{5,7},{6,4},{7,5},{8,10},{9,11},{10,... | collective-permute-start | bytes 786440 | tf_op jit(solution)/shard_map/ppermute | solution.py:516
  39.7 0.0 collective-permute-start.7
  39.7 4.8 %collective-permute-done.8.refs_2_ = bf16[8,128,128]{2,1,0:T(8,128)(2,1)S(1)} collective-permute-done((bf16[8,128,128]{2,1,0:T(8,128)(2,1)S(1)}, bf16[8,128,128]{2,1,0:T(8,128)(2,1)S(1)}, u32[]{:S(2)}, u32[]{:S(2)}) %collective-permute-start.8) | collective-permute-done | bytes 262176 | tf_op jit(solution)/shard_map/ppermute | solution.py:516
  44.6 0.0 collective-permute-start.9
  44.6 0.0 collective-permute-done.7.refs_1_
  44.6 1.5 %collective-permute-done.9.refs_3_ = bf16[8,128,128]{2,1,0:T(8,128)(2,1)S(1)} collective-permute-done((bf16[8,128,128]{2,1,0:T(8,128)(2,1)S(1)}, bf16[8,128,128]{2,1,0:T(8,128)(2,1)S(1)}, u32[]{:S(2)}, u32[]{:S(2)}) %collective-permute-start.9) | collective-permute-done | bytes 262176 | tf_op jit(solution)/shard_map/ppermute | solution.py:516
  46.1 0.0 copy-done
  46.2 6.5 %shard_map.125 = (bf16[8,128,128]{2,1,0:T(8,128)(2,1)S(1)}, bf16[8,128,128]{2,1,0:T(8,128)(2,1)S(1)}, bf16[8,128,128]{2,1,0:T(8,128)(2,1)S(1)}, bf16[8,128,128]{2,1,0:T(8,128)(2,1)S(1)}) custom-call(f32[32,128]{1,0:T(8,128)S(1)} %bitcast.4, s32[16,16]{1,0:T(8,128)S(1)} %copy-done.6, s32[16,16]{1,0:T(8,128)S(1)} %copy-done.7, ...), custom_call_target="tpu_custom_call" | custom-call | tf_op jit(solution)/shard_map/pallas_call | solution.py:389
  52.7 0.2 collective-permute-start.11
  52.8 0.4 collective-permute-start.10
  53.2 1.0 %collective-permute-done.11 = bf16[8,128,128]{2,1,0:T(8,128)(2,1)S(1)} collective-permute-done((bf16[8,128,128]{2,1,0:T(8,128)(2,1)S(1)}, bf16[8,128,128]{2,1,0:T(8,128)(2,1)S(1)}, u32[]{:S(2)}, u32[]{:S(2)}) %collective-permute-start.11) | collective-permute-done | bytes 262176 | tf_op jit(solution)/shard_map/ppermute | solution.py:536
  54.3 0.1 add_convert_fusion
  54.3 1.6 %collective-permute-start.12 = (bf16[8,128,128]{2,1,0:T(8,128)(2,1)S(1)}, bf16[8,128,128]{2,1,0:T(8,128)(2,1)S(1)}, u32[]{:S(2)}, u32[]{:S(2)}) collective-permute-start(bf16[8,128,128]{2,1,0:T(8,128)(2,1)S(1)} %add_convert_fusion), channel_id=1, source_target_pairs={{0,2},{1,3},{2,0},{3,1},{4,6},{5,7},{6,4},{7,5},{8,10},{9,11},{10,... | collective-permute-start | bytes 786440 | tf_op jit(solution)/shard_map/ppermute | solution.py:536
  55.9 0.0 collective-permute-done.10.refs_1_
  55.9 6.8 %collective-permute-done.12.refs_2_ = bf16[8,128,128]{2,1,0:T(8,128)(2,1)S(1)} collective-permute-done((bf16[8,128,128]{2,1,0:T(8,128)(2,1)S(1)}, bf16[8,128,128]{2,1,0:T(8,128)(2,1)S(1)}, u32[]{:S(2)}, u32[]{:S(2)}) %collective-permute-start.12) | collective-permute-done | bytes 262176 | tf_op jit(solution)/shard_map/ppermute | solution.py:536
  62.7 0.8 %shard_map.126 = bf16[128,1024]{1,0:T(8,128)(2,1)} custom-call(bf16[8,128,128]{2,1,0:T(8,128)(2,1)S(1)} %shard_map.124.refs_0_.hidden_ref, bf16[8,128,128]{2,1,0:T(8,128)(2,1)S(1)} %get-tuple-element.43.refs_0_, bf16[8,128,128]{2,1,0:T(8,128)(2,1)S(1)} %collective-permute-done.10.refs_1_, bf16[8,128,128]{2,1,0:T(8,128)(2,1)S(1)} %collective-permute-done.12.refs_2_), custom_call_target="tpu_custom_call" | custom-call | tf_op jit(solution)/shard_map/pallas_call | solution.py:389
  (15 shorter events, 0.0 us)
Async XLA Ops:
  0.0 1.0 %copy-start.1 = (bf16[2,128,8,128]{3,2,1,0:T(8,128)(2,1)S(1)}, bf16[2,128,8,128]{3,2,1,0:T(8,128)(2,1)}, u32[]{:S(2)}) copy-start(bf16[2,128,8,128]{3,2,1,0:T(8,128)(2,1)} %k_hbm.1) | copy-start | bytes 1572868
  1.0 1.0 %copy-start.2 = (bf16[2,128,8,128]{3,2,1,0:T(8,128)(2,1)S(1)}, bf16[2,128,8,128]{3,2,1,0:T(8,128)(2,1)}, u32[]{:S(2)}) copy-start(bf16[2,128,8,128]{3,2,1,0:T(8,128)(2,1)} %v_hbm.1) | copy-start | bytes 1572868
  2.1 0.7 %copy-start.5 = (f32[2,8,128]{2,1,0:T(8,128)S(1)}, f32[2,8,128]{2,1,0:T(8,128)}, u32[]{:S(2)}) copy-start(f32[2,8,128]{2,1,0:T(8,128)} %beta_hbm.1) | copy-start | bytes 24580
  2.8 0.7 %copy-start.8 = (f32[8,128]{1,0:T(8,128)S(1)}, f32[8,128]{1,0:T(8,128)}, u32[]{:S(2)}) copy-start(f32[8,128]{1,0:T(8,128)} %decay_hbm.1) | copy-start | bytes 12292
  3.5 34.3 %copy-start.3 = (bf16[128,1024]{1,0:T(8,128)(2,1)S(1)}, bf16[128,1024]{1,0:T(8,128)(2,1)}, u32[]{:S(2)}) copy-start(bf16[128,1024]{1,0:T(8,128)(2,1)} %residual_ref.1) | copy-start | bytes 786436
  3.5 34.3 %copy-start.9 = (f32[128]{0:T(128)S(1)}, f32[128]{0:T(128)}, u32[]{:S(2)}) copy-start(f32[128]{0:T(128)} %param.17) | copy-start | bytes 1540
  3.5 42.6 %copy-start = (bf16[16,16,128,128]{3,2,1,0:T(8,128)(2,1)S(1)}, bf16[16,16,128,128]{3,2,1,0:T(8,128)(2,1)}, u32[]{:S(2)}) copy-start(bf16[16,16,128,128]{3,2,1,0:T(8,128)(2,1)} %down_ref.1) | copy-start | bytes 25165828
  8.8 37.4 %slice-start = ((s8[8388608]{0:T(1024)(128)(4,1)}), s8[4194304]{0:T(1024)(128)(4,1)S(1)}, s32[]{:S(2)}) async-start(s8[8388608]{0:T(1024)(128)(4,1)} %bitcast.2), calls=%async_computation | async-start | bytes 8388608
  8.8 37.3 %copy-start.4 = (f32[4096]{0:T(1024)S(1)}, f32[4096]{0:T(1024)}, u32[]{:S(2)}) copy-start(f32[4096]{0:T(1024)} %param.19) | copy-start | bytes 49156
  8.8 37.3 %copy-start.6 = (s32[16,16]{1,0:T(8,128)S(1)}, s32[16,16]{1,0:T(8,128)}, u32[]{:S(2)}) copy-start(s32[16,16]{1,0:T(8,128)} %up_at.1) | copy-start | bytes 3076
  8.8 37.3 %copy-start.7 = (s32[16,16]{1,0:T(8,128)S(1)}, s32[16,16]{1,0:T(8,128)}, u32[]{:S(2)}) copy-start(s32[16,16]{1,0:T(8,128)} %down_at.1) | copy-start | bytes 3076
  12.2 8.0 %collective-permute-start.1 = (bf16[2,128,256]{2,1,0:T(8,128)(2,1)S(1)}, bf16[2,128,256]{2,1,0:T(8,128)(2,1)S(1)}, u32[]{:S(2)}, u32[]{:S(2)}) collective-permute-start(bf16[2,128,256]{2,1,0:T(8,128)(2,1)S(1)} %get-tuple-element.34), channel_id=1, source_target_pairs={{0,8},{4,12},{8,0},{12,4},{16,24},{20,28},{24,16},{28,20},{1,9},{5... | collective-permute-start | bytes 393224 | tf_op jit(solution)/shard_map/ppermute | solution.py:470
  15.3 7.8 %collective-permute-start = (bf16[2,128,256]{2,1,0:T(8,128)(2,1)S(1)}, bf16[2,128,256]{2,1,0:T(8,128)(2,1)S(1)}, u32[]{:S(2)}, u32[]{:S(2)}) collective-permute-start(bf16[2,128,256]{2,1,0:T(8,128)(2,1)S(1)} %get-tuple-element.33), channel_id=1, source_target_pairs={{0,4},{4,0},{8,12},{12,8},{16,20},{20,16},{24,28},{28,24},{1,5},{5... | collective-permute-start | bytes 393224 | tf_op jit(solution)/shard_map/ppermute | solution.py:470
  16.8 6.3 %collective-permute-start.2 = (bf16[2,128,256]{2,1,0:T(8,128)(2,1)S(1)}, bf16[2,128,256]{2,1,0:T(8,128)(2,1)S(1)}, u32[]{:S(2)}, u32[]{:S(2)}) collective-permute-start(bf16[2,128,256]{2,1,0:T(8,128)(2,1)S(1)} %get-tuple-element.35), channel_id=1, source_target_pairs={{0,12},{4,8},{8,4},{12,0},{16,28},{20,24},{24,20},{28,16},{1,13},{... | collective-permute-start | bytes 393224 | tf_op jit(solution)/shard_map/ppermute | solution.py:470
  23.8 6.4 %collective-permute-start.3 = (bf16[2,128,128]{2,1,0:T(8,128)(2,1)S(1)}, bf16[2,128,128]{2,1,0:T(8,128)(2,1)S(1)}, u32[]{:S(2)}, u32[]{:S(2)}) collective-permute-start(bf16[2,128,128]{2,1,0:T(8,128)(2,1)S(1)} %get-tuple-element.38), channel_id=1, source_target_pairs={{0,16},{4,20},{8,24},{12,28},{1,17},{5,21},{9,25},{13,29},{2,18},{... | collective-permute-start | bytes 196616 | tf_op jit(solution)/shard_map/ppermute | solution.py:489
  30.5 5.9 %collective-permute-start.4 = (bf16[2,128,128]{2,1,0:T(8,128)(2,1)S(1)}, bf16[2,128,128]{2,1,0:T(8,128)(2,1)S(1)}, u32[]{:S(2)}, u32[]{:S(2)}) collective-permute-start(bf16[2,128,128]{2,1,0:T(8,128)(2,1)S(1)} %get-tuple-element.40), channel_id=1, source_target_pairs={{0,4},{4,0},{8,12},{12,8},{16,20},{20,16},{24,28},{28,24},{1,5},{5... | collective-permute-start | bytes 196616 | tf_op jit(solution)/shard_map/ppermute | solution.py:499
  32.1 4.4 %collective-permute-start.5 = (bf16[2,128,128]{2,1,0:T(8,128)(2,1)S(1)}, bf16[2,128,128]{2,1,0:T(8,128)(2,1)S(1)}, u32[]{:S(2)}, u32[]{:S(2)}) collective-permute-start(bf16[2,128,128]{2,1,0:T(8,128)(2,1)S(1)} %get-tuple-element.41), channel_id=1, source_target_pairs={{0,8},{4,12},{8,0},{12,4},{16,24},{20,28},{24,16},{28,20},{1,9},{5... | collective-permute-start | bytes 196616 | tf_op jit(solution)/shard_map/ppermute | solution.py:499
  32.6 5.2 %collective-permute-start.6 = (bf16[2,128,128]{2,1,0:T(8,128)(2,1)S(1)}, bf16[2,128,128]{2,1,0:T(8,128)(2,1)S(1)}, u32[]{:S(2)}, u32[]{:S(2)}) collective-permute-start(bf16[2,128,128]{2,1,0:T(8,128)(2,1)S(1)} %get-tuple-element.42), channel_id=1, source_target_pairs={{0,12},{4,8},{8,4},{12,0},{16,28},{20,24},{24,20},{28,16},{1,13},{... | collective-permute-start | bytes 196616 | tf_op jit(solution)/shard_map/ppermute | solution.py:499
  34.1 0.9 %copy-start.10 = (bf16[128,8,128]{2,1,0:T(8,128)(2,1)S(1)}, bf16[128,8,128]{2,1,0:T(8,128)(2,1)}, u32[]{:S(2)}) copy-start(bf16[128,8,128]{2,1,0:T(8,128)(2,1)} %q_ref.1) | copy-start | bytes 786436
  35.0 11.1 %slice-start.1 = ((s8[8388608]{0:T(1024)(128)(4,1)}), s8[4194304]{0:T(1024)(128)(4,1)S(1)}, s32[]{:S(2)}) async-start(s8[8388608]{0:T(1024)(128)(4,1)} %bitcast.2), calls=%async_computation.1 | async-start | bytes 8388608
  38.1 6.4 %collective-permute-start.8 = (bf16[8,128,128]{2,1,0:T(8,128)(2,1)S(1)}, bf16[8,128,128]{2,1,0:T(8,128)(2,1)S(1)}, u32[]{:S(2)}, u32[]{:S(2)}) collective-permute-start(bf16[8,128,128]{2,1,0:T(8,128)(2,1)S(1)} %shard_map.124.refs_0_.hidden_ref), channel_id=1, source_target_pairs={{0,2},{1,3},{2,0},{3,1},{4,6},{5,7},{6,4},{7,5},{8,10},{9,11},{10,... | collective-permute-start | bytes 786440 | tf_op jit(solution)/shard_map/ppermute | solution.py:516
  39.7 4.9 %collective-permute-start.7 = (bf16[8,128,128]{2,1,0:T(8,128)(2,1)S(1)}, bf16[8,128,128]{2,1,0:T(8,128)(2,1)S(1)}, u32[]{:S(2)}, u32[]{:S(2)}) collective-permute-start(bf16[8,128,128]{2,1,0:T(8,128)(2,1)S(1)} %shard_map.124.refs_0_.hidden_ref), channel_id=1, source_target_pairs={{0,1},{1,0},{2,3},{3,2},{4,5},{5,4},{6,7},{7,6},{8,9},{9,8},{10,11... | collective-permute-start | bytes 786440 | tf_op jit(solution)/shard_map/ppermute | solution.py:516
  44.6 1.5 %collective-permute-start.9 = (bf16[8,128,128]{2,1,0:T(8,128)(2,1)S(1)}, bf16[8,128,128]{2,1,0:T(8,128)(2,1)S(1)}, u32[]{:S(2)}, u32[]{:S(2)}) collective-permute-start(bf16[8,128,128]{2,1,0:T(8,128)(2,1)S(1)} %collective-permute-done.8.refs_2_), channel_id=1, source_target_pairs={{0,1},{1,0},{2,3},{3,2},{4,5},{5,4},{6,7},{7,6},{8,9},{9,8},{10,11... | collective-permute-start | bytes 786440 | tf_op jit(solution)/shard_map/ppermute | solution.py:516
  52.7 1.6 %collective-permute-start.11 = (bf16[8,128,128]{2,1,0:T(8,128)(2,1)S(1)}, bf16[8,128,128]{2,1,0:T(8,128)(2,1)S(1)}, u32[]{:S(2)}, u32[]{:S(2)}) collective-permute-start(bf16[8,128,128]{2,1,0:T(8,128)(2,1)S(1)} %get-tuple-element.46), channel_id=1, source_target_pairs={{0,1},{1,0},{2,3},{3,2},{4,5},{5,4},{6,7},{7,6},{8,9},{9,8},{10,11... | collective-permute-start | bytes 786440 | tf_op jit(solution)/shard_map/ppermute | solution.py:536
  52.8 3.1 %collective-permute-start.10 = (bf16[8,128,128]{2,1,0:T(8,128)(2,1)S(1)}, bf16[8,128,128]{2,1,0:T(8,128)(2,1)S(1)}, u32[]{:S(2)}, u32[]{:S(2)}) collective-permute-start(bf16[8,128,128]{2,1,0:T(8,128)(2,1)S(1)} %get-tuple-element.44), channel_id=1, source_target_pairs={{0,1},{1,0},{2,3},{3,2},{4,5},{5,4},{6,7},{7,6},{8,9},{9,8},{10,11... | collective-permute-start | bytes 786440 | tf_op jit(solution)/shard_map/ppermute | solution.py:536
  54.3 8.4 %collective-permute-start.12 = (bf16[8,128,128]{2,1,0:T(8,128)(2,1)S(1)}, bf16[8,128,128]{2,1,0:T(8,128)(2,1)S(1)}, u32[]{:S(2)}, u32[]{:S(2)}) collective-permute-start(bf16[8,128,128]{2,1,0:T(8,128)(2,1)S(1)} %add_convert_fusion), channel_id=1, source_target_pairs={{0,2},{1,3},{2,0},{3,1},{4,6},{5,7},{6,4},{7,5},{8,10},{9,11},{10,... | collective-permute-start | bytes 786440 | tf_op jit(solution)/shard_map/ppermute | solution.py:536

commit v3 on v2

--- a/solution.py
+++ b/solution.py
@@ -9,10 +9,11 @@
 
 F32 = jnp.float32
 BF16 = jnp.bfloat16
-HEAD_GROUP = 4
+HEAD_GROUP = 6
 PER_SLOT = 2
-CUTS = (2, 3)
-FIRST_LIMIT = 20 * (1 << 20)
+CUTS = (1, 3)
+PIECES = [[0, 1, 2, 3]]
+FIRST_LIMIT = 52 * (1 << 20) + (1 << 19)
 MIB = 1 << 20
 VMEM = pl.BlockSpec(memory_space=pltpu.VMEM)
 SMEM = pl.BlockSpec(memory_space=pltpu.SMEM)
@@ -84,22 +85,29 @@
     return PER_SLOT * slot + u
 
 
-def first_kernel(exchange, order, beta_hbm, decay_hbm, k_hbm, v_hbm, *refs):
-    _, heads, tokens = beta_hbm.shape
-    width = k_hbm.shape[-1]
-    half = tokens // 2
-    out_refs, (sol_ref, k_heads, v_heads, row_ref) = refs[: len(order)], refs[len(order) :][:4]
-    beta_ref, decay_ref, k_ref, v_ref, k_all, v_all, sems = refs[len(order) + 4 :]
+def sort_kernel(k_hbm, v_hbm, k_heads, v_heads, k_ref, v_ref, wide, sems):
+    _, tokens, heads, width = k_hbm.shape
     copies = [
         pltpu.make_async_copy(source, target, sems.at[n])
-        for n, (source, target) in enumerate(
-            ((beta_hbm, beta_ref), (decay_hbm, decay_ref), (k_hbm, k_ref), (v_hbm, v_ref))
-        )
+        for n, (source, target) in enumerate(((k_hbm, k_ref), (v_hbm, v_ref)))
     ]
     for copy in copies:
         copy.start()
-    for copy in copies[:2]:
-        copy.wait()
+    for n, (source, target) in enumerate(((k_ref, k_heads), (v_ref, v_heads))):
+        copies[n].wait()
+        for j in range(2):
+            wide[n, j] = source[j].astype(F32).reshape(tokens * heads, width)
+        for h in range(heads):
+            rows = stacked(*(head_rows(wide.at[n, j], h, heads) for j in range(2)))
+            for i in range(2):
+                target[h, i] = rows[i].astype(BF16)
+
+
+def first_kernel(exchange, order, given_ref, k_heads, v_heads, *refs):
+    _, heads, tokens = given_ref.shape
+    beta_ref, decay_ref = given_ref.at[:2], given_ref.at[2]
+    half = tokens // 2
+    out_refs, (sol_ref, row_ref) = refs[: len(order)], refs[len(order) :]
     run = running_rows(decay_ref)
     run_half = doubled(run, half)
     beta_half = stacked_beta(beta_ref, half)
@@ -108,22 +116,11 @@
         row_ref[2 + i] = beta_half[i]
     row_ref[4] = jnp.broadcast_to(run[:, tokens - 1 :], (heads, 2 * half))
     row_ref[5] = run
-    for copy, source, wide, target in (
-        (copies[2], k_ref, k_all, k_heads),
-        (copies[3], v_ref, v_all, v_heads),
-    ):
-        copy.wait()
-        for j in range(2):
-            wide[j] = source[j].astype(F32).reshape(tokens * heads, width)
-        for h in range(heads):
-            rows = stacked(*(head_rows(wide.at[j], h, heads) for j in range(2)))
-            for i in range(2):
-                target[h, i] = rows[i].astype(BF16)
     solve_heads(exchange, order, k_heads, v_heads, row_ref, out_refs, sol_ref)
 
 
 def later_kernel(exchange, order, k_heads, v_heads, row_ref, *refs):
-    out_refs, sol_ref = refs[: len(order)], refs[len(order)]
+    *out_refs, sol_ref = refs[-1 - len(order) :]
     solve_heads(exchange, order, k_heads, v_heads, row_ref, out_refs, sol_ref)
 
 
@@ -146,7 +143,6 @@
         for s in places[start : start + HEAD_GROUP]:
             h = head_of(exchange, order[s[0]], s[1])
             keys = [k_heads[h, i] for i in range(2)]
-            values = [v_heads[h, i] for i in range(2)]
             run_row = [row_ref[i, pl.ds(h, 1), :] for i in range(2)]
             beta_row = [row_ref[2 + i, pl.ds(h, 1), :] for i in range(2)]
             run_col = [column(x) for x in run_row]
@@ -175,39 +171,50 @@
             cross = cross * beta_col[1] * jnp.exp(run_col[1] - run_row[0])
             chains.append(
                 dict(
-                    s=s, keys=keys, values=values, run_row=run_row, beta_row=beta_row,
+                    s=s, h=h, keys=keys, run_row=run_row, beta_row=beta_row,
                     run_col=run_col, last_row=last_row, inv_row=inv_row, inv_col=inv_col,
                     lowers=lowers, inverses=inverses, cross=cross,
                 )
             )
         size = 4
         while size < span:
+            top = min(4 * size, span)
             for c in chains:
                 c["parts"] = [split(x) for x in c["inverses"]]
-                c["middle"] = [
-                    dot_wide(
-                        split(jnp.where((apart >= size) & (apart < 2 * size), low, 0.0)), part
+                c["steps"] = [
+                    split(
+                        dot_wide(
+                            part, split(jnp.where((apart >= size) & (apart < top), low, 0.0))
+                        )
                     )
                     for low, part in zip(c["lowers"], c["parts"])
                 ]
             for c in chains:
                 c["inverses"] = [
-                    x - dot_wide(part, split(mid))
-                    for x, part, mid in zip(c["inverses"], c["parts"], c["middle"])
+                    x - dot_wide(step, part)
+                    for x, step, part in zip(c["inverses"], c["steps"], c["parts"])
                 ]
-            size *= 2
+            if top == 4 * size:
+                for c in chains:
+                    c["steps"] = [split(dot_wide(step, step)) for step in c["steps"]]
+                for c in chains:
+                    c["inverses"] = [
+                        x + dot_wide(step, split(x)) for x, step in zip(c["inverses"], c["steps"])
+                    ]
+            size = top
         for c in chains:
             c["parts"] = [split(x) for x in c["inverses"]]
             c["middle"] = dot_wide(split(c["cross"]), c["parts"][0])
         for c in chains:
             c["corner"] = -dot_wide(c["parts"][1], split(c["middle"]))
         for c in chains:
+            values = [v_heads[c["h"], i] for i in range(2)]
             scale_v = c["beta_row"]
             scale_k = [
                 b * jnp.exp(r) * n for b, r, n in zip(c["beta_row"], c["run_row"], c["inv_row"])
             ]
             solved = []
-            for scale, source in ((scale_k, c["keys"]), (scale_v, c["values"])):
+            for scale, source in ((scale_k, c["keys"]), (scale_v, values)):
                 first = split(c["inverses"][0] * scale[0])
                 upper = dot(jnp.concatenate(first, 1), jnp.concatenate([source[0]] * 2, 0))
                 corner = split(c["corner"] * scale[0])
@@ -247,12 +254,19 @@
     ]
 
 
-def mixing_kernel(exchange, orders, q_ref, k_heads, row_ref, *refs):
-    sol_refs, (out_ref, q_all) = refs[: len(orders)], refs[len(orders) :]
+def queries_kernel(q_ref, *refs):
+    out_ref, q_all = refs[-2:]
     tokens, heads, width = q_ref.shape
+    q_all[...] = q_ref[...].astype(F32).reshape(tokens * heads, width)
+    for h in range(heads):
+        out_ref[h] = head_rows(q_all, h, heads).astype(BF16)
+
+
+def mixing_kernel(exchange, orders, q_heads, k_heads, row_ref, *refs):
+    sol_refs, out_ref = refs[: len(orders)], refs[-1]
+    heads, tokens, width = q_heads.shape
     half = tokens // 2
     span = 2 * half
-    q_all[...] = q_ref[...].astype(F32).reshape(tokens * heads, width)
     token_at = lax.broadcasted_iota(jnp.int32, (tokens, 2 * span), 0)
     row_at = lax.broadcasted_iota(jnp.int32, (tokens, 2 * span), 1)
     seen = (row_at // span) * half + lax.rem(row_at, half) <= token_at
@@ -261,7 +275,7 @@
     eye = (row_at == col_at).astype(F32)
 
     def one_head(sol_ref, s, at, h):
-        queries = head_rows(q_all, h, heads)
+        queries = q_heads[h].astype(F32)
         keys = [k_heads[h, i] for i in range(2)]
         run_col = column(row_ref[5, pl.ds(h, 1), :])
         run_row = jnp.concatenate([row_ref[i, pl.ds(h, 1), :] for i in range(2)], 1)
@@ -287,13 +301,14 @@
                 at += 1
 
 
-def chain_kernel(group, *refs):
+def chain_kernel(order, *refs):
+    group = len(order)
     term_refs, (local_ref, prefix_ref, end_ref) = refs[:group], refs[group : group + 3]
     held = refs[group + 3]
     width = term_refs[0].shape[1]
     me = lax.rem(lax.axis_index("seq"), group)
-    for s in range(group):
-        held[s] = term_refs[s][...]
+    for n, s in enumerate(order):
+        held[s] = term_refs[n][...]
     for u in range(PER_SLOT):
         first = held[me, u]
         state = first[:, width:].astype(F32)
@@ -324,45 +339,47 @@
         out_refs[s][...] = held[me ^ s]
 
 
-def emit_kernel(exchange, order, mixed_ref, gain_ref, residual_ref, *refs):
+def emit_kernel(exchange, order, slots, mixed_ref, gain_ref, residual_ref, *refs):
     width = mixed_ref.shape[2] // 2
-    state_refs, out_ref = refs[: len(order)], refs[len(order)]
-    for n, slot in enumerate(order):
+    state_refs, out_ref = refs[: len(slots)], refs[len(slots)]
+    for n, slot in enumerate(slots):
         for u in range(PER_SLOT):
             h = head_of(exchange, slot, u)
-            mixed = mixed_ref[PER_SLOT * n + u]
-            state = state_refs[slot][u]
+            mixed = mixed_ref[PER_SLOT * order.index(slot) + u]
+            state = state_refs[n][u]
             out = dot(
                 jnp.concatenate(split(mixed[:, :width]), 1), jnp.concatenate([state, state], 0)
             ) + mixed[:, width:]
             scale = lax.rsqrt(jnp.mean(out * out, 1, keepdims=True) + 1e-05)
             out = out * scale * gain_ref[...]
             columns = pl.ds(pl.multiple_of(h * width, width), width)
-            out_ref[h] = (residual_ref[:, columns].astype(F32) + out).astype(BF16)
-
-
-def ffn_kernel(count, gain_ref, up_at, down_at, up_ref, down_ref, *refs):
-    parts, outs = refs[:count], refs[count : 2 * count]
-    tiles_in, act, total = refs[2 * count :]
+            out_ref[PER_SLOT * n + u] = (
+                residual_ref[:, columns].astype(F32) + out
+            ).astype(BF16)
+
+
+def ffn_kernel(count, exchange, pieces, gain_ref, up_at, down_at, up_ref, down_ref, *refs):
+    given, outs = refs[: count * len(pieces)], refs[count * len(pieces) :][:count]
+    tiles_in, act, total = refs[count * (len(pieces) + 1) :]
     groups, kept, side, _ = up_ref.shape
     tiles, tokens, _ = tiles_in.shape
     each = tiles // count
     me = lax.axis_index("tensor")
     squares = jnp.zeros((tokens, side), F32)
-    for part in parts:
-        for b in range(each):
-            wide = part[b].astype(F32)
-            squares += wide * wide
+    for n, part in enumerate(given):
+        base = (me ^ (n // len(pieces))) * each
+        for i, slot in enumerate(pieces[n % len(pieces)]):
+            for u in range(PER_SLOT):
+                tile = base + head_of(exchange, slot, u)
+                wide = part[PER_SLOT * i + u].astype(F32)
+                squares += wide * wide
+                tiles_in[tile] = (wide * gain_ref[pl.ds(tile, 1), :]).astype(BF16)
     scale = lax.rsqrt(jnp.sum(squares, 1, keepdims=True) / (tiles * side) + 1e-05)
-    for m, part in enumerate(parts):
-        base = (me ^ m) * each
-        for b in range(each):
-            gain = gain_ref[pl.ds(base + b, 1), :]
-            tiles_in[base + b] = (part[b].astype(F32) * scale * gain).astype(BF16)
+    scale = jnp.broadcast_to(scale, (tokens, side))
     for c in range(groups):
         picked = jnp.concatenate([tiles_in[up_at[c, j]] for j in range(kept)], 1)
         pre = dot(picked, up_ref[c].reshape(kept * side, side))
-        act[c] = jax.nn.gelu(pre).astype(BF16)
+        act[c] = jax.nn.gelu(pre * scale).astype(BF16)
     total[...] = jnp.zeros_like(total)
     for c in range(groups):
         now = act[c]
@@ -375,17 +392,23 @@
         out[...] = total[pl.ds(base, each)].astype(BF16)
 
 
-def final_kernel(hidden_ref, *refs):
-    out_ref = refs[-1]
-    tiles, _, side = hidden_ref.shape
-    for b in range(tiles):
-        total = refs[0][b].astype(F32)
-        for ref in refs[1:-1]:
-            total += ref[b].astype(F32)
-        out_ref[:, b * side : (b + 1) * side] = (hidden_ref[b].astype(F32) + total).astype(BF16)
-
-
-def local_call(kernel, out_shape, ins, args, scratch=(), flops=0, moved=0, limit=20 * MIB):
+def final_kernel(exchange, pieces, *refs):
+    given, sums, out_ref = refs[: len(pieces)], refs[len(pieces) : -1], refs[-1]
+    side = given[0].shape[2]
+    for part, slots in zip(given, pieces):
+        for i, slot in enumerate(slots):
+            for u in range(PER_SLOT):
+                tile = head_of(exchange, slot, u)
+                total = sums[0][tile].astype(F32)
+                for ref in sums[1:]:
+                    total += ref[tile].astype(F32)
+                columns = pl.ds(pl.multiple_of(tile * side, side), side)
+                out_ref[:, columns] = (
+                    part[PER_SLOT * i + u].astype(F32) + total
+                ).astype(BF16)
+
+
+def local_call(kernel, out_shape, ins, args, scratch=(), flops=0, moved=0, limit=8 * MIB):
     return pl.pallas_call(
         kernel,
         out_shape=out_shape,
@@ -440,52 +463,72 @@
         )
         outs = [term] * len(part) + [solution_rows]
         if not terms:
-            *given, sol, k_heads, v_heads, row_terms = local_call(
-                functools.partial(first_kernel, exchange, part),
-                outs + [by_head, by_head, rows],
-                [ANY] * 4,
-                (beta, decay, keys, values),
+            k_heads, v_heads = local_call(
+                sort_kernel,
+                [by_head, by_head],
+                [ANY] * 2,
+                (keys, values),
                 [
-                    pltpu.VMEM(beta.shape, F32),
-                    pltpu.VMEM(decay.shape, F32),
                     pltpu.VMEM(keys.shape, BF16),
                     pltpu.VMEM(values.shape, BF16),
-                    pltpu.VMEM((2, tokens * heads, width), F32),
-                    pltpu.VMEM((2, tokens * heads, width), F32),
-                    pltpu.SemaphoreType.DMA((4,)),
+                    pltpu.VMEM((2, 2, tokens * heads, width), F32),
+                    pltpu.SemaphoreType.DMA((2,)),
                 ],
                 limit=FIRST_LIMIT,
             )
+            *given, sol, row_terms = local_call(
+                functools.partial(first_kernel, exchange, part),
+                outs + [rows],
+                [VMEM] * 3,
+                (jnp.concatenate([beta, decay[None]]), k_heads, v_heads),
+                limit=16 * MIB,
+            )
         else:
+            first = [arrived[order[0]]] if part == order[-1:] and arrived else []
             *given, sol = local_call(
                 functools.partial(later_kernel, exchange, part),
                 outs,
-                [VMEM] * 3,
-                (k_heads, v_heads, row_terms),
+                [VMEM] * 3 + [ANY] * len(first),
+                (k_heads, v_heads, row_terms, *first),
+                flops=0,
             )
         terms.update(zip(part, given))
         solved.append(sol)
         if exchange:
             for s in part:
                 arrived[s] = lax.ppermute(terms[s], "seq", swaps[s]) if s else terms[s]
-    mixed = local_call(
-        functools.partial(mixing_kernel, exchange, orders),
-        jax.ShapeDtypeStruct((heads, tokens, 2 * width), F32),
-        [VMEM] * (3 + len(orders)),
-        (queries, k_heads, row_terms, *solved),
+    groups, _, side, _ = up_blocks.shape
+    tiles = heads * tensor_count
+    state = jax.ShapeDtypeStruct((PER_SLOT, width, width), BF16)
+    q_heads = local_call(
+        queries_kernel,
+        jax.ShapeDtypeStruct((heads, tokens, width), BF16),
+        [VMEM] + [ANY] * len(orders),
+        (queries, *solved),
         [pltpu.VMEM((tokens * heads, width), F32)],
         flops=3_000_000_000,
     )
-    state = jax.ShapeDtypeStruct((PER_SLOT, width, width), BF16)
+
+    def mix(after):
+        return local_call(
+            functools.partial(mixing_kernel, exchange, orders),
+            jax.ShapeDtypeStruct((heads, tokens, 2 * width), F32),
+            [VMEM] * (3 + len(orders)) + [ANY],
+            (q_heads, k_heads, row_terms, *solved, after),
+            flops=3_000_000_000,
+        )
+
     if exchange:
+        late = order[-1:] + order[:-1]
         inner = jax.ShapeDtypeStruct((slots - 1, PER_SLOT, width, width), F32)
         local, prefix, end = local_call(
-            functools.partial(chain_kernel, slots),
+            functools.partial(chain_kernel, late),
             [inner, inner, state],
             [VMEM] * slots,
-            [arrived[s] for s in range(slots)],
+            [arrived[s] for s in late],
             [pltpu.VMEM((slots, PER_SLOT, width, 2 * width), BF16)],
         )
+        mixed = mix(end)
         before = lax.ppermute(end, "seq", [(k, k + slots) for k in range(slots)])
         outgoing = local_call(
             functools.partial(entry_kernel, slots),
@@ -499,47 +542,53 @@
             states[s] = lax.ppermute(outgoing[s], "seq", swaps[s])
     else:
         states = prefix_states(terms)
-    hidden = local_call(
-        functools.partial(emit_kernel, exchange, order),
-        jax.ShapeDtypeStruct((heads, tokens, width), BF16),
-        [VMEM] * (3 + slots),
-        (mixed, out_gain.reshape(1, width), residual, *(states[s] for s in range(slots))),
-    )
+        mixed = mix(terms[0])
+    pieces = PIECES if exchange and slots == 4 else [list(range(slots))]
+    hidden = [
+        local_call(
+            functools.partial(emit_kernel, exchange, order, piece),
+            jax.ShapeDtypeStruct((PER_SLOT * len(piece), tokens, width), BF16),
+            [VMEM] * (3 + len(piece)),
+            (mixed, out_gain.reshape(1, width), residual, *(states[s] for s in piece)),
+        )
+        for piece in pieces
+    ]
 
     flips = {
         d: [(k, k ^ d) for k in range(tensor_count)]
         for d in (1 << b for b in range(tensor_count.bit_length() - 1))
     }
-    parts = {0: hidden}
-    for d in sorted(flips, reverse=True):
-        for m in list(parts):
-            parts[m | d] = lax.ppermute(parts[m], "tensor", flips[d])
-    groups, kept, side, _ = up_blocks.shape
-    tiles = heads * tensor_count
+    parts = [{0: given} for given in hidden]
+    for held in parts:
+        for d in sorted(flips, reverse=True):
+            for m in list(held):
+                held[m | d] = lax.ppermute(held[m], "tensor", flips[d])
     sums = local_call(
-        functools.partial(ffn_kernel, tensor_count),
+        functools.partial(ffn_kernel, tensor_count, exchange, pieces),
         [jax.ShapeDtypeStruct((heads, tokens, side), BF16)] * tensor_count,
-        [VMEM, SMEM, SMEM, VMEM, VMEM] + [VMEM] * tensor_count,
+        [VMEM, SMEM, SMEM, VMEM, VMEM] + [VMEM] * (tensor_count * len(pieces)),
         (
             ffn_gain.reshape(tiles, side), up_index, down_index, up_blocks, down_kept_tiles,
-            *(parts[m] for m in range(tensor_count)),
+            *(held[m] for m in range(tensor_count) for held in parts),
         ),
         [
             pltpu.VMEM((tiles, tokens, side), BF16),
             pltpu.VMEM((groups, tokens, side), BF16),
             pltpu.VMEM((tiles, tokens, side), F32),
         ],
+        limit=20 * MIB,
     )
-    held = {m: [part] for m, part in enumerate(sums)}
+    held = {m: [given] for m, given in enumerate(sums)}
     for d in sorted(flips):
         for m in [m for m in held if not m & d]:
             moved = lax.ppermute(added(held.pop(m | d)), "tensor", flips[d])
             held[m].append(moved)
+    moved = held[0]
     return local_call(
-        final_kernel,
+        functools.partial(final_kernel, exchange, pieces),
         jax.ShapeDtypeStruct((tokens, heads * side), BF16),
-        [VMEM] * (1 + len(held[0])),
-        (hidden, *held[0]),
+        [VMEM] * (len(pieces) + len(moved)),
+        (*hidden, *moved),
     )
 
 

time: 63.9 us -> 59.2 us (0.926)
  local copies, waits for them, and re-layouts: 4.46 us -> 0.99 us
  Pallas kernels: 22.2 us -> 21.2 us
  waiting for transfers between devices: 20 us -> 19.2 us
  other arithmetic: 0.07 us -> 0.79 us
    unnamed x26 -> x20, local copies, waits for them, and re-layouts: 4.46 us -> 0.99 us
    pallas_call x9 -> x11, Pallas kernels: 22.2 us -> 21.2 us  [local_call(): pl.pallas_call(kernel, out_shape=out_shape, in_specs=ins, out_specs=jax.t...]
    ppermute x1, waiting for transfers between devices: 1.7 us -> 0.66 us  [per_device(): before = lax.ppermute(end, 'seq', [(k, k + slots) for k in range(slots)])]
    ppermute x3, waiting for transfers between devices: 1.25 us -> 2.15 us  [per_device(): states[s] = lax.ppermute(outgoing[s], 'seq', swaps[s])]
    concatenate x0 -> x1, other arithmetic: none -> 0.72 us  [per_device(): jnp.concatenate([beta, decay[None]])]
    ppermute x3, waiting for transfers between devices: 2.84 us -> 2.13 us  [per_device(): arrived[s] = lax.ppermute(terms[s], 'seq', swaps[s]) if s else terms[s]]
  transfers between devices with their start and end apart: 13 -> 13, of which waited for: 7 -> 9; matrix products, arithmetic and copies ran while one was open for 0% -> 0% of each run, Pallas kernels for 8% -> 14%
where the time goes in v3:
time: 59.2 us; the launch traced here: 59 us
  Pallas kernels  21.2 us (36%)
  waiting for transfers between devices  19.2 us (32%)
  starting transfers between devices  16.6 us (28%)
  local copies, waits for them, and re-layouts  0.99 us (2%)
  other arithmetic  0.79 us (1%)
    pallas_call x11, Pallas kernels, local_call(): pl.pallas_call(kernel, out_shape=out_shape, in_specs=ins, out_specs=jax.t...  21.2 us
    ppermute x3, waiting for transfers between devices, per_device(): moved = lax.ppermute(added(held.pop(m | d)), 'tensor', flips[d])  7.85 us
    ppermute x3, waiting for transfers between devices, per_device(): held[m | d] = lax.ppermute(held[m], 'tensor', flips[d])  6.38 us
    ppermute x1, starting transfers between devices, per_device(): before = lax.ppermute(end, 'seq', [(k, k + slots) for k in range(slots)])  4.68 us
    ppermute x3, starting transfers between devices, per_device(): arrived[s] = lax.ppermute(terms[s], 'seq', swaps[s]) if s else terms[s]  4.67 us
    ppermute x3, starting transfers between devices, per_device(): states[s] = lax.ppermute(outgoing[s], 'seq', swaps[s])  3.55 us
    ppermute x3, starting transfers between devices, per_device(): moved = lax.ppermute(added(held.pop(m | d)), 'tensor', flips[d])  2.16 us
    ppermute x3, waiting for transfers between devices, per_device(): states[s] = lax.ppermute(outgoing[s], 'seq', swaps[s])  2.15 us
  transfers between devices with their start and end apart: 13, of which 9 were waited for; matrix products, arithmetic and copies ran while one was open for 0% of the time, Pallas kernels for 14%

profile of v3, /device:TPU:0, one launch (start us, length us, event | category | flops | bytes accessed | tf_op | source)
XLA Modules:
  0.0 59.0 jit_solution(10095327880452218439)
XLA Ops:
  0.0 1.5 %shard_map.118 = (bf16[8,2,128,128]{3,2,1,0:T(8,128)(2,1)S(1)}, bf16[8,2,128,128]{3,2,1,0:T(8,128)(2,1)S(1)}) custom-call(bf16[2,128,8,128]{3,2,1,0:T(8,128)(2,1)} %k_hbm.1, bf16[2,128,8,128]{3,2,1,0:T(8,128)(2,1)} %v_hbm.1), custom_call_target="tpu_custom_call" | custom-call | tf_op jit(solution)/shard_map/pallas_call | solution.py:412
  1.5 0.7 %pad_maximum_fusion.given_ref = f32[3,8,128]{2,1,0:T(8,128)S(1)} fusion(f32[1,8,128]{2,1,0:T(8,128)} %bitcast.9, f32[2,8,128]{2,1,0:T(8,128)} %param.15), kind=kLoop, calls=%fused_computation.1 | loop fusion | flops 3072 | bytes 24576 | tf_op jit(solution)/shard_map/concatenate | solution.py:483
  2.2 2.9 %shard_map.119 = (bf16[2,128,256]{2,1,0:T(8,128)(2,1)S(1)}, f32[2,256,256]{2,1,0:T(8,128)S(1)}, f32[6,8,128]{2,1,0:T(8,128)S(1)}) custom-call(f32[3,8,128]{2,1,0:T(8,128)S(1)} %pad_maximum_fusion.given_ref, bf16[8,2,128,128]{3,2,1,0:T(8,128)(2,1)S(1)} %get-tuple-element.26.k_heads, bf16[8,2,128,128]{3,2,1,0:T(8,128)(2,1)S(1)} %get-tuple-element.27.v_heads), custom_call_target="tpu_custom_call" | custom-call | tf_op jit(solution)/shard_map/pallas_call | solution.py:412
  5.2 4.0 %collective-permute-start = (bf16[2,128,256]{2,1,0:T(8,128)(2,1)S(1)}, bf16[2,128,256]{2,1,0:T(8,128)(2,1)S(1)}, u32[]{:S(2)}, u32[]{:S(2)}) collective-permute-start(bf16[2,128,256]{2,1,0:T(8,128)(2,1)S(1)} %get-tuple-element.31), channel_id=1, source_target_pairs={{0,12},{4,8},{8,4},{12,0},{16,28},{20,24},{24,20},{28,16},{1,13},{... | collective-permute-start | bytes 393224 | tf_op jit(solution)/shard_map/ppermute | solution.py:499
  9.2 4.2 %shard_map.120 = (bf16[2,128,256]{2,1,0:T(8,128)(2,1)S(1)}, bf16[2,128,256]{2,1,0:T(8,128)(2,1)S(1)}, f32[4,256,256]{2,1,0:T(8,128)S(1)}) custom-call(bf16[8,2,128,128]{3,2,1,0:T(8,128)(2,1)S(1)} %get-tuple-element.26.k_heads, bf16[8,2,128,128]{3,2,1,0:T(8,128)(2,1)S(1)} %get-tuple-element.27.v_heads, f32[6,8,128]{2,1,0:T(8,128)S(1)} %get-tuple-element.29.row_ref), custom_call_target="tpu_custom_call" | custom-call | tf_op jit(solution)/shard_map/pallas_call | solution.py:412
  13.4 0.6 %collective-permute-start.1 = (bf16[2,128,256]{2,1,0:T(8,128)(2,1)S(1)}, bf16[2,128,256]{2,1,0:T(8,128)(2,1)S(1)}, u32[]{:S(2)}, u32[]{:S(2)}) collective-permute-start(bf16[2,128,256]{2,1,0:T(8,128)(2,1)S(1)} %get-tuple-element.34), channel_id=1, source_target_pairs={{0,4},{4,0},{8,12},{12,8},{16,20},{20,16},{24,28},{28,24},{1,5},{5... | collective-permute-start | bytes 393224 | tf_op jit(solution)/shard_map/ppermute | solution.py:499
  14.0 0.0 collective-permute-start.2
  14.0 0.0 collective-permute-done.refs_0_.refs_1_
  14.0 2.8 %shard_map.121 = (bf16[2,128,256]{2,1,0:T(8,128)(2,1)S(1)}, f32[2,256,256]{2,1,0:T(8,128)S(1)}) custom-call(bf16[8,2,128,128]{3,2,1,0:T(8,128)(2,1)S(1)} %get-tuple-element.26.k_heads, bf16[8,2,128,128]{3,2,1,0:T(8,128)(2,1)S(1)} %get-tuple-element.27.v_heads, f32[6,8,128]{2,1,0:T(8,128)S(1)} %get-tuple-element.29.row_ref, ...), custom_call_target="tpu_custom_call" | custom-call | tf_op jit(solution)/shard_map/pallas_call | solution.py:412
  16.8 1.6 %collective-permute-done.1.refs_2_ = bf16[2,128,256]{2,1,0:T(8,128)(2,1)S(1)} collective-permute-done((bf16[2,128,256]{2,1,0:T(8,128)(2,1)S(1)}, bf16[2,128,256]{2,1,0:T(8,128)(2,1)S(1)}, u32[]{:S(2)}, u32[]{:S(2)}) %collective-permute-start.1) | collective-permute-done | bytes 131104 | tf_op jit(solution)/shard_map/ppermute | solution.py:499
  18.4 0.5 collective-permute-done.2.refs_3_
  19.0 0.7 %shard_map.123 = (f32[3,2,128,128]{3,2,1,0:T(8,128)S(1)}, f32[3,2,128,128]{3,2,1,0:T(8,128)S(1)}, bf16[2,128,128]{2,1,0:T(8,128)(2,1)S(1)}) custom-call(bf16[2,128,256]{2,1,0:T(8,128)(2,1)S(1)} %get-tuple-element.33.refs_0_, bf16[2,128,256]{2,1,0:T(8,128)(2,1)S(1)} %collective-permute-done.refs_0_.refs_1_, ...), custom_call_target="tpu_custom_call" | custom-call | tf_op jit(solution)/shard_map/pallas_call | solution.py:412
  19.7 4.7 %collective-permute-start.3 = (bf16[2,128,128]{2,1,0:T(8,128)(2,1)S(1)}, bf16[2,128,128]{2,1,0:T(8,128)(2,1)S(1)}, u32[]{:S(2)}, u32[]{:S(2)}) collective-permute-start(bf16[2,128,128]{2,1,0:T(8,128)(2,1)S(1)} %get-tuple-element.36.refs_3_), channel_id=1, source_target_pairs={{0,16},{4,20},{8,24},{12,28},{1,17},{5,21},{9,25},{13,29},{2,18},{... | collective-permute-start | bytes 196616 | tf_op jit(solution)/shard_map/ppermute | solution.py:532
  24.4 0.0 copy-start.5
  24.4 0.9 %copy-done.5 = bf16[128,8,128]{2,1,0:T(8,128)(2,1)S(1)} copy-done((bf16[128,8,128]{2,1,0:T(8,128)(2,1)S(1)}, bf16[128,8,128]{2,1,0:T(8,128)(2,1)}, u32[]{:S(2)}) %copy-start.5) | copy-done | bytes 262168
  25.4 0.1 shard_map.122.q_heads
  25.5 0.0 copy-start
  25.5 0.0 copy-start.4
  25.5 0.0 copy-start.1
  25.5 0.0 copy-start.2
  25.5 0.0 copy-start.3
  25.5 0.7 %collective-permute-done.3.before_ref = bf16[2,128,128]{2,1,0:T(8,128)(2,1)S(1)} collective-permute-done((bf16[2,128,128]{2,1,0:T(8,128)(2,1)S(1)}, bf16[2,128,128]{2,1,0:T(8,128)(2,1)S(1)}, u32[]{:S(2)}, u32[]{:S(2)}) %collective-permute-start.3) | collective-permute-done | bytes 65568 | tf_op jit(solution)/shard_map/ppermute | solution.py:532
  26.2 0.3 shard_map.125
  26.5 1.6 %collective-permute-start.4 = (bf16[2,128,128]{2,1,0:T(8,128)(2,1)S(1)}, bf16[2,128,128]{2,1,0:T(8,128)(2,1)S(1)}, u32[]{:S(2)}, u32[]{:S(2)}) collective-permute-start(bf16[2,128,128]{2,1,0:T(8,128)(2,1)S(1)} %get-tuple-element.40), channel_id=1, source_target_pairs={{0,4},{4,0},{8,12},{12,8},{16,20},{20,16},{24,28},{28,24},{1,5},{5... | collective-permute-start | bytes 196616 | tf_op jit(solution)/shard_map/ppermute | solution.py:542
  28.1 0.3 collective-permute-start.5
  28.4 1.6 %collective-permute-start.6 = (bf16[2,128,128]{2,1,0:T(8,128)(2,1)S(1)}, bf16[2,128,128]{2,1,0:T(8,128)(2,1)S(1)}, u32[]{:S(2)}, u32[]{:S(2)}) collective-permute-start(bf16[2,128,128]{2,1,0:T(8,128)(2,1)S(1)} %get-tuple-element.42), channel_id=1, source_target_pairs={{0,12},{4,8},{8,4},{12,0},{16,28},{20,24},{24,20},{28,16},{1,13},{... | collective-permute-start | bytes 196616 | tf_op jit(solution)/shard_map/ppermute | solution.py:542
  30.0 1.4 %shard_map.124.mixed_ref = f32[8,128,256]{2,1,0:T(8,128)S(1)} custom-call(bf16[8,128,128]{2,1,0:T(8,128)(2,1)S(1)} %shard_map.122.q_heads, bf16[8,2,128,128]{3,2,1,0:T(8,128)(2,1)S(1)} %get-tuple-element.26.k_heads, f32[6,8,128]{2,1,0:T(8,128)S(1)} %get-tuple-element.29.row_ref, f32[2,256,256]{2,1,0:T(8,128)S(1)} %get-tuple-element.28.refs_0_, ...), custom_call_target="tpu_custom_call" | custom-call | flops 3000000000 | tf_op jit(solution)/shard_map/pallas_call | solution.py:412
  31.4 0.0 collective-permute-done.4.refs_1_
  31.4 0.9 %collective-permute-done.5.refs_2_ = bf16[2,128,128]{2,1,0:T(8,128)(2,1)S(1)} collective-permute-done((bf16[2,128,128]{2,1,0:T(8,128)(2,1)S(1)}, bf16[2,128,128]{2,1,0:T(8,128)(2,1)S(1)}, u32[]{:S(2)}, u32[]{:S(2)}) %collective-permute-start.5) | collective-permute-done | bytes 65568 | tf_op jit(solution)/shard_map/ppermute | solution.py:542
  32.4 1.2 %collective-permute-done.6.refs_3_ = bf16[2,128,128]{2,1,0:T(8,128)(2,1)S(1)} collective-permute-done((bf16[2,128,128]{2,1,0:T(8,128)(2,1)S(1)}, bf16[2,128,128]{2,1,0:T(8,128)(2,1)S(1)}, u32[]{:S(2)}, u32[]{:S(2)}) %collective-permute-start.6) | collective-permute-done | bytes 65568 | tf_op jit(solution)/shard_map/ppermute | solution.py:542
  33.6 0.0 copy-done.4
  33.6 0.4 shard_map.126.refs_0_
  34.0 1.6 %collective-permute-start.8 = (bf16[8,128,128]{2,1,0:T(8,128)(2,1)S(1)}, bf16[8,128,128]{2,1,0:T(8,128)(2,1)S(1)}, u32[]{:S(2)}, u32[]{:S(2)}) collective-permute-start(bf16[8,128,128]{2,1,0:T(8,128)(2,1)S(1)} %shard_map.126.refs_0_), channel_id=1, source_target_pairs={{0,2},{1,3},{2,0},{3,1},{4,6},{5,7},{6,4},{7,5},{8,10},{9,11},{10,... | collective-permute-start | bytes 786440 | tf_op jit(solution)/shard_map/ppermute | solution.py:565
  35.6 0.0 collective-permute-start.7
  35.6 4.8 %collective-permute-done.8.refs_2_ = bf16[8,128,128]{2,1,0:T(8,128)(2,1)S(1)} collective-permute-done((bf16[8,128,128]{2,1,0:T(8,128)(2,1)S(1)}, bf16[8,128,128]{2,1,0:T(8,128)(2,1)S(1)}, u32[]{:S(2)}, u32[]{:S(2)}) %collective-permute-start.8) | collective-permute-done | bytes 262176 | tf_op jit(solution)/shard_map/ppermute | solution.py:565
  40.4 0.0 collective-permute-start.9
  40.4 0.0 collective-permute-done.7.refs_1_
  40.4 1.5 %collective-permute-done.9.refs_3_ = bf16[8,128,128]{2,1,0:T(8,128)(2,1)S(1)} collective-permute-done((bf16[8,128,128]{2,1,0:T(8,128)(2,1)S(1)}, bf16[8,128,128]{2,1,0:T(8,128)(2,1)S(1)}, u32[]{:S(2)}, u32[]{:S(2)}) %collective-permute-start.9) | collective-permute-done | bytes 262176 | tf_op jit(solution)/shard_map/ppermute | solution.py:565
  42.0 0.0 slice-done
  42.0 6.0 %shard_map.127 = (bf16[8,128,128]{2,1,0:T(8,128)(2,1)S(1)}, bf16[8,128,128]{2,1,0:T(8,128)(2,1)S(1)}, bf16[8,128,128]{2,1,0:T(8,128)(2,1)S(1)}, bf16[8,128,128]{2,1,0:T(8,128)(2,1)S(1)}) custom-call(f32[32,128]{1,0:T(8,128)S(1)} %bitcast.7, s32[16,16]{1,0:T(8,128)S(1)} %copy-done.2, s32[16,16]{1,0:T(8,128)S(1)} %copy-done.3, ...), custom_call_target="tpu_custom_call" | custom-call | tf_op jit(solution)/shard_map/pallas_call | solution.py:412
  48.0 0.2 collective-permute-start.11
  48.2 0.4 collective-permute-start.10
  48.6 1.0 %collective-permute-done.11 = bf16[8,128,128]{2,1,0:T(8,128)(2,1)S(1)} collective-permute-done((bf16[8,128,128]{2,1,0:T(8,128)(2,1)S(1)}, bf16[8,128,128]{2,1,0:T(8,128)(2,1)S(1)}, u32[]{:S(2)}, u32[]{:S(2)}) %collective-permute-start.11) | collective-permute-done | bytes 262176 | tf_op jit(solution)/shard_map/ppermute | solution.py:584
  49.6 0.1 add_convert_fusion
  49.7 1.6 %collective-permute-start.12 = (bf16[8,128,128]{2,1,0:T(8,128)(2,1)S(1)}, bf16[8,128,128]{2,1,0:T(8,128)(2,1)S(1)}, u32[]{:S(2)}, u32[]{:S(2)}) collective-permute-start(bf16[8,128,128]{2,1,0:T(8,128)(2,1)S(1)} %add_convert_fusion), channel_id=1, source_target_pairs={{0,2},{1,3},{2,0},{3,1},{4,6},{5,7},{6,4},{7,5},{8,10},{9,11},{10,... | collective-permute-start | bytes 786440 | tf_op jit(solution)/shard_map/ppermute | solution.py:584
  51.3 0.0 collective-permute-done.10.refs_2_
  51.3 6.8 %collective-permute-done.12.refs_3_ = bf16[8,128,128]{2,1,0:T(8,128)(2,1)S(1)} collective-permute-done((bf16[8,128,128]{2,1,0:T(8,128)(2,1)S(1)}, bf16[8,128,128]{2,1,0:T(8,128)(2,1)S(1)}, u32[]{:S(2)}, u32[]{:S(2)}) %collective-permute-start.12) | collective-permute-done | bytes 262176 | tf_op jit(solution)/shard_map/ppermute | solution.py:584
  58.1 0.9 %shard_map.128 = bf16[128,1024]{1,0:T(8,128)(2,1)} custom-call(bf16[8,128,128]{2,1,0:T(8,128)(2,1)S(1)} %shard_map.126.refs_0_, bf16[8,128,128]{2,1,0:T(8,128)(2,1)S(1)} %get-tuple-element.43.refs_1_, bf16[8,128,128]{2,1,0:T(8,128)(2,1)S(1)} %collective-permute-done.10.refs_2_, bf16[8,128,128]{2,1,0:T(8,128)(2,1)S(1)} %collective-permute-done.12.refs_3_), custom_call_target="tpu_custom_call" | custom-call | tf_op jit(solution)/shard_map/pallas_call | solution.py:412
  (13 shorter events, 0.0 us)
Async XLA Ops:
  5.2 8.9 %collective-permute-start = (bf16[2,128,256]{2,1,0:T(8,128)(2,1)S(1)}, bf16[2,128,256]{2,1,0:T(8,128)(2,1)S(1)}, u32[]{:S(2)}, u32[]{:S(2)}) collective-permute-start(bf16[2,128,256]{2,1,0:T(8,128)(2,1)S(1)} %get-tuple-element.31), channel_id=1, source_target_pairs={{0,12},{4,8},{8,4},{12,0},{16,28},{20,24},{24,20},{28,16},{1,13},{... | collective-permute-start | bytes 393224 | tf_op jit(solution)/shard_map/ppermute | solution.py:499
  13.4 5.0 %collective-permute-start.1 = (bf16[2,128,256]{2,1,0:T(8,128)(2,1)S(1)}, bf16[2,128,256]{2,1,0:T(8,128)(2,1)S(1)}, u32[]{:S(2)}, u32[]{:S(2)}) collective-permute-start(bf16[2,128,256]{2,1,0:T(8,128)(2,1)S(1)} %get-tuple-element.34), channel_id=1, source_target_pairs={{0,4},{4,0},{8,12},{12,8},{16,20},{20,16},{24,28},{28,24},{1,5},{5... | collective-permute-start | bytes 393224 | tf_op jit(solution)/shard_map/ppermute | solution.py:499
  14.0 5.0 %collective-permute-start.2 = (bf16[2,128,256]{2,1,0:T(8,128)(2,1)S(1)}, bf16[2,128,256]{2,1,0:T(8,128)(2,1)S(1)}, u32[]{:S(2)}, u32[]{:S(2)}) collective-permute-start(bf16[2,128,256]{2,1,0:T(8,128)(2,1)S(1)} %get-tuple-element.35), channel_id=1, source_target_pairs={{0,8},{4,12},{8,0},{12,4},{16,24},{20,28},{24,16},{28,20},{1,9},{5... | collective-permute-start | bytes 393224 | tf_op jit(solution)/shard_map/ppermute | solution.py:499
  19.7 6.5 %collective-permute-start.3 = (bf16[2,128,128]{2,1,0:T(8,128)(2,1)S(1)}, bf16[2,128,128]{2,1,0:T(8,128)(2,1)S(1)}, u32[]{:S(2)}, u32[]{:S(2)}) collective-permute-start(bf16[2,128,128]{2,1,0:T(8,128)(2,1)S(1)} %get-tuple-element.36.refs_3_), channel_id=1, source_target_pairs={{0,16},{4,20},{8,24},{12,28},{1,17},{5,21},{9,25},{13,29},{2,18},{... | collective-permute-start | bytes 196616 | tf_op jit(solution)/shard_map/ppermute | solution.py:532
  24.4 1.0 %copy-start.5 = (bf16[128,8,128]{2,1,0:T(8,128)(2,1)S(1)}, bf16[128,8,128]{2,1,0:T(8,128)(2,1)}, u32[]{:S(2)}) copy-start(bf16[128,8,128]{2,1,0:T(8,128)(2,1)} %q_ref.1) | copy-start | bytes 786436
  25.3 16.6 %slice-start = ((s8[8388608]{0:T(1024)(128)(4,1)}), s8[4194304]{0:T(1024)(128)(4,1)S(1)}, s32[]{:S(2)}) async-start(s8[8388608]{0:T(1024)(128)(4,1)} %bitcast.3), calls=%async_computation | async-start | bytes 8388608
  25.4 16.6 %slice-start.2 = ((s8[8388608]{0:T(1024)(128)(4,1)}), s8[4194304]{0:T(1024)(128)(4,1)S(1)}, s32[]{:S(2)}) async-start(s8[8388608]{0:T(1024)(128)(4,1)} %bitcast.5), calls=%async_computation.2 | async-start | bytes 8388608
  25.5 8.1 %copy-start = (bf16[128,1024]{1,0:T(8,128)(2,1)S(1)}, bf16[128,1024]{1,0:T(8,128)(2,1)}, u32[]{:S(2)}) copy-start(bf16[128,1024]{1,0:T(8,128)(2,1)} %residual_ref.1) | copy-start | bytes 786436
  25.5 8.1 %copy-start.4 = (f32[128]{0:T(128)S(1)}, f32[128]{0:T(128)}, u32[]{:S(2)}) copy-start(f32[128]{0:T(128)} %param.17) | copy-start | bytes 1540
  25.5 16.5 %copy-start.1 = (f32[4096]{0:T(1024)S(1)}, f32[4096]{0:T(1024)}, u32[]{:S(2)}) copy-start(f32[4096]{0:T(1024)} %param.19) | copy-start | bytes 49156
  25.5 16.5 %copy-start.2 = (s32[16,16]{1,0:T(8,128)S(1)}, s32[16,16]{1,0:T(8,128)}, u32[]{:S(2)}) copy-start(s32[16,16]{1,0:T(8,128)} %up_at.1) | copy-start | bytes 3076
  25.5 16.5 %copy-start.3 = (s32[16,16]{1,0:T(8,128)S(1)}, s32[16,16]{1,0:T(8,128)}, u32[]{:S(2)}) copy-start(s32[16,16]{1,0:T(8,128)} %down_at.1) | copy-start | bytes 3076
  26.5 5.0 %collective-permute-start.4 = (bf16[2,128,128]{2,1,0:T(8,128)(2,1)S(1)}, bf16[2,128,128]{2,1,0:T(8,128)(2,1)S(1)}, u32[]{:S(2)}, u32[]{:S(2)}) collective-permute-start(bf16[2,128,128]{2,1,0:T(8,128)(2,1)S(1)} %get-tuple-element.40), channel_id=1, source_target_pairs={{0,4},{4,0},{8,12},{12,8},{16,20},{20,16},{24,28},{28,24},{1,5},{5... | collective-permute-start | bytes 196616 | tf_op jit(solution)/shard_map/ppermute | solution.py:542
  28.1 4.3 %collective-permute-start.5 = (bf16[2,128,128]{2,1,0:T(8,128)(2,1)S(1)}, bf16[2,128,128]{2,1,0:T(8,128)(2,1)S(1)}, u32[]{:S(2)}, u32[]{:S(2)}) collective-permute-start(bf16[2,128,128]{2,1,0:T(8,128)(2,1)S(1)} %get-tuple-element.41), channel_id=1, source_target_pairs={{0,8},{4,12},{8,0},{12,4},{16,24},{20,28},{24,16},{28,20},{1,9},{5... | collective-permute-start | bytes 196616 | tf_op jit(solution)/shard_map/ppermute | solution.py:542
  28.4 13.6 %slice-start.1 = ((s8[8388608]{0:T(1024)(128)(4,1)}), s8[4194304]{0:T(1024)(128)(4,1)S(1)}, s32[]{:S(2)}) async-start(s8[8388608]{0:T(1024)(128)(4,1)} %bitcast.3), calls=%async_computation.1 | async-start | bytes 8388608
  28.4 13.6 %slice-start.3 = ((s8[8388608]{0:T(1024)(128)(4,1)}), s8[4194304]{0:T(1024)(128)(4,1)S(1)}, s32[]{:S(2)}) async-start(s8[8388608]{0:T(1024)(128)(4,1)} %bitcast.5), calls=%async_computation.3 | async-start | bytes 8388608
  28.4 5.2 %collective-permute-start.6 = (bf16[2,128,128]{2,1,0:T(8,128)(2,1)S(1)}, bf16[2,128,128]{2,1,0:T(8,128)(2,1)S(1)}, u32[]{:S(2)}, u32[]{:S(2)}) collective-permute-start(bf16[2,128,128]{2,1,0:T(8,128)(2,1)S(1)} %get-tuple-element.42), channel_id=1, source_target_pairs={{0,12},{4,8},{8,4},{12,0},{16,28},{20,24},{24,20},{28,16},{1,13},{... | collective-permute-start | bytes 196616 | tf_op jit(solution)/shard_map/ppermute | solution.py:542
  34.0 6.4 %collective-permute-start.8 = (bf16[8,128,128]{2,1,0:T(8,128)(2,1)S(1)}, bf16[8,128,128]{2,1,0:T(8,128)(2,1)S(1)}, u32[]{:S(2)}, u32[]{:S(2)}) collective-permute-start(bf16[8,128,128]{2,1,0:T(8,128)(2,1)S(1)} %shard_map.126.refs_0_), channel_id=1, source_target_pairs={{0,2},{1,3},{2,0},{3,1},{4,6},{5,7},{6,4},{7,5},{8,10},{9,11},{10,... | collective-permute-start | bytes 786440 | tf_op jit(solution)/shard_map/ppermute | solution.py:565
  35.6 4.9 %collective-permute-start.7 = (bf16[8,128,128]{2,1,0:T(8,128)(2,1)S(1)}, bf16[8,128,128]{2,1,0:T(8,128)(2,1)S(1)}, u32[]{:S(2)}, u32[]{:S(2)}) collective-permute-start(bf16[8,128,128]{2,1,0:T(8,128)(2,1)S(1)} %shard_map.126.refs_0_), channel_id=1, source_target_pairs={{0,1},{1,0},{2,3},{3,2},{4,5},{5,4},{6,7},{7,6},{8,9},{9,8},{10,11... | collective-permute-start | bytes 786440 | tf_op jit(solution)/shard_map/ppermute | solution.py:565
  40.4 1.5 %collective-permute-start.9 = (bf16[8,128,128]{2,1,0:T(8,128)(2,1)S(1)}, bf16[8,128,128]{2,1,0:T(8,128)(2,1)S(1)}, u32[]{:S(2)}, u32[]{:S(2)}) collective-permute-start(bf16[8,128,128]{2,1,0:T(8,128)(2,1)S(1)} %collective-permute-done.8.refs_2_), channel_id=1, source_target_pairs={{0,1},{1,0},{2,3},{3,2},{4,5},{5,4},{6,7},{7,6},{8,9},{9,8},{10,11... | collective-permute-start | bytes 786440 | tf_op jit(solution)/shard_map/ppermute | solution.py:565
  48.0 1.6 %collective-permute-start.11 = (bf16[8,128,128]{2,1,0:T(8,128)(2,1)S(1)}, bf16[8,128,128]{2,1,0:T(8,128)(2,1)S(1)}, u32[]{:S(2)}, u32[]{:S(2)}) collective-permute-start(bf16[8,128,128]{2,1,0:T(8,128)(2,1)S(1)} %get-tuple-element.46), channel_id=1, source_target_pairs={{0,1},{1,0},{2,3},{3,2},{4,5},{5,4},{6,7},{7,6},{8,9},{9,8},{10,11... | collective-permute-start | bytes 786440 | tf_op jit(solution)/shard_map/ppermute | solution.py:584
  48.2 3.1 %collective-permute-start.10 = (bf16[8,128,128]{2,1,0:T(8,128)(2,1)S(1)}, bf16[8,128,128]{2,1,0:T(8,128)(2,1)S(1)}, u32[]{:S(2)}, u32[]{:S(2)}) collective-permute-start(bf16[8,128,128]{2,1,0:T(8,128)(2,1)S(1)} %get-tuple-element.44), channel_id=1, source_target_pairs={{0,1},{1,0},{2,3},{3,2},{4,5},{5,4},{6,7},{7,6},{8,9},{9,8},{10,11... | collective-permute-start | bytes 786440 | tf_op jit(solution)/shard_map/ppermute | solution.py:584
  49.7 8.4 %collective-permute-start.12 = (bf16[8,128,128]{2,1,0:T(8,128)(2,1)S(1)}, bf16[8,128,128]{2,1,0:T(8,128)(2,1)S(1)}, u32[]{:S(2)}, u32[]{:S(2)}) collective-permute-start(bf16[8,128,128]{2,1,0:T(8,128)(2,1)S(1)} %add_convert_fusion), channel_id=1, source_target_pairs={{0,2},{1,3},{2,0},{3,1},{4,6},{5,7},{6,4},{7,5},{8,10},{9,11},{10,... | collective-permute-start | bytes 786440 | tf_op jit(solution)/shard_map/ppermute | solution.py:584

commit v4 on v3

--- a/solution.py
+++ b/solution.py
@@ -309,18 +309,27 @@
     me = lax.rem(lax.axis_index("seq"), group)
     for n, s in enumerate(order):
         held[s] = term_refs[n][...]
+    states, prefixes = [], []
     for u in range(PER_SLOT):
         first = held[me, u]
-        state = first[:, width:].astype(F32)
-        prefix = first[:, :width].astype(F32)
-        for k in range(1, group):
-            local_ref[k - 1, u] = state
-            prefix_ref[k - 1, u] = prefix
-            block = held[me ^ k, u]
-            both = dot(block[:, :width], jnp.concatenate([*split(state), *split(prefix)], 1))
-            state = both[:, :width] + both[:, width : 2 * width] + block[:, width:].astype(F32)
-            prefix = both[:, 2 * width : 3 * width] + both[:, 3 * width :]
-        end_ref[u] = state.astype(BF16)
+        states.append(first[:, width:].astype(F32))
+        prefixes.append(first[:, :width].astype(F32))
+    for k in range(1, group):
+        for u in range(PER_SLOT):
+            local_ref[k - 1, u] = states[u]
+            prefix_ref[k - 1, u] = prefixes[u]
+        blocks = [held[me ^ k, u] for u in range(PER_SLOT)]
+        both = [
+            dot(block[:, :width], jnp.concatenate([*split(state), *split(prefix)], 1))
+            for block, state, prefix in zip(blocks, states, prefixes)
+        ]
+        states = [
+            x[:, :width] + x[:, width : 2 * width] + block[:, width:].astype(F32)
+            for x, block in zip(both, blocks)
+        ]
+        prefixes = [x[:, 2 * width : 3 * width] + x[:, 3 * width :] for x in both]
+    for u in range(PER_SLOT):
+        end_ref[u] = states[u].astype(BF16)
 
 
 def entry_kernel(group, local_ref, prefix_ref, before_ref, *refs):
@@ -358,9 +367,8 @@
             ).astype(BF16)
 
 
-def ffn_kernel(count, exchange, pieces, gain_ref, up_at, down_at, up_ref, down_ref, *refs):
-    given, outs = refs[: count * len(pieces)], refs[count * len(pieces) :][:count]
-    tiles_in, act, total = refs[count * (len(pieces) + 1) :]
+def ffn_kernel(count, exchange, pieces, gain_ref, up_at, up_ref, down_ref, *refs):
+    given, (act, *outs, tiles_in) = refs[: count * len(pieces)], refs[count * len(pieces) :]
     groups, kept, side, _ = up_ref.shape
     tiles, tokens, _ = tiles_in.shape
     each = tiles // count
@@ -379,17 +387,48 @@
     for c in range(groups):
         picked = jnp.concatenate([tiles_in[up_at[c, j]] for j in range(kept)], 1)
         pre = dot(picked, up_ref[c].reshape(kept * side, side))
-        act[c] = jax.nn.gelu(pre * scale).astype(BF16)
-    total[...] = jnp.zeros_like(total)
-    for c in range(groups):
-        now = act[c]
-        for j in range(0, kept, 2):
-            both = dot(now, jnp.concatenate([down_ref[c, j], down_ref[c, j + 1]], 1))
-            total[down_at[c, j]] += both[:, :side]
-            total[down_at[c, j + 1]] += both[:, side:]
-    for m, out in enumerate(outs):
-        base = (me ^ m) * each
-        out[...] = total[pl.ds(base, each)].astype(BF16)
+        act[:, c * side : (c + 1) * side] = jax.nn.gelu(pre * scale).astype(BF16)
+    down_sums(range(count - 1, 0, -1), down_ref, act, outs)
+
+
+def down_sums(ms, down_ref, act_ref, outs):
+    given = act_ref[...]
+    for m, out in zip(ms, outs):
+        each, _, side = out.shape
+        for b in range(0, each, 2):
+            pair = jnp.concatenate([down_ref[m * each + b], down_ref[m * each + b + 1]], 1)
+            both = dot(given, pair).astype(BF16)
+            out[b] = both[:, :side]
+            out[b + 1] = both[:, side:]
+
+
+def own_down_kernel(down_ref, act_ref, after_ref, out_ref):
+    down_sums([0], down_ref, act_ref, [out_ref])
+
+
+def relay_kernel(given_ref, after_ref, out_ref):
+    out_ref[...] = given_ref[...]
+
+
+def dense_kernel(count, at_ref, tiles_ref, after_ref, out_ref):
+    groups, kept, side, _ = tiles_ref.shape
+    tiles, rows, _ = out_ref.shape
+    each = tiles // count
+    me = lax.axis_index("tensor")
+
+    def clear(n, carry):
+        out_ref[n] = jnp.zeros((rows, side), BF16)
+        return carry
+
+    def place(c, carry):
+        hidden = pl.ds(pl.multiple_of(c * side, side), side)
+        for j in range(kept):
+            at = at_ref[c, j]
+            out_ref[((at // each) ^ me) * each + lax.rem(at, each), hidden] = tiles_ref[c, j]
+        return carry
+
+    lax.fori_loop(0, tiles, clear, 0, unroll=4)
+    lax.fori_loop(0, groups, place, 0, unroll=2)
 
 
 def final_kernel(exchange, pieces, *refs):
@@ -481,6 +520,7 @@
                 outs + [rows],
                 [VMEM] * 3,
                 (jnp.concatenate([beta, decay[None]]), k_heads, v_heads),
+                flops=3_000_000_000,
                 limit=16 * MIB,
             )
         else:
@@ -490,7 +530,7 @@
                 outs,
                 [VMEM] * 3 + [ANY] * len(first),
                 (k_heads, v_heads, row_terms, *first),
-                flops=0,
+                flops=4_000_000_000,
             )
         terms.update(zip(part, given))
         solved.append(sol)
@@ -508,6 +548,15 @@
         [pltpu.VMEM((tokens * heads, width), F32)],
         flops=3_000_000_000,
     )
+
+    def densely(after):
+        return local_call(
+            functools.partial(dense_kernel, tensor_count),
+            jax.ShapeDtypeStruct((tiles, groups * side, side), BF16),
+            [SMEM, VMEM, ANY],
+            (down_index, down_kept_tiles, after),
+            flops=3_000_000_000,
+        )
 
     def mix(after):
         return local_call(
@@ -558,32 +607,45 @@
         d: [(k, k ^ d) for k in range(tensor_count)]
         for d in (1 << b for b in range(tensor_count.bit_length() - 1))
     }
+    down_dense = densely(hidden[0])
     parts = [{0: given} for given in hidden]
     for held in parts:
         for d in sorted(flips, reverse=True):
             for m in list(held):
-                held[m | d] = lax.ppermute(held[m], "tensor", flips[d])
-    sums = local_call(
+                sent = held[m]
+                if m and d == 1:
+                    sent = local_call(
+                        relay_kernel,
+                        jax.ShapeDtypeStruct(sent.shape, sent.dtype),
+                        [VMEM, ANY],
+                        (sent, down_dense),
+                    )
+                held[m | d] = lax.ppermute(sent, "tensor", flips[d])
+    part = jax.ShapeDtypeStruct((heads, tokens, side), BF16)
+    others = list(range(tensor_count - 1, 0, -1))
+    act, *sums = local_call(
         functools.partial(ffn_kernel, tensor_count, exchange, pieces),
-        [jax.ShapeDtypeStruct((heads, tokens, side), BF16)] * tensor_count,
-        [VMEM, SMEM, SMEM, VMEM, VMEM] + [VMEM] * (tensor_count * len(pieces)),
+        [jax.ShapeDtypeStruct((tokens, groups * side), BF16)] + [part] * len(others),
+        [VMEM, SMEM, VMEM, VMEM] + [VMEM] * (tensor_count * len(pieces)),
         (
-            ffn_gain.reshape(tiles, side), up_index, down_index, up_blocks, down_kept_tiles,
+            ffn_gain.reshape(tiles, side), up_index, up_blocks, down_dense,
             *(held[m] for m in range(tensor_count) for held in parts),
         ),
-        [
-            pltpu.VMEM((tiles, tokens, side), BF16),
-            pltpu.VMEM((groups, tokens, side), BF16),
-            pltpu.VMEM((tiles, tokens, side), F32),
-        ],
-        limit=20 * MIB,
+        [pltpu.VMEM((tiles, tokens, side), BF16)],
+        limit=12 * MIB,
     )
-    held = {m: [given] for m, given in enumerate(sums)}
+    held = {m: [given] for m, given in zip(others, sums)}
     for d in sorted(flips):
-        for m in [m for m in held if not m & d]:
-            moved = lax.ppermute(added(held.pop(m | d)), "tensor", flips[d])
-            held[m].append(moved)
-    moved = held[0]
+        for m in sorted(m for m in held if not m & d and m | d in held):
+            held[m].append(lax.ppermute(added(held.pop(m | d)), "tensor", flips[d]))
+    crossing = {m: added(held[m]) for m in held}
+    own = local_call(
+        own_down_kernel, part, [VMEM, VMEM, ANY], (down_dense, act, crossing[max(crossing)]),
+        flops=1_000_000_000,
+    )
+    moved = [own] + [
+        lax.ppermute(crossing[m], "tensor", flips[m]) for m in sorted(crossing)
+    ]
     return local_call(
         functools.partial(final_kernel, exchange, pieces),
         jax.ShapeDtypeStruct((tokens, heads * side), BF16),

time: 59.2 us -> 58.8 us (level)
  Pallas kernels: 21.2 us -> 25.8 us
  waiting for transfers between devices: 19.2 us -> 14.8 us
  local copies, waits for them, and re-layouts: 0.99 us -> 0.06 us
    ppermute x6, waiting for transfers between devices: 14.2 us -> 8.89 us  [the longest x2 6.7 us: per_device(): lax.ppermute(crossing[m], 'tensor', flips[m])]
    pallas_call x11 -> x14, Pallas kernels: 21.2 us -> 25.8 us  [local_call(): pl.pallas_call(kernel, out_shape=out_shape, in_specs=ins, out_specs=jax.t...]
    ppermute x1, waiting for transfers between devices: 0.66 us -> 1.63 us  [per_device(): before = lax.ppermute(end, 'seq', [(k, k + slots) for k in range(slots)])]
    unnamed x20, local copies, waits for them, and re-layouts: 0.99 us -> 0.06 us
  transfers between devices with their start and end apart: 13 -> 13, of which waited for: 9 -> 8; matrix products, arithmetic and copies ran while one was open for 0% -> 0% of each run, Pallas kernels for 14% -> 24%
where the time goes in v4:
time: 58.8 us; the launch traced here: 58.5 us
  Pallas kernels  25.8 us (44%)
  starting transfers between devices  16.8 us (29%)
  waiting for transfers between devices  14.8 us (25%)
  other arithmetic  0.79 us (1%)
    pallas_call x14, Pallas kernels, local_call(): pl.pallas_call(kernel, out_shape=out_shape, in_specs=ins, out_specs=jax.t...  25.8 us
    ppermute x2, waiting for transfers between devices, per_device(): lax.ppermute(crossing[m], 'tensor', flips[m])  6.7 us
    ppermute x1, starting transfers between devices, per_device(): before = lax.ppermute(end, 'seq', [(k, k + slots) for k in range(slots)])  4.68 us
    ppermute x3, starting transfers between devices, per_device(): arrived[s] = lax.ppermute(terms[s], 'seq', swaps[s]) if s else terms[s]  4.67 us
    ppermute x3, starting transfers between devices, per_device(): states[s] = lax.ppermute(outgoing[s], 'seq', swaps[s])  3.55 us
    ppermute x3, starting transfers between devices, per_device(): held[m | d] = lax.ppermute(sent, 'tensor', flips[d])  2.14 us
    ppermute x3, waiting for transfers between devices, per_device(): arrived[s] = lax.ppermute(terms[s], 'seq', swaps[s]) if s else terms[s]  2.13 us
    ppermute x3, waiting for transfers between devices, per_device(): states[s] = lax.ppermute(outgoing[s], 'seq', swaps[s])  2.1 us
  transfers between devices with their start and end apart: 13, of which 8 were waited for; matrix products, arithmetic and copies ran while one was open for 0% of the time, Pallas kernels for 24%

profile of v4, /device:TPU:0, one launch (start us, length us, event | category | flops | bytes accessed | tf_op | source)
XLA Modules:
  0.0 58.5 jit_solution(11879838808346782116)
XLA Ops:
  0.0 0.7 %pad_maximum_fusion.given_ref = f32[3,8,128]{2,1,0:T(8,128)S(1)} fusion(f32[1,8,128]{2,1,0:T(8,128)} %bitcast.9, f32[2,8,128]{2,1,0:T(8,128)} %param.15), kind=kLoop, calls=%fused_computation.1 | loop fusion | flops 3072 | bytes 24576 | tf_op jit(solution)/shard_map/concatenate | solution.py:522
  0.7 1.5 %shard_map.118 = (bf16[8,2,128,128]{3,2,1,0:T(8,128)(2,1)S(1)}, bf16[8,2,128,128]{3,2,1,0:T(8,128)(2,1)S(1)}) custom-call(bf16[2,128,8,128]{3,2,1,0:T(8,128)(2,1)} %k_hbm.1, bf16[2,128,8,128]{3,2,1,0:T(8,128)(2,1)} %v_hbm.1), custom_call_target="tpu_custom_call" | custom-call | tf_op jit(solution)/shard_map/pallas_call | solution.py:451
  2.2 2.9 %shard_map.119 = (bf16[2,128,256]{2,1,0:T(8,128)(2,1)S(1)}, f32[2,256,256]{2,1,0:T(8,128)S(1)}, f32[6,8,128]{2,1,0:T(8,128)S(1)}) custom-call(f32[3,8,128]{2,1,0:T(8,128)S(1)} %pad_maximum_fusion.given_ref, bf16[8,2,128,128]{3,2,1,0:T(8,128)(2,1)S(1)} %get-tuple-element.26.k_heads, bf16[8,2,128,128]{3,2,1,0:T(8,128)(2,1)S(1)} %get-tuple-element.27.v_heads), custom_call_target="tpu_custom_call" | custom-call | flops 3000000000 | tf_op jit(solution)/shard_map/pallas_call | solution.py:451
  5.2 4.0 %collective-permute-start = (bf16[2,128,256]{2,1,0:T(8,128)(2,1)S(1)}, bf16[2,128,256]{2,1,0:T(8,128)(2,1)S(1)}, u32[]{:S(2)}, u32[]{:S(2)}) collective-permute-start(bf16[2,128,256]{2,1,0:T(8,128)(2,1)S(1)} %get-tuple-element.31), channel_id=1, source_target_pairs={{0,12},{4,8},{8,4},{12,0},{16,28},{20,24},{24,20},{28,16},{1,13},{... | collective-permute-start | bytes 393224 | tf_op jit(solution)/shard_map/ppermute | solution.py:539
  9.2 4.2 %shard_map.120 = (bf16[2,128,256]{2,1,0:T(8,128)(2,1)S(1)}, bf16[2,128,256]{2,1,0:T(8,128)(2,1)S(1)}, f32[4,256,256]{2,1,0:T(8,128)S(1)}) custom-call(bf16[8,2,128,128]{3,2,1,0:T(8,128)(2,1)S(1)} %get-tuple-element.26.k_heads, bf16[8,2,128,128]{3,2,1,0:T(8,128)(2,1)S(1)} %get-tuple-element.27.v_heads, f32[6,8,128]{2,1,0:T(8,128)S(1)} %get-tuple-element.29.row_ref), custom_call_target="tpu_custom_call" | custom-call | flops 4000000000 | tf_op jit(solution)/shard_map/pallas_call | solution.py:451
  13.4 0.0 copy-start.5
  13.4 0.6 %collective-permute-start.1 = (bf16[2,128,256]{2,1,0:T(8,128)(2,1)S(1)}, bf16[2,128,256]{2,1,0:T(8,128)(2,1)S(1)}, u32[]{:S(2)}, u32[]{:S(2)}) collective-permute-start(bf16[2,128,256]{2,1,0:T(8,128)(2,1)S(1)} %get-tuple-element.34), channel_id=1, source_target_pairs={{0,4},{4,0},{8,12},{12,8},{16,20},{20,16},{24,28},{28,24},{1,5},{5... | collective-permute-start | bytes 393224 | tf_op jit(solution)/shard_map/ppermute | solution.py:539
  14.0 0.0 collective-permute-start.2
  14.1 0.0 collective-permute-done.refs_0_.refs_1_
  14.1 2.8 %shard_map.121 = (bf16[2,128,256]{2,1,0:T(8,128)(2,1)S(1)}, f32[2,256,256]{2,1,0:T(8,128)S(1)}) custom-call(bf16[8,2,128,128]{3,2,1,0:T(8,128)(2,1)S(1)} %get-tuple-element.26.k_heads, bf16[8,2,128,128]{3,2,1,0:T(8,128)(2,1)S(1)} %get-tuple-element.27.v_heads, f32[6,8,128]{2,1,0:T(8,128)S(1)} %get-tuple-element.29.row_ref, ...), custom_call_target="tpu_custom_call" | custom-call | flops 4000000000 | tf_op jit(solution)/shard_map/pallas_call | solution.py:451
  16.8 1.6 %collective-permute-done.1.refs_2_ = bf16[2,128,256]{2,1,0:T(8,128)(2,1)S(1)} collective-permute-done((bf16[2,128,256]{2,1,0:T(8,128)(2,1)S(1)}, bf16[2,128,256]{2,1,0:T(8,128)(2,1)S(1)}, u32[]{:S(2)}, u32[]{:S(2)}) %collective-permute-start.1) | collective-permute-done | bytes 131104 | tf_op jit(solution)/shard_map/ppermute | solution.py:539
  18.4 0.5 collective-permute-done.2.refs_3_
  19.0 0.6 shard_map.123
  19.5 4.7 %collective-permute-start.3 = (bf16[2,128,128]{2,1,0:T(8,128)(2,1)S(1)}, bf16[2,128,128]{2,1,0:T(8,128)(2,1)S(1)}, u32[]{:S(2)}, u32[]{:S(2)}) collective-permute-start(bf16[2,128,128]{2,1,0:T(8,128)(2,1)S(1)} %get-tuple-element.36.refs_3_), channel_id=1, source_target_pairs={{0,16},{4,20},{8,24},{12,28},{1,17},{5,21},{9,25},{13,29},{2,18},{... | collective-permute-start | bytes 196616 | tf_op jit(solution)/shard_map/ppermute | solution.py:581
  24.2 0.0 slice-start
  24.2 0.1 shard_map.122.q_heads
  24.4 0.0 copy-start
  24.4 0.0 copy-start.4
  24.4 0.0 copy-start.2
  24.4 1.6 %collective-permute-done.3.before_ref = bf16[2,128,128]{2,1,0:T(8,128)(2,1)S(1)} collective-permute-done((bf16[2,128,128]{2,1,0:T(8,128)(2,1)S(1)}, bf16[2,128,128]{2,1,0:T(8,128)(2,1)S(1)}, u32[]{:S(2)}, u32[]{:S(2)}) %collective-permute-start.3) | collective-permute-done | bytes 65568 | tf_op jit(solution)/shard_map/ppermute | solution.py:581
  26.0 0.3 shard_map.125
  26.3 1.6 %collective-permute-start.4 = (bf16[2,128,128]{2,1,0:T(8,128)(2,1)S(1)}, bf16[2,128,128]{2,1,0:T(8,128)(2,1)S(1)}, u32[]{:S(2)}, u32[]{:S(2)}) collective-permute-start(bf16[2,128,128]{2,1,0:T(8,128)(2,1)S(1)} %get-tuple-element.40), channel_id=1, source_target_pairs={{0,4},{4,0},{8,12},{12,8},{16,20},{20,16},{24,28},{28,24},{1,5},{5... | collective-permute-start | bytes 196616 | tf_op jit(solution)/shard_map/ppermute | solution.py:591
  27.9 0.3 collective-permute-start.5
  28.2 1.6 %collective-permute-start.6 = (bf16[2,128,128]{2,1,0:T(8,128)(2,1)S(1)}, bf16[2,128,128]{2,1,0:T(8,128)(2,1)S(1)}, u32[]{:S(2)}, u32[]{:S(2)}) collective-permute-start(bf16[2,128,128]{2,1,0:T(8,128)(2,1)S(1)} %get-tuple-element.42), channel_id=1, source_target_pairs={{0,12},{4,8},{8,4},{12,0},{16,28},{20,24},{24,20},{28,16},{1,13},{... | collective-permute-start | bytes 196616 | tf_op jit(solution)/shard_map/ppermute | solution.py:591
  29.9 1.4 %shard_map.124.mixed_ref = f32[8,128,256]{2,1,0:T(8,128)S(1)} custom-call(bf16[8,128,128]{2,1,0:T(8,128)(2,1)S(1)} %shard_map.122.q_heads, bf16[8,2,128,128]{3,2,1,0:T(8,128)(2,1)S(1)} %get-tuple-element.26.k_heads, f32[6,8,128]{2,1,0:T(8,128)S(1)} %get-tuple-element.29.row_ref, f32[2,256,256]{2,1,0:T(8,128)S(1)} %get-tuple-element.28.refs_0_, ...), custom_call_target="tpu_custom_call" | custom-call | flops 3000000000 | tf_op jit(solution)/shard_map/pallas_call | solution.py:451
  31.3 0.0 collective-permute-done.4.refs_1_
  31.3 0.9 %collective-permute-done.5.refs_2_ = bf16[2,128,128]{2,1,0:T(8,128)(2,1)S(1)} collective-permute-done((bf16[2,128,128]{2,1,0:T(8,128)(2,1)S(1)}, bf16[2,128,128]{2,1,0:T(8,128)(2,1)S(1)}, u32[]{:S(2)}, u32[]{:S(2)}) %collective-permute-start.5) | collective-permute-done | bytes 65568 | tf_op jit(solution)/shard_map/ppermute | solution.py:591
  32.2 1.2 %collective-permute-done.6.refs_3_ = bf16[2,128,128]{2,1,0:T(8,128)(2,1)S(1)} collective-permute-done((bf16[2,128,128]{2,1,0:T(8,128)(2,1)S(1)}, bf16[2,128,128]{2,1,0:T(8,128)(2,1)S(1)}, u32[]{:S(2)}, u32[]{:S(2)}) %collective-permute-start.6) | collective-permute-done | bytes 65568 | tf_op jit(solution)/shard_map/ppermute | solution.py:591
  33.4 0.4 shard_map.126.after_ref.refs_0_
  33.8 0.0 slice-start.3
  33.8 1.6 %collective-permute-start.8 = (bf16[8,128,128]{2,1,0:T(8,128)(2,1)S(1)}, bf16[8,128,128]{2,1,0:T(8,128)(2,1)S(1)}, u32[]{:S(2)}, u32[]{:S(2)}) collective-permute-start(bf16[8,128,128]{2,1,0:T(8,128)(2,1)S(1)} %shard_map.126.after_ref.refs_0_), channel_id=1, source_target_pairs={{0,2},{1,3},{2,0},{3,1},{4,6},{5,7},{6,4},{7,5},{8,10},{9,11},{10,... | collective-permute-start | bytes 786440 | tf_op jit(solution)/shard_map/ppermute | solution.py:623
  35.4 0.0 collective-permute-start.7
  35.4 5.0 %shard_map.127.after_ref.down_ref = bf16[32,2048,128]{2,1,0:T(8,128)(2,1)S(1)} custom-call(s32[16,16]{1,0:T(8,128)S(1)} %copy-done.2, bf16[16,16,128,128]{3,2,1,0:T(8,128)(2,1)S(1)} %bitcast.4, bf16[8,128,128]{2,1,0:T(8,128)(2,1)S(1)} %shard_map.126.after_ref.refs_0_), custom_call_target="tpu_custom_call" | custom-call | flops 3000000000 | tf_op jit(solution)/shard_map/pallas_call | solution.py:451
  40.5 0.0 copy-start.1
  40.5 0.0 copy-start.3
  40.5 0.0 collective-permute-done.8.given_ref.refs_2_
  40.5 0.6 collective-permute-start.9
  41.1 0.0 collective-permute-done.7.refs_1_
  41.1 1.2 %collective-permute-done.9.refs_3_ = bf16[8,128,128]{2,1,0:T(8,128)(2,1)S(1)} collective-permute-done((bf16[8,128,128]{2,1,0:T(8,128)(2,1)S(1)}, bf16[8,128,128]{2,1,0:T(8,128)(2,1)S(1)}, u32[]{:S(2)}, u32[]{:S(2)}) %collective-permute-start.9) | collective-permute-done | bytes 262176 | tf_op jit(solution)/shard_map/ppermute | solution.py:623
  42.3 5.0 %shard_map.129 = (bf16[128,2048]{1,0:T(8,128)(2,1)S(1)}, bf16[8,128,128]{2,1,0:T(8,128)(2,1)S(1)}, bf16[8,128,128]{2,1,0:T(8,128)(2,1)S(1)}, bf16[8,128,128]{2,1,0:T(8,128)(2,1)S(1)}) custom-call(f32[32,128]{1,0:T(8,128)S(1)} %bitcast.7, s32[16,16]{1,0:T(8,128)S(1)} %copy-done.3, bf16[16,16,128,128]{3,2,1,0:T(8,128)(2,1)S(1)} %bitcast.6, ...), custom_call_target="tpu_custom_call" | custom-call | tf_op jit(solution)/shard_map/pallas_call | solution.py:451
  47.3 0.4 collective-permute-start.10
  47.7 0.1 collective-permute-start.11
  47.9 1.0 %collective-permute-done.10 = bf16[8,128,128]{2,1,0:T(8,128)(2,1)S(1)} collective-permute-done((bf16[8,128,128]{2,1,0:T(8,128)(2,1)S(1)}, bf16[8,128,128]{2,1,0:T(8,128)(2,1)S(1)}, u32[]{:S(2)}, u32[]{:S(2)}) %collective-permute-start.10) | collective-permute-done | bytes 262176 | tf_op jit(solution)/shard_map/ppermute | solution.py:640
  48.9 0.1 add_convert_fusion.after_ref
  49.0 1.2 %collective-permute-start.12 = (bf16[8,128,128]{2,1,0:T(8,128)(2,1)S(1)}, bf16[8,128,128]{2,1,0:T(8,128)(2,1)S(1)}, u32[]{:S(2)}, u32[]{:S(2)}) collective-permute-start(bf16[8,128,128]{2,1,0:T(8,128)(2,1)S(1)} %add_convert_fusion.after_ref), channel_id=1, source_target_pairs={{0,2},{1,3},{2,0},{3,1},{4,6},{5,7},{6,4},{7,5},{8,10},{9,11},{10,... | collective-permute-start | bytes 786440 | tf_op jit(solution)/shard_map/ppermute | solution.py:647
  50.2 0.7 %shard_map.130.refs_1_ = bf16[8,128,128]{2,1,0:T(8,128)(2,1)S(1)} custom-call(bf16[32,2048,128]{2,1,0:T(8,128)(2,1)S(1)} %shard_map.127.after_ref.down_ref, bf16[128,2048]{1,0:T(8,128)(2,1)S(1)} %get-tuple-element.43.act_ref, bf16[8,128,128]{2,1,0:T(8,128)(2,1)S(1)} %add_convert_fusion.after_ref), custom_call_target="tpu_custom_call" | custom-call | flops 1000000000 | tf_op jit(solution)/shard_map/pallas_call | solution.py:451
  50.9 6.7 %collective-permute-done.12.refs_3_ = bf16[8,128,128]{2,1,0:T(8,128)(2,1)S(1)} collective-permute-done((bf16[8,128,128]{2,1,0:T(8,128)(2,1)S(1)}, bf16[8,128,128]{2,1,0:T(8,128)(2,1)S(1)}, u32[]{:S(2)}, u32[]{:S(2)}) %collective-permute-start.12) | collective-permute-done | bytes 262176 | tf_op jit(solution)/shard_map/ppermute | solution.py:647
  57.6 0.9 %shard_map.131 = bf16[128,1024]{1,0:T(8,128)(2,1)} custom-call(bf16[8,128,128]{2,1,0:T(8,128)(2,1)S(1)} %shard_map.126.after_ref.refs_0_, bf16[8,128,128]{2,1,0:T(8,128)(2,1)S(1)} %shard_map.130.refs_1_, bf16[8,128,128]{2,1,0:T(8,128)(2,1)S(1)} %collective-permute-done.11.refs_2_, bf16[8,128,128]{2,1,0:T(8,128)(2,1)S(1)} %collective-permute-done.12.refs_3_), custom_call_target="tpu_custom_call" | custom-call | tf_op jit(solution)/shard_map/pallas_call | solution.py:451
  (16 shorter events, 0.0 us)
Async XLA Ops:
  5.2 8.9 %collective-permute-start = (bf16[2,128,256]{2,1,0:T(8,128)(2,1)S(1)}, bf16[2,128,256]{2,1,0:T(8,128)(2,1)S(1)}, u32[]{:S(2)}, u32[]{:S(2)}) collective-permute-start(bf16[2,128,256]{2,1,0:T(8,128)(2,1)S(1)} %get-tuple-element.31), channel_id=1, source_target_pairs={{0,12},{4,8},{8,4},{12,0},{16,28},{20,24},{24,20},{28,16},{1,13},{... | collective-permute-start | bytes 393224 | tf_op jit(solution)/shard_map/ppermute | solution.py:539
  13.4 10.8 %copy-start.5 = (bf16[128,8,128]{2,1,0:T(8,128)(2,1)S(1)}, bf16[128,8,128]{2,1,0:T(8,128)(2,1)}, u32[]{:S(2)}) copy-start(bf16[128,8,128]{2,1,0:T(8,128)(2,1)} %q_ref.1) | copy-start | bytes 786436
  13.4 5.0 %collective-permute-start.1 = (bf16[2,128,256]{2,1,0:T(8,128)(2,1)S(1)}, bf16[2,128,256]{2,1,0:T(8,128)(2,1)S(1)}, u32[]{:S(2)}, u32[]{:S(2)}) collective-permute-start(bf16[2,128,256]{2,1,0:T(8,128)(2,1)S(1)} %get-tuple-element.34), channel_id=1, source_target_pairs={{0,4},{4,0},{8,12},{12,8},{16,20},{20,16},{24,28},{28,24},{1,5},{5... | collective-permute-start | bytes 393224 | tf_op jit(solution)/shard_map/ppermute | solution.py:539
  14.0 5.0 %collective-permute-start.2 = (bf16[2,128,256]{2,1,0:T(8,128)(2,1)S(1)}, bf16[2,128,256]{2,1,0:T(8,128)(2,1)S(1)}, u32[]{:S(2)}, u32[]{:S(2)}) collective-permute-start(bf16[2,128,256]{2,1,0:T(8,128)(2,1)S(1)} %get-tuple-element.35), channel_id=1, source_target_pairs={{0,8},{4,12},{8,0},{12,4},{16,24},{20,28},{24,16},{28,20},{1,9},{5... | collective-permute-start | bytes 393224 | tf_op jit(solution)/shard_map/ppermute | solution.py:539
  19.5 6.5 %collective-permute-start.3 = (bf16[2,128,128]{2,1,0:T(8,128)(2,1)S(1)}, bf16[2,128,128]{2,1,0:T(8,128)(2,1)S(1)}, u32[]{:S(2)}, u32[]{:S(2)}) collective-permute-start(bf16[2,128,128]{2,1,0:T(8,128)(2,1)S(1)} %get-tuple-element.36.refs_3_), channel_id=1, source_target_pairs={{0,16},{4,20},{8,24},{12,28},{1,17},{5,21},{9,25},{13,29},{2,18},{... | collective-permute-start | bytes 196616 | tf_op jit(solution)/shard_map/ppermute | solution.py:581
  24.2 11.2 %slice-start = ((s8[8388608]{0:T(1024)(128)(4,1)}), s8[4194304]{0:T(1024)(128)(4,1)S(1)}, s32[]{:S(2)}) async-start(s8[8388608]{0:T(1024)(128)(4,1)} %bitcast.3), calls=%async_computation | async-start | bytes 8388608
  24.4 9.0 %copy-start = (bf16[128,1024]{1,0:T(8,128)(2,1)S(1)}, bf16[128,1024]{1,0:T(8,128)(2,1)}, u32[]{:S(2)}) copy-start(bf16[128,1024]{1,0:T(8,128)(2,1)} %residual_ref.1) | copy-start | bytes 786436
  24.4 9.0 %copy-start.4 = (f32[128]{0:T(128)S(1)}, f32[128]{0:T(128)}, u32[]{:S(2)}) copy-start(f32[128]{0:T(128)} %param.17) | copy-start | bytes 1540
  24.4 11.0 %copy-start.2 = (s32[16,16]{1,0:T(8,128)S(1)}, s32[16,16]{1,0:T(8,128)}, u32[]{:S(2)}) copy-start(s32[16,16]{1,0:T(8,128)} %at_ref.1) | copy-start | bytes 3076
  26.3 5.0 %collective-permute-start.4 = (bf16[2,128,128]{2,1,0:T(8,128)(2,1)S(1)}, bf16[2,128,128]{2,1,0:T(8,128)(2,1)S(1)}, u32[]{:S(2)}, u32[]{:S(2)}) collective-permute-start(bf16[2,128,128]{2,1,0:T(8,128)(2,1)S(1)} %get-tuple-element.40), channel_id=1, source_target_pairs={{0,4},{4,0},{8,12},{12,8},{16,20},{20,16},{24,28},{28,24},{1,5},{5... | collective-permute-start | bytes 196616 | tf_op jit(solution)/shard_map/ppermute | solution.py:591
  27.9 4.3 %collective-permute-start.5 = (bf16[2,128,128]{2,1,0:T(8,128)(2,1)S(1)}, bf16[2,128,128]{2,1,0:T(8,128)(2,1)S(1)}, u32[]{:S(2)}, u32[]{:S(2)}) collective-permute-start(bf16[2,128,128]{2,1,0:T(8,128)(2,1)S(1)} %get-tuple-element.41), channel_id=1, source_target_pairs={{0,8},{4,12},{8,0},{12,4},{16,24},{20,28},{24,16},{28,20},{1,9},{5... | collective-permute-start | bytes 196616 | tf_op jit(solution)/shard_map/ppermute | solution.py:591
  28.2 7.2 %slice-start.1 = ((s8[8388608]{0:T(1024)(128)(4,1)}), s8[4194304]{0:T(1024)(128)(4,1)S(1)}, s32[]{:S(2)}) async-start(s8[8388608]{0:T(1024)(128)(4,1)} %bitcast.3), calls=%async_computation.1 | async-start | bytes 8388608
  28.2 5.2 %collective-permute-start.6 = (bf16[2,128,128]{2,1,0:T(8,128)(2,1)S(1)}, bf16[2,128,128]{2,1,0:T(8,128)(2,1)S(1)}, u32[]{:S(2)}, u32[]{:S(2)}) collective-permute-start(bf16[2,128,128]{2,1,0:T(8,128)(2,1)S(1)} %get-tuple-element.42), channel_id=1, source_target_pairs={{0,12},{4,8},{8,4},{12,0},{16,28},{20,24},{24,20},{28,16},{1,13},{... | collective-permute-start | bytes 196616 | tf_op jit(solution)/shard_map/ppermute | solution.py:591
  33.4 8.9 %slice-start.2 = ((s8[8388608]{0:T(1024)(128)(4,1)}), s8[4194304]{0:T(1024)(128)(4,1)S(1)}, s32[]{:S(2)}) async-start(s8[8388608]{0:T(1024)(128)(4,1)} %bitcast.5), calls=%async_computation.2 | async-start | bytes 8388608
  33.8 8.4 %slice-start.3 = ((s8[8388608]{0:T(1024)(128)(4,1)}), s8[4194304]{0:T(1024)(128)(4,1)S(1)}, s32[]{:S(2)}) async-start(s8[8388608]{0:T(1024)(128)(4,1)} %bitcast.5), calls=%async_computation.3 | async-start | bytes 8388608
  33.8 6.7 %collective-permute-start.8 = (bf16[8,128,128]{2,1,0:T(8,128)(2,1)S(1)}, bf16[8,128,128]{2,1,0:T(8,128)(2,1)S(1)}, u32[]{:S(2)}, u32[]{:S(2)}) collective-permute-start(bf16[8,128,128]{2,1,0:T(8,128)(2,1)S(1)} %shard_map.126.after_ref.refs_0_), channel_id=1, source_target_pairs={{0,2},{1,3},{2,0},{3,1},{4,6},{5,7},{6,4},{7,5},{8,10},{9,11},{10,... | collective-permute-start | bytes 786440 | tf_op jit(solution)/shard_map/ppermute | solution.py:623
  35.4 5.7 %collective-permute-start.7 = (bf16[8,128,128]{2,1,0:T(8,128)(2,1)S(1)}, bf16[8,128,128]{2,1,0:T(8,128)(2,1)S(1)}, u32[]{:S(2)}, u32[]{:S(2)}) collective-permute-start(bf16[8,128,128]{2,1,0:T(8,128)(2,1)S(1)} %shard_map.126.after_ref.refs_0_), channel_id=1, source_target_pairs={{0,1},{1,0},{2,3},{3,2},{4,5},{5,4},{6,7},{7,6},{8,9},{9,8},{10,11... | collective-permute-start | bytes 786440 | tf_op jit(solution)/shard_map/ppermute | solution.py:623
  40.5 1.8 %copy-start.1 = (f32[4096]{0:T(1024)S(1)}, f32[4096]{0:T(1024)}, u32[]{:S(2)}) copy-start(f32[4096]{0:T(1024)} %param.19) | copy-start | bytes 49156
  40.5 1.8 %copy-start.3 = (s32[16,16]{1,0:T(8,128)S(1)}, s32[16,16]{1,0:T(8,128)}, u32[]{:S(2)}) copy-start(s32[16,16]{1,0:T(8,128)} %up_at.1) | copy-start | bytes 3076
  40.5 1.7 %collective-permute-start.9 = (bf16[8,128,128]{2,1,0:T(8,128)(2,1)S(1)}, bf16[8,128,128]{2,1,0:T(8,128)(2,1)S(1)}, u32[]{:S(2)}, u32[]{:S(2)}) collective-permute-start(bf16[8,128,128]{2,1,0:T(8,128)(2,1)S(1)} %shard_map.128), channel_id=1, source_target_pairs={{0,1},{1,0},{2,3},{3,2},{4,5},{5,4},{6,7},{7,6},{8,9},{9,8},{10,11... | collective-permute-start | bytes 786440 | tf_op jit(solution)/shard_map/ppermute | solution.py:623
  47.3 1.6 %collective-permute-start.10 = (bf16[8,128,128]{2,1,0:T(8,128)(2,1)S(1)}, bf16[8,128,128]{2,1,0:T(8,128)(2,1)S(1)}, u32[]{:S(2)}, u32[]{:S(2)}) collective-permute-start(bf16[8,128,128]{2,1,0:T(8,128)(2,1)S(1)} %get-tuple-element.45), channel_id=1, source_target_pairs={{0,1},{1,0},{2,3},{3,2},{4,5},{5,4},{6,7},{7,6},{8,9},{9,8},{10,11... | collective-permute-start | bytes 786440 | tf_op jit(solution)/shard_map/ppermute | solution.py:640
  47.7 3.2 %collective-permute-start.11 = (bf16[8,128,128]{2,1,0:T(8,128)(2,1)S(1)}, bf16[8,128,128]{2,1,0:T(8,128)(2,1)S(1)}, u32[]{:S(2)}, u32[]{:S(2)}) collective-permute-start(bf16[8,128,128]{2,1,0:T(8,128)(2,1)S(1)} %get-tuple-element.46), channel_id=1, source_target_pairs={{0,1},{1,0},{2,3},{3,2},{4,5},{5,4},{6,7},{7,6},{8,9},{9,8},{10,11... | collective-permute-start | bytes 786440 | tf_op jit(solution)/shard_map/ppermute | solution.py:647
  49.0 8.7 %collective-permute-start.12 = (bf16[8,128,128]{2,1,0:T(8,128)(2,1)S(1)}, bf16[8,128,128]{2,1,0:T(8,128)(2,1)S(1)}, u32[]{:S(2)}, u32[]{:S(2)}) collective-permute-start(bf16[8,128,128]{2,1,0:T(8,128)(2,1)S(1)} %add_convert_fusion.after_ref), channel_id=1, source_target_pairs={{0,2},{1,3},{2,0},{3,1},{4,6},{5,7},{6,4},{7,5},{8,10},{9,11},{10,... | collective-permute-start | bytes 786440 | tf_op jit(solution)/shard_map/ppermute | solution.py:647

commit v5 on v4

--- a/solution.py
+++ b/solution.py
@@ -49,8 +49,8 @@
     return jnp.broadcast_to(row, (n, n)).T
 
 
-def head_rows(ref, h, stride):
-    return ref[pl.ds(h, ref.shape[0] // stride, stride=stride), :]
+def head_rows(ref, h, heads):
+    return ref[pl.ds(h, ref.shape[0] // heads - 1, stride=heads), :]
 
 
 def stacked(first, second):
@@ -96,7 +96,7 @@
     for n, (source, target) in enumerate(((k_ref, k_heads), (v_ref, v_heads))):
         copies[n].wait()
         for j in range(2):
-            wide[n, j] = source[j].astype(F32).reshape(tokens * heads, width)
+            wide[n, j, : tokens * heads] = source[j].astype(F32).reshape(tokens * heads, width)
         for h in range(heads):
             rows = stacked(*(head_rows(wide.at[n, j], h, heads) for j in range(2)))
             for i in range(2):
@@ -257,7 +257,7 @@
 def queries_kernel(q_ref, *refs):
     out_ref, q_all = refs[-2:]
     tokens, heads, width = q_ref.shape
-    q_all[...] = q_ref[...].astype(F32).reshape(tokens * heads, width)
+    q_all[: tokens * heads] = q_ref[...].astype(F32).reshape(tokens * heads, width)
     for h in range(heads):
         out_ref[h] = head_rows(q_all, h, heads).astype(BF16)
 
@@ -510,7 +510,7 @@
                 [
                     pltpu.VMEM(keys.shape, BF16),
                     pltpu.VMEM(values.shape, BF16),
-                    pltpu.VMEM((2, 2, tokens * heads, width), F32),
+                    pltpu.VMEM((2, 2, (tokens + 1) * heads, width), F32),
                     pltpu.SemaphoreType.DMA((2,)),
                 ],
                 limit=FIRST_LIMIT,
@@ -545,7 +545,7 @@
         jax.ShapeDtypeStruct((heads, tokens, width), BF16),
         [VMEM] + [ANY] * len(orders),
         (queries, *solved),
-        [pltpu.VMEM((tokens * heads, width), F32)],
+        [pltpu.VMEM(((tokens + 1) * heads, width), F32)],
         flops=3_000_000_000,
     )
 

time: 58.8 us -> 58.8 us (level)
  no operation moved by 1% of the time
where the time goes in v5:
time: 58.8 us; the launch traced here: 58.5 us
  Pallas kernels  25.8 us (44%)
  starting transfers between devices  16.8 us (29%)
  waiting for transfers between devices  14.8 us (25%)
  other arithmetic  0.79 us (1%)
    pallas_call x14, Pallas kernels, local_call(): pl.pallas_call(kernel, out_shape=out_shape, in_specs=ins, out_specs=jax.t...  25.8 us
    ppermute x2, waiting for transfers between devices, per_device(): lax.ppermute(crossing[m], 'tensor', flips[m])  6.7 us
    ppermute x1, starting transfers between devices, per_device(): before = lax.ppermute(end, 'seq', [(k, k + slots) for k in range(slots)])  4.68 us
    ppermute x3, starting transfers between devices, per_device(): arrived[s] = lax.ppermute(terms[s], 'seq', swaps[s]) if s else terms[s]  4.67 us
    ppermute x3, starting transfers between devices, per_device(): states[s] = lax.ppermute(outgoing[s], 'seq', swaps[s])  3.55 us
    ppermute x3, starting transfers between devices, per_device(): held[m | d] = lax.ppermute(sent, 'tensor', flips[d])  2.14 us
    ppermute x3, waiting for transfers between devices, per_device(): arrived[s] = lax.ppermute(terms[s], 'seq', swaps[s]) if s else terms[s]  2.13 us
    ppermute x3, waiting for transfers between devices, per_device(): states[s] = lax.ppermute(outgoing[s], 'seq', swaps[s])  2.1 us
  transfers between devices with their start and end apart: 13, of which 8 were waited for; matrix products, arithmetic and copies ran while one was open for 0% of the time, Pallas kernels for 24%

profile of v5, /device:TPU:0, one launch (start us, length us, event | category | flops | bytes accessed | tf_op | source)
XLA Modules:
  0.0 58.5 jit_solution(13236648106780196002)
XLA Ops:
  0.0 0.7 %pad_maximum_fusion.given_ref = f32[3,8,128]{2,1,0:T(8,128)S(1)} fusion(f32[1,8,128]{2,1,0:T(8,128)} %bitcast.9, f32[2,8,128]{2,1,0:T(8,128)} %param.15), kind=kLoop, calls=%fused_computation.1 | loop fusion | flops 3072 | bytes 24576 | tf_op jit(solution)/shard_map/concatenate | solution.py:522
  0.7 1.5 %shard_map.118 = (bf16[8,2,128,128]{3,2,1,0:T(8,128)(2,1)S(1)}, bf16[8,2,128,128]{3,2,1,0:T(8,128)(2,1)S(1)}) custom-call(bf16[2,128,8,128]{3,2,1,0:T(8,128)(2,1)} %k_hbm.1, bf16[2,128,8,128]{3,2,1,0:T(8,128)(2,1)} %v_hbm.1), custom_call_target="tpu_custom_call" | custom-call | tf_op jit(solution)/shard_map/pallas_call | solution.py:451
  2.2 2.9 %shard_map.119 = (bf16[2,128,256]{2,1,0:T(8,128)(2,1)S(1)}, f32[2,256,256]{2,1,0:T(8,128)S(1)}, f32[6,8,128]{2,1,0:T(8,128)S(1)}) custom-call(f32[3,8,128]{2,1,0:T(8,128)S(1)} %pad_maximum_fusion.given_ref, bf16[8,2,128,128]{3,2,1,0:T(8,128)(2,1)S(1)} %get-tuple-element.26.k_heads, bf16[8,2,128,128]{3,2,1,0:T(8,128)(2,1)S(1)} %get-tuple-element.27.v_heads), custom_call_target="tpu_custom_call" | custom-call | flops 3000000000 | tf_op jit(solution)/shard_map/pallas_call | solution.py:451
  5.2 4.0 %collective-permute-start = (bf16[2,128,256]{2,1,0:T(8,128)(2,1)S(1)}, bf16[2,128,256]{2,1,0:T(8,128)(2,1)S(1)}, u32[]{:S(2)}, u32[]{:S(2)}) collective-permute-start(bf16[2,128,256]{2,1,0:T(8,128)(2,1)S(1)} %get-tuple-element.31), channel_id=1, source_target_pairs={{0,12},{4,8},{8,4},{12,0},{16,28},{20,24},{24,20},{28,16},{1,13},{... | collective-permute-start | bytes 393224 | tf_op jit(solution)/shard_map/ppermute | solution.py:539
  9.2 4.2 %shard_map.120 = (bf16[2,128,256]{2,1,0:T(8,128)(2,1)S(1)}, bf16[2,128,256]{2,1,0:T(8,128)(2,1)S(1)}, f32[4,256,256]{2,1,0:T(8,128)S(1)}) custom-call(bf16[8,2,128,128]{3,2,1,0:T(8,128)(2,1)S(1)} %get-tuple-element.26.k_heads, bf16[8,2,128,128]{3,2,1,0:T(8,128)(2,1)S(1)} %get-tuple-element.27.v_heads, f32[6,8,128]{2,1,0:T(8,128)S(1)} %get-tuple-element.29.row_ref), custom_call_target="tpu_custom_call" | custom-call | flops 4000000000 | tf_op jit(solution)/shard_map/pallas_call | solution.py:451
  13.4 0.0 copy-start.5
  13.4 0.6 %collective-permute-start.1 = (bf16[2,128,256]{2,1,0:T(8,128)(2,1)S(1)}, bf16[2,128,256]{2,1,0:T(8,128)(2,1)S(1)}, u32[]{:S(2)}, u32[]{:S(2)}) collective-permute-start(bf16[2,128,256]{2,1,0:T(8,128)(2,1)S(1)} %get-tuple-element.34), channel_id=1, source_target_pairs={{0,4},{4,0},{8,12},{12,8},{16,20},{20,16},{24,28},{28,24},{1,5},{5... | collective-permute-start | bytes 393224 | tf_op jit(solution)/shard_map/ppermute | solution.py:539
  14.0 0.0 collective-permute-start.2
  14.1 0.0 collective-permute-done.refs_0_.refs_1_
  14.1 2.8 %shard_map.121 = (bf16[2,128,256]{2,1,0:T(8,128)(2,1)S(1)}, f32[2,256,256]{2,1,0:T(8,128)S(1)}) custom-call(bf16[8,2,128,128]{3,2,1,0:T(8,128)(2,1)S(1)} %get-tuple-element.26.k_heads, bf16[8,2,128,128]{3,2,1,0:T(8,128)(2,1)S(1)} %get-tuple-element.27.v_heads, f32[6,8,128]{2,1,0:T(8,128)S(1)} %get-tuple-element.29.row_ref, ...), custom_call_target="tpu_custom_call" | custom-call | flops 4000000000 | tf_op jit(solution)/shard_map/pallas_call | solution.py:451
  16.8 1.6 %collective-permute-done.1.refs_2_ = bf16[2,128,256]{2,1,0:T(8,128)(2,1)S(1)} collective-permute-done((bf16[2,128,256]{2,1,0:T(8,128)(2,1)S(1)}, bf16[2,128,256]{2,1,0:T(8,128)(2,1)S(1)}, u32[]{:S(2)}, u32[]{:S(2)}) %collective-permute-start.1) | collective-permute-done | bytes 131104 | tf_op jit(solution)/shard_map/ppermute | solution.py:539
  18.4 0.5 collective-permute-done.2.refs_3_
  19.0 0.6 shard_map.123
  19.5 4.7 %collective-permute-start.3 = (bf16[2,128,128]{2,1,0:T(8,128)(2,1)S(1)}, bf16[2,128,128]{2,1,0:T(8,128)(2,1)S(1)}, u32[]{:S(2)}, u32[]{:S(2)}) collective-permute-start(bf16[2,128,128]{2,1,0:T(8,128)(2,1)S(1)} %get-tuple-element.36.refs_3_), channel_id=1, source_target_pairs={{0,16},{4,20},{8,24},{12,28},{1,17},{5,21},{9,25},{13,29},{2,18},{... | collective-permute-start | bytes 196616 | tf_op jit(solution)/shard_map/ppermute | solution.py:581
  24.2 0.0 slice-start
  24.2 0.1 shard_map.122.q_heads
  24.4 0.0 copy-start
  24.4 0.0 copy-start.4
  24.4 0.0 copy-start.2
  24.4 1.6 %collective-permute-done.3.before_ref = bf16[2,128,128]{2,1,0:T(8,128)(2,1)S(1)} collective-permute-done((bf16[2,128,128]{2,1,0:T(8,128)(2,1)S(1)}, bf16[2,128,128]{2,1,0:T(8,128)(2,1)S(1)}, u32[]{:S(2)}, u32[]{:S(2)}) %collective-permute-start.3) | collective-permute-done | bytes 65568 | tf_op jit(solution)/shard_map/ppermute | solution.py:581
  26.0 0.3 shard_map.125
  26.3 1.6 %collective-permute-start.4 = (bf16[2,128,128]{2,1,0:T(8,128)(2,1)S(1)}, bf16[2,128,128]{2,1,0:T(8,128)(2,1)S(1)}, u32[]{:S(2)}, u32[]{:S(2)}) collective-permute-start(bf16[2,128,128]{2,1,0:T(8,128)(2,1)S(1)} %get-tuple-element.40), channel_id=1, source_target_pairs={{0,4},{4,0},{8,12},{12,8},{16,20},{20,16},{24,28},{28,24},{1,5},{5... | collective-permute-start | bytes 196616 | tf_op jit(solution)/shard_map/ppermute | solution.py:591
  27.9 0.3 collective-permute-start.5
  28.2 1.6 %collective-permute-start.6 = (bf16[2,128,128]{2,1,0:T(8,128)(2,1)S(1)}, bf16[2,128,128]{2,1,0:T(8,128)(2,1)S(1)}, u32[]{:S(2)}, u32[]{:S(2)}) collective-permute-start(bf16[2,128,128]{2,1,0:T(8,128)(2,1)S(1)} %get-tuple-element.42), channel_id=1, source_target_pairs={{0,12},{4,8},{8,4},{12,0},{16,28},{20,24},{24,20},{28,16},{1,13},{... | collective-permute-start | bytes 196616 | tf_op jit(solution)/shard_map/ppermute | solution.py:591
  29.9 1.4 %shard_map.124.mixed_ref = f32[8,128,256]{2,1,0:T(8,128)S(1)} custom-call(bf16[8,128,128]{2,1,0:T(8,128)(2,1)S(1)} %shard_map.122.q_heads, bf16[8,2,128,128]{3,2,1,0:T(8,128)(2,1)S(1)} %get-tuple-element.26.k_heads, f32[6,8,128]{2,1,0:T(8,128)S(1)} %get-tuple-element.29.row_ref, f32[2,256,256]{2,1,0:T(8,128)S(1)} %get-tuple-element.28.refs_0_, ...), custom_call_target="tpu_custom_call" | custom-call | flops 3000000000 | tf_op jit(solution)/shard_map/pallas_call | solution.py:451
  31.3 0.0 collective-permute-done.4.refs_1_
  31.3 0.9 %collective-permute-done.5.refs_2_ = bf16[2,128,128]{2,1,0:T(8,128)(2,1)S(1)} collective-permute-done((bf16[2,128,128]{2,1,0:T(8,128)(2,1)S(1)}, bf16[2,128,128]{2,1,0:T(8,128)(2,1)S(1)}, u32[]{:S(2)}, u32[]{:S(2)}) %collective-permute-start.5) | collective-permute-done | bytes 65568 | tf_op jit(solution)/shard_map/ppermute | solution.py:591
  32.2 1.2 %collective-permute-done.6.refs_3_ = bf16[2,128,128]{2,1,0:T(8,128)(2,1)S(1)} collective-permute-done((bf16[2,128,128]{2,1,0:T(8,128)(2,1)S(1)}, bf16[2,128,128]{2,1,0:T(8,128)(2,1)S(1)}, u32[]{:S(2)}, u32[]{:S(2)}) %collective-permute-start.6) | collective-permute-done | bytes 65568 | tf_op jit(solution)/shard_map/ppermute | solution.py:591
  33.4 0.4 shard_map.126.after_ref.refs_0_
  33.8 0.0 slice-start.3
  33.8 1.6 %collective-permute-start.8 = (bf16[8,128,128]{2,1,0:T(8,128)(2,1)S(1)}, bf16[8,128,128]{2,1,0:T(8,128)(2,1)S(1)}, u32[]{:S(2)}, u32[]{:S(2)}) collective-permute-start(bf16[8,128,128]{2,1,0:T(8,128)(2,1)S(1)} %shard_map.126.after_ref.refs_0_), channel_id=1, source_target_pairs={{0,2},{1,3},{2,0},{3,1},{4,6},{5,7},{6,4},{7,5},{8,10},{9,11},{10,... | collective-permute-start | bytes 786440 | tf_op jit(solution)/shard_map/ppermute | solution.py:623
  35.4 0.0 collective-permute-start.7
  35.4 5.0 %shard_map.127.after_ref.down_ref = bf16[32,2048,128]{2,1,0:T(8,128)(2,1)S(1)} custom-call(s32[16,16]{1,0:T(8,128)S(1)} %copy-done.2, bf16[16,16,128,128]{3,2,1,0:T(8,128)(2,1)S(1)} %bitcast.4, bf16[8,128,128]{2,1,0:T(8,128)(2,1)S(1)} %shard_map.126.after_ref.refs_0_), custom_call_target="tpu_custom_call" | custom-call | flops 3000000000 | tf_op jit(solution)/shard_map/pallas_call | solution.py:451
  40.5 0.0 copy-start.1
  40.5 0.0 copy-start.3
  40.5 0.0 collective-permute-done.8.given_ref.refs_2_
  40.5 0.6 collective-permute-start.9
  41.1 0.0 collective-permute-done.7.refs_1_
  41.1 1.2 %collective-permute-done.9.refs_3_ = bf16[8,128,128]{2,1,0:T(8,128)(2,1)S(1)} collective-permute-done((bf16[8,128,128]{2,1,0:T(8,128)(2,1)S(1)}, bf16[8,128,128]{2,1,0:T(8,128)(2,1)S(1)}, u32[]{:S(2)}, u32[]{:S(2)}) %collective-permute-start.9) | collective-permute-done | bytes 262176 | tf_op jit(solution)/shard_map/ppermute | solution.py:623
  42.3 5.0 %shard_map.129 = (bf16[128,2048]{1,0:T(8,128)(2,1)S(1)}, bf16[8,128,128]{2,1,0:T(8,128)(2,1)S(1)}, bf16[8,128,128]{2,1,0:T(8,128)(2,1)S(1)}, bf16[8,128,128]{2,1,0:T(8,128)(2,1)S(1)}) custom-call(f32[32,128]{1,0:T(8,128)S(1)} %bitcast.7, s32[16,16]{1,0:T(8,128)S(1)} %copy-done.3, bf16[16,16,128,128]{3,2,1,0:T(8,128)(2,1)S(1)} %bitcast.6, ...), custom_call_target="tpu_custom_call" | custom-call | tf_op jit(solution)/shard_map/pallas_call | solution.py:451
  47.3 0.4 collective-permute-start.10
  47.7 0.1 collective-permute-start.11
  47.9 1.0 %collective-permute-done.10 = bf16[8,128,128]{2,1,0:T(8,128)(2,1)S(1)} collective-permute-done((bf16[8,128,128]{2,1,0:T(8,128)(2,1)S(1)}, bf16[8,128,128]{2,1,0:T(8,128)(2,1)S(1)}, u32[]{:S(2)}, u32[]{:S(2)}) %collective-permute-start.10) | collective-permute-done | bytes 262176 | tf_op jit(solution)/shard_map/ppermute | solution.py:640
  48.9 0.1 add_convert_fusion.after_ref
  49.0 1.2 %collective-permute-start.12 = (bf16[8,128,128]{2,1,0:T(8,128)(2,1)S(1)}, bf16[8,128,128]{2,1,0:T(8,128)(2,1)S(1)}, u32[]{:S(2)}, u32[]{:S(2)}) collective-permute-start(bf16[8,128,128]{2,1,0:T(8,128)(2,1)S(1)} %add_convert_fusion.after_ref), channel_id=1, source_target_pairs={{0,2},{1,3},{2,0},{3,1},{4,6},{5,7},{6,4},{7,5},{8,10},{9,11},{10,... | collective-permute-start | bytes 786440 | tf_op jit(solution)/shard_map/ppermute | solution.py:647
  50.2 0.7 %shard_map.130.refs_1_ = bf16[8,128,128]{2,1,0:T(8,128)(2,1)S(1)} custom-call(bf16[32,2048,128]{2,1,0:T(8,128)(2,1)S(1)} %shard_map.127.after_ref.down_ref, bf16[128,2048]{1,0:T(8,128)(2,1)S(1)} %get-tuple-element.43.act_ref, bf16[8,128,128]{2,1,0:T(8,128)(2,1)S(1)} %add_convert_fusion.after_ref), custom_call_target="tpu_custom_call" | custom-call | flops 1000000000 | tf_op jit(solution)/shard_map/pallas_call | solution.py:451
  50.9 6.7 %collective-permute-done.12.refs_3_ = bf16[8,128,128]{2,1,0:T(8,128)(2,1)S(1)} collective-permute-done((bf16[8,128,128]{2,1,0:T(8,128)(2,1)S(1)}, bf16[8,128,128]{2,1,0:T(8,128)(2,1)S(1)}, u32[]{:S(2)}, u32[]{:S(2)}) %collective-permute-start.12) | collective-permute-done | bytes 262176 | tf_op jit(solution)/shard_map/ppermute | solution.py:647
  57.6 0.9 %shard_map.131 = bf16[128,1024]{1,0:T(8,128)(2,1)} custom-call(bf16[8,128,128]{2,1,0:T(8,128)(2,1)S(1)} %shard_map.126.after_ref.refs_0_, bf16[8,128,128]{2,1,0:T(8,128)(2,1)S(1)} %shard_map.130.refs_1_, bf16[8,128,128]{2,1,0:T(8,128)(2,1)S(1)} %collective-permute-done.11.refs_2_, bf16[8,128,128]{2,1,0:T(8,128)(2,1)S(1)} %collective-permute-done.12.refs_3_), custom_call_target="tpu_custom_call" | custom-call | tf_op jit(solution)/shard_map/pallas_call | solution.py:451
  (16 shorter events, 0.0 us)
Async XLA Ops:
  5.2 8.9 %collective-permute-start = (bf16[2,128,256]{2,1,0:T(8,128)(2,1)S(1)}, bf16[2,128,256]{2,1,0:T(8,128)(2,1)S(1)}, u32[]{:S(2)}, u32[]{:S(2)}) collective-permute-start(bf16[2,128,256]{2,1,0:T(8,128)(2,1)S(1)} %get-tuple-element.31), channel_id=1, source_target_pairs={{0,12},{4,8},{8,4},{12,0},{16,28},{20,24},{24,20},{28,16},{1,13},{... | collective-permute-start | bytes 393224 | tf_op jit(solution)/shard_map/ppermute | solution.py:539
  13.4 10.8 %copy-start.5 = (bf16[128,8,128]{2,1,0:T(8,128)(2,1)S(1)}, bf16[128,8,128]{2,1,0:T(8,128)(2,1)}, u32[]{:S(2)}) copy-start(bf16[128,8,128]{2,1,0:T(8,128)(2,1)} %q_ref.1) | copy-start | bytes 786436
  13.4 5.0 %collective-permute-start.1 = (bf16[2,128,256]{2,1,0:T(8,128)(2,1)S(1)}, bf16[2,128,256]{2,1,0:T(8,128)(2,1)S(1)}, u32[]{:S(2)}, u32[]{:S(2)}) collective-permute-start(bf16[2,128,256]{2,1,0:T(8,128)(2,1)S(1)} %get-tuple-element.34), channel_id=1, source_target_pairs={{0,4},{4,0},{8,12},{12,8},{16,20},{20,16},{24,28},{28,24},{1,5},{5... | collective-permute-start | bytes 393224 | tf_op jit(solution)/shard_map/ppermute | solution.py:539
  14.0 5.0 %collective-permute-start.2 = (bf16[2,128,256]{2,1,0:T(8,128)(2,1)S(1)}, bf16[2,128,256]{2,1,0:T(8,128)(2,1)S(1)}, u32[]{:S(2)}, u32[]{:S(2)}) collective-permute-start(bf16[2,128,256]{2,1,0:T(8,128)(2,1)S(1)} %get-tuple-element.35), channel_id=1, source_target_pairs={{0,8},{4,12},{8,0},{12,4},{16,24},{20,28},{24,16},{28,20},{1,9},{5... | collective-permute-start | bytes 393224 | tf_op jit(solution)/shard_map/ppermute | solution.py:539
  19.5 6.5 %collective-permute-start.3 = (bf16[2,128,128]{2,1,0:T(8,128)(2,1)S(1)}, bf16[2,128,128]{2,1,0:T(8,128)(2,1)S(1)}, u32[]{:S(2)}, u32[]{:S(2)}) collective-permute-start(bf16[2,128,128]{2,1,0:T(8,128)(2,1)S(1)} %get-tuple-element.36.refs_3_), channel_id=1, source_target_pairs={{0,16},{4,20},{8,24},{12,28},{1,17},{5,21},{9,25},{13,29},{2,18},{... | collective-permute-start | bytes 196616 | tf_op jit(solution)/shard_map/ppermute | solution.py:581
  24.2 11.2 %slice-start = ((s8[8388608]{0:T(1024)(128)(4,1)}), s8[4194304]{0:T(1024)(128)(4,1)S(1)}, s32[]{:S(2)}) async-start(s8[8388608]{0:T(1024)(128)(4,1)} %bitcast.3), calls=%async_computation | async-start | bytes 8388608
  24.4 9.0 %copy-start = (bf16[128,1024]{1,0:T(8,128)(2,1)S(1)}, bf16[128,1024]{1,0:T(8,128)(2,1)}, u32[]{:S(2)}) copy-start(bf16[128,1024]{1,0:T(8,128)(2,1)} %residual_ref.1) | copy-start | bytes 786436
  24.4 9.0 %copy-start.4 = (f32[128]{0:T(128)S(1)}, f32[128]{0:T(128)}, u32[]{:S(2)}) copy-start(f32[128]{0:T(128)} %param.17) | copy-start | bytes 1540
  24.4 11.0 %copy-start.2 = (s32[16,16]{1,0:T(8,128)S(1)}, s32[16,16]{1,0:T(8,128)}, u32[]{:S(2)}) copy-start(s32[16,16]{1,0:T(8,128)} %at_ref.1) | copy-start | bytes 3076
  26.3 5.0 %collective-permute-start.4 = (bf16[2,128,128]{2,1,0:T(8,128)(2,1)S(1)}, bf16[2,128,128]{2,1,0:T(8,128)(2,1)S(1)}, u32[]{:S(2)}, u32[]{:S(2)}) collective-permute-start(bf16[2,128,128]{2,1,0:T(8,128)(2,1)S(1)} %get-tuple-element.40), channel_id=1, source_target_pairs={{0,4},{4,0},{8,12},{12,8},{16,20},{20,16},{24,28},{28,24},{1,5},{5... | collective-permute-start | bytes 196616 | tf_op jit(solution)/shard_map/ppermute | solution.py:591
  27.9 4.3 %collective-permute-start.5 = (bf16[2,128,128]{2,1,0:T(8,128)(2,1)S(1)}, bf16[2,128,128]{2,1,0:T(8,128)(2,1)S(1)}, u32[]{:S(2)}, u32[]{:S(2)}) collective-permute-start(bf16[2,128,128]{2,1,0:T(8,128)(2,1)S(1)} %get-tuple-element.41), channel_id=1, source_target_pairs={{0,8},{4,12},{8,0},{12,4},{16,24},{20,28},{24,16},{28,20},{1,9},{5... | collective-permute-start | bytes 196616 | tf_op jit(solution)/shard_map/ppermute | solution.py:591
  28.2 7.2 %slice-start.1 = ((s8[8388608]{0:T(1024)(128)(4,1)}), s8[4194304]{0:T(1024)(128)(4,1)S(1)}, s32[]{:S(2)}) async-start(s8[8388608]{0:T(1024)(128)(4,1)} %bitcast.3), calls=%async_computation.1 | async-start | bytes 8388608
  28.2 5.2 %collective-permute-start.6 = (bf16[2,128,128]{2,1,0:T(8,128)(2,1)S(1)}, bf16[2,128,128]{2,1,0:T(8,128)(2,1)S(1)}, u32[]{:S(2)}, u32[]{:S(2)}) collective-permute-start(bf16[2,128,128]{2,1,0:T(8,128)(2,1)S(1)} %get-tuple-element.42), channel_id=1, source_target_pairs={{0,12},{4,8},{8,4},{12,0},{16,28},{20,24},{24,20},{28,16},{1,13},{... | collective-permute-start | bytes 196616 | tf_op jit(solution)/shard_map/ppermute | solution.py:591
  33.4 8.9 %slice-start.2 = ((s8[8388608]{0:T(1024)(128)(4,1)}), s8[4194304]{0:T(1024)(128)(4,1)S(1)}, s32[]{:S(2)}) async-start(s8[8388608]{0:T(1024)(128)(4,1)} %bitcast.5), calls=%async_computation.2 | async-start | bytes 8388608
  33.8 8.4 %slice-start.3 = ((s8[8388608]{0:T(1024)(128)(4,1)}), s8[4194304]{0:T(1024)(128)(4,1)S(1)}, s32[]{:S(2)}) async-start(s8[8388608]{0:T(1024)(128)(4,1)} %bitcast.5), calls=%async_computation.3 | async-start | bytes 8388608
  33.8 6.7 %collective-permute-start.8 = (bf16[8,128,128]{2,1,0:T(8,128)(2,1)S(1)}, bf16[8,128,128]{2,1,0:T(8,128)(2,1)S(1)}, u32[]{:S(2)}, u32[]{:S(2)}) collective-permute-start(bf16[8,128,128]{2,1,0:T(8,128)(2,1)S(1)} %shard_map.126.after_ref.refs_0_), channel_id=1, source_target_pairs={{0,2},{1,3},{2,0},{3,1},{4,6},{5,7},{6,4},{7,5},{8,10},{9,11},{10,... | collective-permute-start | bytes 786440 | tf_op jit(solution)/shard_map/ppermute | solution.py:623
  35.4 5.7 %collective-permute-start.7 = (bf16[8,128,128]{2,1,0:T(8,128)(2,1)S(1)}, bf16[8,128,128]{2,1,0:T(8,128)(2,1)S(1)}, u32[]{:S(2)}, u32[]{:S(2)}) collective-permute-start(bf16[8,128,128]{2,1,0:T(8,128)(2,1)S(1)} %shard_map.126.after_ref.refs_0_), channel_id=1, source_target_pairs={{0,1},{1,0},{2,3},{3,2},{4,5},{5,4},{6,7},{7,6},{8,9},{9,8},{10,11... | collective-permute-start | bytes 786440 | tf_op jit(solution)/shard_map/ppermute | solution.py:623
  40.5 1.8 %copy-start.1 = (f32[4096]{0:T(1024)S(1)}, f32[4096]{0:T(1024)}, u32[]{:S(2)}) copy-start(f32[4096]{0:T(1024)} %param.19) | copy-start | bytes 49156
  40.5 1.8 %copy-start.3 = (s32[16,16]{1,0:T(8,128)S(1)}, s32[16,16]{1,0:T(8,128)}, u32[]{:S(2)}) copy-start(s32[16,16]{1,0:T(8,128)} %up_at.1) | copy-start | bytes 3076
  40.5 1.7 %collective-permute-start.9 = (bf16[8,128,128]{2,1,0:T(8,128)(2,1)S(1)}, bf16[8,128,128]{2,1,0:T(8,128)(2,1)S(1)}, u32[]{:S(2)}, u32[]{:S(2)}) collective-permute-start(bf16[8,128,128]{2,1,0:T(8,128)(2,1)S(1)} %shard_map.128), channel_id=1, source_target_pairs={{0,1},{1,0},{2,3},{3,2},{4,5},{5,4},{6,7},{7,6},{8,9},{9,8},{10,11... | collective-permute-start | bytes 786440 | tf_op jit(solution)/shard_map/ppermute | solution.py:623
  47.3 1.6 %collective-permute-start.10 = (bf16[8,128,128]{2,1,0:T(8,128)(2,1)S(1)}, bf16[8,128,128]{2,1,0:T(8,128)(2,1)S(1)}, u32[]{:S(2)}, u32[]{:S(2)}) collective-permute-start(bf16[8,128,128]{2,1,0:T(8,128)(2,1)S(1)} %get-tuple-element.45), channel_id=1, source_target_pairs={{0,1},{1,0},{2,3},{3,2},{4,5},{5,4},{6,7},{7,6},{8,9},{9,8},{10,11... | collective-permute-start | bytes 786440 | tf_op jit(solution)/shard_map/ppermute | solution.py:640
  47.7 3.2 %collective-permute-start.11 = (bf16[8,128,128]{2,1,0:T(8,128)(2,1)S(1)}, bf16[8,128,128]{2,1,0:T(8,128)(2,1)S(1)}, u32[]{:S(2)}, u32[]{:S(2)}) collective-permute-start(bf16[8,128,128]{2,1,0:T(8,128)(2,1)S(1)} %get-tuple-element.46), channel_id=1, source_target_pairs={{0,1},{1,0},{2,3},{3,2},{4,5},{5,4},{6,7},{7,6},{8,9},{9,8},{10,11... | collective-permute-start | bytes 786440 | tf_op jit(solution)/shard_map/ppermute | solution.py:647
  49.0 8.7 %collective-permute-start.12 = (bf16[8,128,128]{2,1,0:T(8,128)(2,1)S(1)}, bf16[8,128,128]{2,1,0:T(8,128)(2,1)S(1)}, u32[]{:S(2)}, u32[]{:S(2)}) collective-permute-start(bf16[8,128,128]{2,1,0:T(8,128)(2,1)S(1)} %add_convert_fusion.after_ref), channel_id=1, source_target_pairs={{0,2},{1,3},{2,0},{3,1},{4,6},{5,7},{6,4},{7,5},{8,10},{9,11},{10,... | collective-permute-start | bytes 786440 | tf_op jit(solution)/shard_map/ppermute | solution.py:647
